TPU v7x, 32 devices: a whole 2x2x4 slice. The times are simulated.
32 devices in a mesh: gx: 2 (over x), gy: 4 (over z), gz: 4 (over y, core).
Axes of the slice: x: 2, y: 2, z: 4, core: 2. Of those that a mesh axis runs over, the one named last changes fastest.
Arguments:
- velocity: float32 [3, 64, 256, 512], P(None, 'gx', 'gy', 'gz'), may hold values from -12 to 12
- inv_density: float32 [64, 256, 512], P('gx', 'gy', 'gz'), may hold values from 0.2 to 5
- factor_x: float32 [64, 64], P('gx'), may hold values from -1 to 1
- factor_y: float32 [256, 64], P('gy'), may hold values from -0.5 to 0.5
- factor_z: float32 [512, 64], P('gz'), may hold values from -0.375 to 0.375
Outputs:
- pressure: float32 [64, 256, 512], P('gx', 'gy', 'gz')
- corrected: float32 [3, 64, 256, 512], P(None, 'gx', 'gy', 'gz')
- core: float32 [64, 4, 64, 64], P('gx', None, 'gy', 'gz')
All inputs are finite; a program needn't handle non-finite values.
Results may differ from a plain program's by a relative error of at most 0.00013.
Values sent between devices are 32-bit elements; how exact they have to be, the bound alone decides.
No kernel may reach another device: no remote copies, remote signals or barrier semaphores. Data moves between devices by JAX's collectives and lax.ppermute only.
A program may use at most 128 MiB of HBM per device.

v0:
```python
import jax
import jax.numpy as jnp
from jax import lax
from jax.sharding import PartitionSpec as P

ITERS = 4


SHIFT = 0.1
HIGHEST = lax.Precision.HIGHEST


def padded_2(cells, sides, width):
    for axis, dim in sides:
        count = lax.axis_size(axis)
        ends = count - 1
        head = lax.slice_in_dim(cells, 0, width, axis=dim)
        tail = lax.slice_in_dim(cells, cells.shape[dim] - width, cells.shape[dim], axis=dim)
        cells = jnp.concatenate(
            [
                lax.ppermute(tail, axis, [(i, (i + 1) % count) for i in range(ends)]),
                cells,
                lax.ppermute(head, axis, [((i + 1) % count, i) for i in range(ends)]),
            ],
            axis=dim,
        )
    return cells


def neighbours(padded):
    centre_cut = (slice(None),) + (slice(1, -1),) * 3
    result = []
    for dimension in range(1, 4):
        forward = list(centre_cut)
        forward[dimension] = slice(2, None)
        backward = list(centre_cut)
        backward[dimension] = slice(None, -2)
        result.append((padded[tuple(forward)], padded[tuple(backward)]))
    return result


def widen(stack):
    return padded_2(stack, (("gx", 1), ("gy", 2), ("gz", 3)), 1)


def assemble(sides, inv_density):
    couplings = []
    diagonal = SHIFT + jnp.zeros_like(inv_density)
    divergence = jnp.zeros_like(inv_density)
    for dimension in range(3):
        forward, backward = sides[dimension]
        c_forward = 0.5 * (inv_density + forward[3])
        c_backward = 0.5 * (inv_density + backward[3])
        couplings.append((c_forward, c_backward))
        diagonal = diagonal + c_forward + c_backward
        divergence = divergence + 0.5 * (forward[dimension] - backward[dimension])
    return (couplings, diagonal, -divergence)


def apply_operator(sides, field, couplings, diagonal):
    result = diagonal * field
    for dimension in range(3):
        forward, backward = sides[dimension]
        result = (
            result - couplings[dimension][0] * forward[0] - couplings[dimension][1] * backward[0]
        )
    return result


def correct(sides, velocity, inv_density):
    parts = []
    for dimension in range(3):
        gradient = 0.5 * (sides[dimension][0][0] - sides[dimension][1][0])
        parts.append(velocity[dimension] - inv_density * gradient)
    return jnp.stack(parts, 0)


def residual_product(residual, precond):
    return lax.psum(jnp.sum(residual * precond), ("gx", "gy", "gz"))


def per_device(velocity, inv_density, factor_x, factor_y, factor_z):
    padded = widen(jnp.concatenate([velocity, inv_density[None]], 0))
    couplings, diagonal, rhs = assemble(neighbours(padded), inv_density)
    pressure = jnp.zeros_like(rhs)
    residual = rhs
    precond = residual / diagonal
    direction = precond
    product = residual_product(residual, precond)
    for iteration in range(ITERS):
        image = apply_operator(neighbours(widen(direction[None])), direction, couplings, diagonal)
        alpha = product / lax.psum(jnp.sum(direction * image), ("gx", "gy", "gz"))
        pressure = pressure + alpha * direction
        residual = residual - alpha * image
        precond = residual / diagonal
        fresh = residual_product(residual, precond)
        direction = precond + fresh / product * direction
        product = fresh
    corrected = correct(neighbours(widen(pressure[None])), velocity, inv_density)
    fields = jnp.concatenate([corrected, pressure[None]], 0)
    cells_x, cells_y = (fields.shape[1], fields.shape[2])
    rank = factor_x.shape[1]
    groups_x = lax.axis_size("gx")
    groups_y = lax.axis_size("gy")
    groups_z = lax.axis_size("gz")
    columns = factor_z
    reduced_z = lax.psum_scatter(
        jnp.einsum("fijk,kc->cfij", fields, columns, precision=HIGHEST).reshape(
            rank // groups_z * lax.axis_size("gz"), -1
        ),
        "gz",
        scatter_dimension=0,
        tiled=True,
    )
    shaped_z = reduced_z.reshape(rank // groups_z, 4, cells_x, cells_y)
    columns = factor_x
    reduced_x = lax.psum_scatter(
        jnp.einsum("cfij,ia->acfj", shaped_z, columns, precision=HIGHEST).reshape(
            rank // groups_x * lax.axis_size("gx"), -1
        ),
        "gx",
        scatter_dimension=0,
        tiled=True,
    )
    shaped_x = reduced_x.reshape(rank // groups_x, rank // groups_z, 4, cells_y)
    columns = factor_y
    reduced_y = lax.psum_scatter(
        jnp.einsum("acfj,jb->bafc", shaped_x, columns, precision=HIGHEST).reshape(
            rank // groups_y * lax.axis_size("gy"), -1
        ),
        "gy",
        scatter_dimension=0,
        tiled=True,
    )
    shaped_y = reduced_y.reshape(rank // groups_y, rank // groups_x, 4, rank // groups_z)
    core = jnp.transpose(shaped_y, (1, 2, 0, 3))
    return (pressure, corrected, core)


def solution(mesh):
    placed = (
        P(None, "gx", "gy", "gz"),
        P("gx", "gy", "gz"),
        P("gx", None),
        P("gy", None),
        P("gz", None),
    )
    return jax.shard_map(
        per_device,
        mesh=mesh,
        in_specs=placed,
        out_specs=(P("gx", "gy", "gz"), P(None, "gx", "gy", "gz"), P("gx", None, "gy", "gz")),
        check_vma=False,
    )
```

profile of v0, /device:TPU:0, one launch (start us, length us, event | category | flops | bytes accessed | tf_op | source)
XLA Modules:
  0.0 674.3 jit_solution(15961214212507236761)
XLA Ops:
  8.4 5.0 collective-permute-start.1
  25.8 4.3 collective-permute-done.2
  32.0 5.4 fusion.141
  53.7 11.3 %fusion.133 = (f32[32,64,128]{2,1,0:T(8,128)S(1)}, f32[32,64,128]{2,1,0:T(8,128)S(1)}, f32[32,64,128]{2,1,0:T(8,128)}, f32[32,64,128]{2,1,0:T(8,128)}, f32[32,64...) fusion(f32[32,64,128]{2,1,0:T(8,128)S(1)} %copy-done.3, ...), kind=kLoop, calls=%fused_computation.291 | loop fusion | flops 19398656 | bytes 15153280 | tf_op jit(solution)/shard_map/div | solution.py:87
  68.1 4.2 collective-permute-done.6
  77.2 4.2 collective-permute-done.8
  93.0 7.0 %multiply_reduce_fusion.5 = (f32[]{:T(128)}, f32[]{:T(128)}, f32[32,64,128]{2,1,0:T(8,128)}) fusion(f32[32,64,128]{2,1,0:T(8,128)S(1)} %get-tuple-element.24, f32[32,64,128]{2,1,0:T(8,128)} %get-tuple-element.32, f32[32,64,128]{2,1,0:T(8,128)} %get-tuple-element.31, f32[1,34,1,128]{3,2,1,0:T(1,128)S(1)} %collective-permute-done.8, ...), kind=kLoop, calls=%fused_computation.261 | loop fusion | flops 9175038 | bytes 11652648 | tf_op jit(solution)/shard_map/reduce_sum | solution.py:92
  100.0 42.6 %all-reduce = (f32[]{:T(128)}, f32[]{:T(128)}) all-reduce(f32[]{:T(128)} %get-tuple-element.10, f32[]{:T(128)} %get-tuple-element.9), channel_id=1, replica_groups=mesh['gx'=2,'gy'=4,'gz'=4] {'gx','gy','gz'}, use_global_device_ids=true, to_apply=%region_1.0 | all-reduce | flops 2 | bytes 16 | tf_op jit(solution)/shard_map/psum | solution.py:79
  147.9 40.8 %psum.58 = f32[]{:T(128)} all-reduce(f32[]{:T(128)} %get-tuple-element.20), channel_id=1, replica_groups=mesh['gx'=2,'gy'=4,'gz'=4] {'gx','gy','gz'}, use_global_device_ids=true, to_apply=%region_5.0 | all-reduce | flops 1 | bytes 8 | tf_op jit(solution)/shard_map/psum | solution.py:79
  191.4 4.2 collective-permute-start.13
  197.2 4.2 collective-permute-done.12
  206.4 4.2 collective-permute-done.14
  223.6 6.9 %multiply_reduce_fusion.3 = (f32[]{:T(128)}, f32[32,64,128]{2,1,0:T(8,128)}) fusion(f32[32,64,128]{2,1,0:T(8,128)S(1)} %multiply_add_fusion.3, f32[32,64,128]{2,1,0:T(8,128)} %get-tuple-element.31, f32[1,34,1,128]{3,2,1,0:T(1,128)S(1)} %collective-permute-done.14, f32[1,1,64,128]{3,2,1,0:T(8,128)S(1)} %collective-permute-done.12, ...), kind=kLoop, calls=%fused_computation.257 | loop fusion | flops 8650751 | bytes 10604068 | tf_op jit(solution)/shard_map/reduce_sum | solution.py:92
  230.5 38.5 %psum.59 = f32[]{:T(128)} all-reduce(f32[]{:T(128)} %get-tuple-element.18), channel_id=1, replica_groups=mesh['gx'=2,'gy'=4,'gz'=4] {'gx','gy','gz'}, use_global_device_ids=true, to_apply=%region_7.0 | all-reduce | flops 1 | bytes 8 | tf_op jit(solution)/shard_map/psum | solution.py:92
  274.3 41.4 %psum.60 = f32[]{:T(128)} all-reduce(f32[]{:T(128)} %get-tuple-element.15), channel_id=1, replica_groups=mesh['gx'=2,'gy'=4,'gz'=4] {'gx','gy','gz'}, use_global_device_ids=true, to_apply=%region_9.0 | all-reduce | flops 1 | bytes 8 | tf_op jit(solution)/shard_map/psum | solution.py:79
  318.5 4.2 collective-permute-start.19
  324.2 4.2 collective-permute-done.18
  332.3 4.2 collective-permute-done.20
  349.7 9.4 %multiply_reduce_fusion.1 = (f32[]{:T(128)}, f32[32,64,128]{2,1,0:T(8,128)}) fusion(f32[32,64,128]{2,1,0:T(8,128)} %copy-done.2, f32[32,64,128]{2,1,0:T(8,128)} %get-tuple-element.31, f32[1,34,1,128]{3,2,1,0:T(1,128)S(1)} %collective-permute-done.20, f32[1,1,64,128]{3,2,1,0:T(8,128)S(1)} %collective-permute-done.18, f32[1,32,64,128]{3,2,1,0:T(8,128)} %bitcast.334, ...), kind=kLoop, calls=%fused_computation.253 | loop fusion | flops 8650751 | bytes 10604068 | tf_op jit(solution)/shard_map/reduce_sum | solution.py:92
  359.1 38.7 %psum.61 = f32[]{:T(128)} all-reduce(f32[]{:T(128)} %get-tuple-element.13), channel_id=1, replica_groups=mesh['gx'=2,'gy'=4,'gz'=4] {'gx','gy','gz'}, use_global_device_ids=true, to_apply=%region_11.0 | all-reduce | flops 1 | bytes 8 | tf_op jit(solution)/shard_map/psum | solution.py:92
  401.5 41.3 %psum.62 = f32[]{:T(128)} all-reduce(f32[]{:T(128)} %multiply_reduce_fusion), channel_id=1, replica_groups=mesh['gx'=2,'gy'=4,'gz'=4] {'gx','gy','gz'}, use_global_device_ids=true, to_apply=%region_13.0 | all-reduce | flops 1 | bytes 8 | tf_op jit(solution)/shard_map/psum | solution.py:79
  446.5 4.2 collective-permute-start.25
  452.2 4.2 collective-permute-done.24
  460.6 4.2 collective-permute-done.26
  477.8 8.9 %fusion.30 = f32[]{:T(128)} fusion(f32[32,64,128]{2,1,0:T(8,128)} %copy-done.5, f32[32,64,128]{2,1,0:T(8,128)} %get-tuple-element.31, f32[1,34,66,1]{3,2,1,0:T(8,128)} %copy.34, f32[1,34,1,128]{3,2,1,0:T(1,128)S(1)} %collective-permute-done.26, f32[1,34,1,128]{3,2,1,0:T(1,128)S(1)} %collective-permute-done.27, ...), kind=kLoop, calls=%fused_computation.57 | loop fusion | flops 8650751 | bytes 9555492 | tf_op jit(solution)/shard_map/reduce_sum | solution.py:92
  486.7 39.4 %psum.63 = f32[]{:T(128)} all-reduce(f32[]{:T(128)} %fusion.30), channel_id=1, replica_groups=mesh['gx'=2,'gy'=4,'gz'=4] {'gx','gy','gz'}, use_global_device_ids=true, to_apply=%region_15.0 | all-reduce | flops 1 | bytes 8 | tf_op jit(solution)/shard_map/psum | solution.py:92
  535.2 4.2 collective-permute-done.30
  543.4 4.2 collective-permute-done.32
  563.9 5.0 fusion
  572.8 31.9 %reduce-scatter.10.cloned.1.call-done = f32[16,8192]{1,0:T(8,128)} async-done(((f32[64,8192]{1,0:T(8,128)}), f32[16,8192]{1,0:T(8,128)}) %reduce-scatter.10.cloned.1.call-update) | async-done | bytes 524304
  616.7 20.2 %reduce-scatter.8.cloned.1.call-done = f32[32,4096]{1,0:T(8,128)} async-done(((f32[64,4096]{1,0:T(8,128)}), f32[32,4096]{1,0:T(8,128)}) %reduce-scatter.8.cloned.1.call-update) | async-done | bytes 524304 | tf_op jit(solution)/shard_map/reduce_scatter | solution.py:117
  645.9 18.0 %reduce-scatter.12.cloned.1.call-done = f32[16,2048]{1,0:T(8,128)} async-done(((f32[64,2048]{1,0:T(8,128)}), f32[16,2048]{1,0:T(8,128)}) %reduce-scatter.12.cloned.1.call-update) | async-done | bytes 131088
  (164 shorter events, 179.5 us)
Async XLA Ops:
  7.2 597.5 %reduce-scatter.10.cloned.1.call-start = ((), (), s32[]{:S(2)}) async-start(), calls=%async_computation.4 | async-start | bytes 2621440
  8.4 7.7 %collective-permute-start.1 = (f32[4,1,64,128]{3,2,1,0:T(8,128)S(1)}, f32[4,1,64,128]{3,2,1,0:T(8,128)S(1)}, u32[]{:S(2)}, u32[]{:S(2)}) collective-permute-start(f32[4,1,64,128]{3,2,1,0:T(8,128)S(1)} %get-tuple-element.39), channel_id=1, source_target_pairs={{0,16},{1,17},{2,18},{3,19},{4,20},{5,21},{6,22},{7,23},{8,24},{9,... | collective-permute-start | bytes 393224 | tf_op jit(solution)/shard_map/ppermute | solution.py:21
  13.4 6.9 %collective-permute-start = (f32[4,1,64,128]{3,2,1,0:T(8,128)S(1)}, f32[4,1,64,128]{3,2,1,0:T(8,128)S(1)}, u32[]{:S(2)}, u32[]{:S(2)}) collective-permute-start(f32[4,1,64,128]{3,2,1,0:T(8,128)S(1)} %get-tuple-element.40), channel_id=1, source_target_pairs={{16,0},{17,1},{18,2},{19,3},{20,4},{21,5},{22,6},{23,7},{24,8},{25... | collective-permute-start | bytes 393224 | tf_op jit(solution)/shard_map/ppermute | solution.py:23
  20.4 5.4 collective-permute-start.3
  23.8 6.2 collective-permute-start.2
  40.8 6.0 collective-permute-start.5
  45.5 4.9 collective-permute-start.4
  66.5 5.8 collective-permute-start.6
  72.3 4.9 collective-permute-start.9
  75.8 5.6 collective-permute-start.8
  84.8 5.1 collective-permute-start.10
  86.5 4.9 collective-permute-start.11
  191.4 5.8 collective-permute-start.13
  195.6 5.8 collective-permute-start.12
  201.4 5.0 collective-permute-start.15
  205.0 5.6 collective-permute-start.14
  214.4 6.1 collective-permute-start.16
  318.5 5.8 collective-permute-start.19
  322.6 5.8 collective-permute-start.18
  330.9 5.6 collective-permute-start.20
  340.3 6.3 collective-permute-start.22
  446.5 5.8 collective-permute-start.25
  450.7 5.8 collective-permute-start.24
  459.2 5.6 collective-permute-start.26
  468.6 6.1 collective-permute-start.28
  529.4 5.8 collective-permute-start.31
  533.6 5.8 collective-permute-start.30
  542.0 5.6 collective-permute-start.32
  551.5 7.8 %collective-permute-start.35 = (f32[1,34,66,1]{2,3,1,0:T(1,128)S(1)}, f32[1,34,66,1]{2,3,1,0:T(1,128)S(1)}, u32[]{:S(2)}, u32[]{:S(2)}) collective-permute-start(f32[1,34,66,1]{2,3,1,0:T(1,128)S(1)} %copy.37), channel_id=1, source_target_pairs={{0,1},{1,2},{2,3},{4,5},{5,6},{6,7},{8,9},{9,10},{10,11},{12,13},{... | collective-permute-start | bytes 26936 | tf_op jit(solution)/shard_map/ppermute | solution.py:21
  552.8 5.3 collective-permute-start.34
  572.7 64.2 %reduce-scatter.8.cloned.1.call-start = ((), (), s32[]{:S(2)}) async-start(), calls=%async_computation.3 | async-start | bytes 1572864 | tf_op jit(solution)/shard_map/reduce_scatter | solution.py:117
  616.4 47.5 %reduce-scatter.12.cloned.1.call-start = ((), (), s32[]{:S(2)}) async-start(), calls=%async_computation.5 | async-start | bytes 655360
  (23 other events, 737.8 us)
Sparse Core Ops, SparseCore 0:
  572.8 31.8 reduce-scatter.9
  616.5 20.3 reduce-scatter.7
  642.1 21.6 reduce-scatter.11
where the time goes:
time: 683 us; the launch traced here: 674 us
  blocking collectives  283 us (41%)
  waiting for transfers between devices  126 us (18%)
  starting transfers between devices  80.5 us (12%)
  local copies, waits for them, and re-layouts  77 us (11%)
  other arithmetic  73.7 us (11%)
  between operations  24.3 us (4%)
  matrix products  10 us (1%)
    psum x4, blocking collectives, residual_product(): return lax.psum(jnp.sum(residual * precond), ('gx', 'gy', 'gz'))  166 us
    psum x3, blocking collectives, per_device(): alpha = product / lax.psum(jnp.sum(direction * image), ('gx', 'gy', 'gz'))  117 us
    ppermute x18, starting transfers between devices, padded_2(): lax.ppermute(tail, axis, [(i, (i + 1) % count) for i in range(ends)])  56.5 us
    ppermute x18, waiting for transfers between devices, padded_2(): lax.ppermute(head, axis, [((i + 1) % count, i) for i in range(ends)])  52 us
    unnamed x5, waiting for transfers between devices  49.9 us
    reduce_sum x4, other arithmetic, per_device(): alpha = product / lax.psum(jnp.sum(direction * image), ('gx', 'gy', 'gz'))  32.1 us
    ppermute x18, starting transfers between devices, padded_2(): lax.ppermute(head, axis, [((i + 1) % count, i) for i in range(ends)])  23.6 us
    slice x11, local copies, waits for them, and re-layouts, padded_2(): head = lax.slice_in_dim(cells, 0, width, axis=dim)  20.7 us
  transfers between devices with their start and end apart: 39, of which 29 were waited for; matrix products, arithmetic and copies ran while one was open for 4% of the time, Pallas kernels for 0%

commit v1 on v0

v1 whole, which is shorter than its diff:
```python
import functools

import jax
import jax.numpy as jnp
from jax import lax
from jax.experimental import pallas as pl
from jax.experimental.pallas import tpu as pltpu
from jax.sharding import PartitionSpec as P

ITERS = 4
SHIFT = 0.1
AXES = ("gx", "gy", "gz")

REACH = ITERS
LAYERS = ITERS + 1
WIDE = 8
SLOT = 16
ROWS = 24
NEWTON = (0.5, 0.5, 0.5)
PAIRS = [(a, b) for a in range(ITERS) for b in range(a, ITERS)]
VMEM = pl.BlockSpec(memory_space=pltpu.VMEM)
SMEM = pl.BlockSpec(memory_space=pltpu.SMEM)
F32 = jnp.float32
BF16 = jnp.bfloat16


def call(body, outs, operands, scratch=(), smem=0, limit=56):
    return pl.pallas_call(
        body,
        out_shape=[jax.ShapeDtypeStruct(shape, F32) for shape in outs],
        in_specs=[SMEM] * smem + [VMEM] * (len(operands) - smem),
        out_specs=[VMEM] * len(outs),
        scratch_shapes=[pltpu.VMEM(shape, F32) for shape in scratch],
        compiler_params=pltpu.CompilerParams(vmem_limit_bytes=limit * 2**20),
    )(*operands)


def lanes(shape):
    return lax.broadcasted_iota(jnp.int32, shape, len(shape) - 1)


def sublanes(shape):
    return lax.broadcasted_iota(jnp.int32, shape, len(shape) - 2)


def exchange(up, down, axis):
    count = lax.axis_size(axis)
    ends = count - 1
    below = lax.ppermute(up, axis, [(i, i + 1) for i in range(ends)])
    above = lax.ppermute(down, axis, [(i + 1, i) for i in range(ends)])
    return below, above


def pack_x(velocity, inv, rhs, up, down):
    nx, ny, nz = inv.shape
    shape = (ny, nz)
    first_lane, last_lane = lanes(shape) == 0, lanes(shape) == nz - 1
    first_row, last_row = sublanes(shape) == 0, sublanes(shape) == ny - 1

    def plane(x, carry):
        before = jnp.where(x == 0, 0.0, velocity[0, jnp.maximum(x - 1, 0)])
        after = jnp.where(x == nx - 1, 0.0, velocity[0, jnp.minimum(x + 1, nx - 1)])
        along_y = velocity[1, x]
        along_z = velocity[2, x]
        total = after - before
        total = total + jnp.where(last_row, 0.0, pltpu.roll(along_y, ny - 1, 0))
        total = total - jnp.where(first_row, 0.0, pltpu.roll(along_y, 1, 0))
        total = total + jnp.where(last_lane, 0.0, pltpu.roll(along_z, nz - 1, 1))
        total = total - jnp.where(first_lane, 0.0, pltpu.roll(along_z, 1, 1))
        rhs[x] = -0.5 * total
        return carry

    lax.fori_loop(0, nx, plane, 0)
    for message, start, own, sign, layer in (
        (up, nx - REACH, nx - 1, 0.5, nx - LAYERS),
        (down, 0, 0, -0.5, 0),
    ):
        for k in range(REACH):
            message[k * ny : (k + 1) * ny, :] = rhs[start + k]
        base = REACH * ny
        message[base : base + ny, :] = sign * velocity[0, own]
        base += ny
        for k in range(LAYERS):
            message[base : base + ny, :] = inv[layer + k]
            base += ny
        ends = jnp.zeros(shape, F32)
        for k in range(REACH):
            plane_z = velocity[2, start + k]
            ends = jnp.where(lanes(shape) == 2 * k, plane_z[:, 0:1], ends)
            ends = jnp.where(lanes(shape) == 2 * k + 1, plane_z[:, nz - 1 : nz], ends)
        message[base : base + ny, :] = ends
        base += ny
        for k in range(REACH):
            message[base + 2 * k : base + 2 * k + 1, :] = velocity[1, start + k, 0:1, :]
            message[base + 2 * k + 1 : base + 2 * k + 2, :] = velocity[1, start + k, ny - 1 : ny, :]


def pack_y(velocity, inv, rhs, below, above, up, down):
    nx, ny, nz = inv.shape
    each = REACH + 1 + LAYERS + 1

    def put(pair, parity, rows_rhs, ghost, rows_inv, first, last):
        offset = parity * each
        for message, part in ((up, 1), (down, 0)):
            message[pair, pl.ds(offset, REACH), :] = rows_rhs[part]
            message[pair, pl.ds(offset + REACH, 1), :] = (0.5 if part else -0.5) * ghost[part]
            message[pair, pl.ds(offset + REACH + 1, LAYERS), :] = rows_inv[part]
            ends = jnp.zeros((1, nz), F32)
            for k in range(REACH):
                ends = jnp.where(lanes((1, nz)) == 2 * k, first[part][k : k + 1], ends)
                ends = jnp.where(lanes((1, nz)) == 2 * k + 1, last[part][k : k + 1], ends)
            message[pair, pl.ds(offset + each - 1, 1), :] = ends

    def halo(x, message, k_rhs, k_inv, extra):
        base = (REACH + 1 + k_inv) * ny
        rows_inv = (message[pl.ds(base, LAYERS), :], message[pl.ds(base + ny - LAYERS, LAYERS), :])
        zero_row = jnp.zeros((1, nz), F32)
        zero = jnp.zeros((REACH, nz), F32)
        if k_rhs is None:
            column = jnp.zeros((REACH, 1), F32)
            put(x // 2, x % 2, (zero, zero), (zero_row, zero_row), rows_inv, (column, column), (column, column))
            return
        low, high = message[pl.ds(k_rhs * ny, REACH), :], message[pl.ds((k_rhs + 1) * ny - REACH, REACH), :]
        if extra is not None:
            sign, source = extra
            low = low + sign * velocity[0, source, 0:REACH, :]
            high = high + sign * velocity[0, source, ny - REACH : ny, :]
        ends = (REACH + 1 + LAYERS) * ny
        lines = ends + ny + 2 * k_rhs
        ghost = (message[pl.ds(lines, 1), :], message[pl.ds(lines + 1, 1), :])
        head, tail = message[pl.ds(ends, REACH), :], message[pl.ds(ends + ny - REACH, REACH), :]
        first = (head[:, 2 * k_rhs : 2 * k_rhs + 1], tail[:, 2 * k_rhs : 2 * k_rhs + 1])
        last = (head[:, 2 * k_rhs + 1 : 2 * k_rhs + 2], tail[:, 2 * k_rhs + 1 : 2 * k_rhs + 2])
        put(x // 2, x % 2, (low, high), ghost, rows_inv, first, last)

    for k in range(LAYERS):
        halo(k, below, k - 1 if k else None, k, (-0.5, 0) if k == LAYERS - 1 else None)
        halo(
            nx + LAYERS + k,
            above,
            k if k < REACH else None,
            k,
            (0.5, nx - 1) if k == 0 else None,
        )

    def own(x, pair, parity, extra):
        low, high = rhs[x, 0:REACH, :], rhs[x, ny - REACH : ny, :]
        if extra is not None:
            low = low + extra[pl.ds(REACH * ny, REACH), :]
            high = high + extra[pl.ds((REACH + 1) * ny - REACH, REACH), :]
        ghost = (velocity[1, x, 0:1, :], velocity[1, x, ny - 1 : ny, :])
        rows_inv = (inv[x, 0:LAYERS, :], inv[x, ny - LAYERS : ny, :])
        head, tail = velocity[2, x, 0:REACH, :], velocity[2, x, ny - REACH : ny, :]
        first = (head[:, 0:1], tail[:, 0:1])
        last = (head[:, nz - 1 : nz], tail[:, nz - 1 : nz])
        put(pair, parity, (low, high), ghost, rows_inv, first, last)

    def at(x, extra):
        own(x, (x + LAYERS) // 2, (x + LAYERS) % 2, extra)

    at(0, below)
    at(nx - 1, above)
    begin = 1 + (1 + LAYERS) % 2
    finish = begin + (nx - 1 - begin) // 2 * 2
    for x in (*range(1, begin), *range(finish, nx - 1)):
        at(x, None)

    def planes(n, carry):
        for parity in range(2):
            own(begin + 2 * n + parity, (begin + LAYERS) // 2 + n, parity, None)
        return carry

    lax.fori_loop(0, (finish - begin) // 2, planes, 0)


def pack_z(velocity, inv, rhs, below, above, before, after, rhs_wide, inv_wide, up, down, ends):
    nx, ny, nz = inv.shape
    wide = nx + 2 * LAYERS
    rows = ny + 2 * WIDE
    each = REACH + 1 + LAYERS + 1
    group = nz // SLOT
    mine = pl.ds(WIDE, ny)

    edge = (WIDE, nz)
    zero_edge = jnp.zeros(edge, F32)
    for k in range(LAYERS):
        for message, x, layer in ((below, k, k - 1), (above, nx + LAYERS + k, k if k < REACH else -1)):
            base = (REACH + 1 + k) * ny
            inv_wide[x, mine, :] = message[pl.ds(base, ny), :]
            if layer < 0:
                rhs_wide[x, mine, :] = jnp.zeros((ny, nz), F32)
                ends[x, mine, :] = jnp.zeros((ny, nz), F32)
                continue
            part = message[pl.ds(layer * ny, ny), :]
            if x == LAYERS - 1:
                part = part - 0.5 * velocity[0, 0]
            if x == nx + LAYERS:
                part = part + 0.5 * velocity[0, nx - 1]
            rhs_wide[x, mine, :] = part
            line = message[pl.ds((REACH + 1 + LAYERS) * ny, ny), :]
            ends[x, mine, :] = jnp.where(
                lanes((ny, nz)) == 0, line[:, 2 * layer : 2 * layer + 1], line[:, 2 * layer + 1 : 2 * layer + 2]
            )

    def plane(x, carry):
        inv_wide[x + LAYERS, mine, :] = inv[x]
        rhs_wide[x + LAYERS, mine, :] = rhs[x]
        ends[x + LAYERS, mine, :] = velocity[2, x]
        return carry

    lax.fori_loop(0, nx, plane, 0)
    rhs_wide[LAYERS, mine, :] += below[pl.ds(REACH * ny, ny), :]
    rhs_wide[LAYERS + nx - 1, mine, :] += above[pl.ds(REACH * ny, ny), :]

    def finish(x, ghost_low, ghost_high):
        low, high = before[x // 2], after[x // 2]
        low = jnp.where(x % 2 == 0, low, pltpu.roll(low, ROWS - each, 0))[0:SLOT]
        high = jnp.where(x % 2 == 0, high, pltpu.roll(high, ROWS - each, 0))[0:SLOT]
        row = sublanes((SLOT, nz))
        part = pltpu.roll(low, WIDE - REACH, 0)[0:WIDE]
        part = jnp.where(sublanes(edge) >= WIDE - REACH, part, 0.0)
        part = part - jnp.where(sublanes(edge) == WIDE - 1, 0.5 * ghost_low, 0.0)
        rhs_wide[x, 0:WIDE, :] = part
        part = pltpu.roll(low, SLOT - (REACH + 1) + WIDE - LAYERS, 0)[0:WIDE]
        inv_wide[x, 0:WIDE, :] = jnp.where(sublanes(edge) >= WIDE - LAYERS, part, 0.0)
        part = jnp.where(sublanes(edge) < REACH, high[0:WIDE], 0.0)
        part = part + jnp.where(sublanes(edge) == 0, 0.5 * ghost_high, 0.0)
        rhs_wide[x, WIDE + ny : rows, :] = part
        part = pltpu.roll(high, SLOT - (REACH + 1), 0)[0:WIDE]
        inv_wide[x, WIDE + ny : rows, :] = jnp.where(sublanes(edge) < LAYERS, part, 0.0)
        head = rhs_wide[x, WIDE : 2 * WIDE, :]
        rhs_wide[x, WIDE : 2 * WIDE, :] = head + jnp.where(sublanes(edge) == 0, low[REACH : REACH + 1], 0.0)
        tail = rhs_wide[x, ny : WIDE + ny, :]
        rhs_wide[x, ny : WIDE + ny, :] = tail + jnp.where(
            sublanes(edge) == WIDE - 1, high[REACH : REACH + 1], 0.0
        )
        for message, start, place in ((low, WIDE - REACH, 0), (high, 0, WIDE + ny)):
            line = message[each - 1 : each]
            one = jnp.zeros(edge, F32)
            two = jnp.zeros(edge, F32)
            for k in range(REACH):
                here = sublanes(edge) == start + k
                one = jnp.where(here, line[:, 2 * k : 2 * k + 1], one)
                two = jnp.where(here, line[:, 2 * k + 1 : 2 * k + 2], two)
            ends[x, place : place + WIDE, :] = jnp.where(lanes(edge) == 0, one, two)
        slot = x // group, (x % group) * SLOT
        whole = (rows, nz)
        lane = lanes(whole)
        r, i, e = rhs_wide[x], inv_wide[x], ends[x]
        base = slot[1]
        inside = (lane >= base) & (lane < base + SLOT)
        place = lane - base
        value = jnp.where(place < REACH, pltpu.roll(r, base + REACH, 1), pltpu.roll(i, base + REACH + 1 + LAYERS, 1))
        value = jnp.where(place == REACH, 0.5 * e[:, nz - 1 : nz], value)
        up[slot[0]] = jnp.where(inside, value, up[slot[0]])
        value = jnp.where(place < REACH, pltpu.roll(r, base, 1), pltpu.roll(i, base + REACH + 1, 1))
        value = jnp.where(place == REACH, -0.5 * e[:, 0:1], value)
        down[slot[0]] = jnp.where(inside, value, down[slot[0]])

    up[...] = jnp.zeros(up.shape, F32)
    down[...] = jnp.zeros(down.shape, F32)
    for k in range(LAYERS):
        for message, x, layer in ((below, k, k - 1), (above, nx + LAYERS + k, k if k < REACH else -1)):
            lines = (REACH + 1 + LAYERS + 1) * ny + 2 * layer
            if layer < 0:
                zero = jnp.zeros((1, nz), F32)
                finish(x, zero, zero)
            else:
                finish(x, message[lines : lines + 1, :], message[lines + 1 : lines + 2, :])

    def middle(x, carry):
        finish(x + LAYERS, velocity[1, x, 0:1, :], velocity[1, x, ny - 1 : ny, :])
        return carry

    lax.fori_loop(0, nx, middle, 0)


def basis(rhs_wide, inv_wide, ends, before, after, *refs):
    outs, dots, (im, ih, axm, axh, aym, ayh, azm, azh, hdm, hdh, vm, vh) = refs[: ITERS + 1], refs[ITERS + 1], refs[ITERS + 2 :]
    wide, rows, nz = inv_wide.shape
    nx, ny = wide - 2 * LAYERS, rows - 2 * WIDE
    group = nz // SLOT
    tile = (WIDE, nz)
    tiles = rows // WIDE
    lane = lanes(tile)
    first, last = lane == 0, lane == nz - 1

    def left(main, side):
        a, b = pltpu.roll(main, 1, 1), pltpu.roll(side, 1, 1)
        return jnp.where(first, b, a), jnp.where(first, a, b)

    def right(main, side):
        a, b = pltpu.roll(main, nz - 1, 1), pltpu.roll(side, nz - 1, 1)
        return jnp.where(last, b, a), jnp.where(last, a, b)

    def shifted(ref, x, t, step):
        start = t * WIDE + step
        if start < 0:
            return pltpu.roll(ref[x, 0:WIDE, :], 1, 0)
        if start + WIDE > rows:
            return pltpu.roll(ref[x, rows - WIDE : rows, :], WIDE - 1, 0)
        return ref[x, start : start + WIDE, :]

    def load(x, carry):
        g, s = x // group, (x % group) * SLOT
        for t in range(tiles):
            here = slice(t * WIDE, (t + 1) * WIDE)
            low, high = before[g, here, :], after[g, here, :]
            i = inv_wide[x, here, :]
            im[x, here, :] = i
            side = pltpu.roll(high, lax.rem(2 * nz - s - REACH - 1, nz), 1)
            other = pltpu.roll(low, lax.rem(2 * nz - s - REACH - 1 - LAYERS, nz), 1)
            ih[x, here, :] = jnp.where(lane < LAYERS, side, jnp.where(lane >= nz - LAYERS, other, 0.0))
            p = pltpu.roll(low, lax.rem(2 * nz - s - REACH, nz), 1)
            r = rhs_wide[x, here, :]
            r = r + jnp.where(first, p, 0.0) + jnp.where(last, side, 0.0)
            e = ends[x, here, :]
            q = pltpu.roll(high, lax.rem(nz - s, nz), 1)
            q = jnp.where(lane < REACH, q, 0.0) + jnp.where(first, 0.5 * e[:, nz - 1 : nz], 0.0)
            p = jnp.where(lane >= nz - REACH, p, 0.0) - jnp.where(last, 0.5 * e[:, 0:1], 0.0)
            vm[0, x, here, :] = r
            vh[0, x, here, :] = jnp.where(lane < REACH, q, p)
        return carry

    lax.fori_loop(0, wide, load, 0)

    def setup(x, carry):
        for t in range(tiles):
            here = slice(t * WIDE, (t + 1) * WIDE)
            m, h = im[x, here, :], ih[x, here, :]
            m_r, h_r = right(m, h)
            m_l, h_l = left(m, h)
            for ref, ax, ay, az, hd, v, c, c_r, c_l in (
                (im, axm, aym, azm, hdm, vm, m, m_r, m_l),
                (ih, axh, ayh, azh, hdh, vh, h, h_r, h_l),
            ):
                x_f, x_b = ref[x + 1, here, :], ref[x - 1, here, :]
                y_f, y_b = shifted(ref, x, t, 1), shifted(ref, x, t, -1)
                ax[x, here, :] = 0.5 * (c + x_f)
                ay[x, here, :] = 0.5 * (c + y_f)
                az[x, here, :] = 0.5 * (c + c_r)
                total = (x_f + x_b) + (y_f + y_b) + (c_r + c_l)
                diagonal = SHIFT + 0.5 * (6.0 * c + total)
                inverse = jnp.where(c > 0.0, 1.0 / diagonal, 0.0)
                hd[x, here, :] = inverse
                v[0, x, here, :] = v[0, x, here, :] * inverse
        return carry

    lax.fori_loop(1, wide - 1, setup, 0)
    for ref in (vm, vh):
        ref[0, 0] = jnp.zeros((rows, nz), F32)
        ref[0, wide - 1] = jnp.zeros((rows, nz), F32)
    for ref in (axm, axh):
        ref[0] = jnp.zeros((rows, nz), F32)

    def couple(k, x, t, sides):
        here = slice(t * WIDE, (t + 1) * WIDE)
        m, h = vm[k, x, here, :], vh[k, x, here, :]
        fm, fh = azm[x, here, :] * m, azh[x, here, :] * h
        m_r, h_r = right(m, h)
        m_l, h_l = left(fm, fh)
        result = []
        for v, ax, ay, az, c, c_r, c_l in (
            (vm, axm, aym, azm, m, m_r, m_l),
            (vh, axh, ayh, azh, h, h_r, h_l),
        )[:sides]:
            total = ax[x, here, :] * v[k, x + 1, here, :] + ax[x - 1, here, :] * v[k, x - 1, here, :]
            total = total + (az[x, here, :] * c_r + c_l)
            y_f = shifted(v.at[k], x, t, 1)
            y_b = shifted(v.at[k], x, t, -1)
            total = total + (ay[x, here, :] * y_f + shifted(ay, x, t, -1) * y_b)
            result.append((c, total))
        return result

    for k in range(ITERS - 1):
        scale = 1.0 - NEWTON[k]

        def step(x, carry, k=k, scale=scale):
            for t in range(tiles):
                here = slice(t * WIDE, (t + 1) * WIDE)
                for (c, total), hd, v in zip(couple(k, x, t, 2), (hdm, hdh), (vm, vh)):
                    value = -hd[x, here, :] * total
                    if scale:
                        value = value + scale * c
                    v[k + 1, x, here, :] = value
            return carry

        lax.fori_loop(2 + k, wide - 2 - k, step, 0)

    def measure(x, sums):
        sums = list(sums)
        for t in range(1, tiles - 1):
            here = slice(t * WIDE, (t + 1) * WIDE)
            (own, total), = couple(ITERS - 1, x, t, 1)
            d = 1.0 / hdm[x, here, :]
            v = [vm[k, x, here, :] for k in range(ITERS)]
            w = [d * one for one in v]
            for n, (a, b) in enumerate(PAIRS):
                sums[n] = sums[n] + v[a] * w[b]
            sums[-1] = sums[-1] + own * (w[-1] - total)
        return tuple(sums)

    sums = lax.fori_loop(
        LAYERS, LAYERS + nx, measure, (jnp.zeros(tile, F32),) * (len(PAIRS) + 1)
    )
    row = sublanes((2 * WIDE, nz))
    message = jnp.zeros((2 * WIDE, nz), F32)
    for n, one in enumerate(sums):
        message = jnp.where(row == n, jnp.sum(one, axis=0, keepdims=True), message)

    def send(n, carry):
        dots[n] = message
        return carry

    lax.fori_loop(0, dots.shape[0], send, 0)

    def result(x, carry):
        for k in range(ITERS):
            outs[k][x] = vm[k, x + LAYERS - 1]
        pieces = jnp.zeros((ny, nz), F32)
        for k in range(ITERS):
            side = vh[k, x + LAYERS - 1, WIDE : WIDE + ny, :]
            pieces = jnp.where(lanes((ny, nz)) == 2 * k, side[:, nz - 1 : nz], pieces)
            pieces = jnp.where(lanes((ny, nz)) == 2 * k + 1, side[:, 0:1], pieces)
        outs[ITERS][x] = pieces
        return carry

    lax.fori_loop(0, nx + 2, result, 0)


def coefficients(dots):
    total = jnp.sum(dots, axis=1, keepdims=True)

    def entry(n):
        return total[n : n + 1]

    gram = {}
    for n, (a, b) in enumerate(PAIRS):
        gram[a, b] = gram[b, a] = entry(n)
    last = ITERS - 1
    image = {}
    for b in range(last):
        for a in range(ITERS):
            image[a, b] = gram[a, b + 1]
            if NEWTON[b]:
                image[a, b] = image[a, b] + NEWTON[b] * gram[a, b]
    for a in range(last):
        image[a, last] = image[last, a]
    image[last, last] = entry(len(PAIRS))

    def product(table, one, two):
        total = None
        for a, left in enumerate(one):
            for b, right in enumerate(two):
                term = left * right * table[a, b]
                total = term if total is None else total + term
        return total

    unit = jnp.ones((1, 1), F32)
    pressure = []
    precond = [unit]
    direction = [unit]
    rz = gram[0, 0]
    for iteration in range(ITERS):
        alpha = rz / product(image, direction, direction)
        pressure = [
            (pressure[n] if n < len(pressure) else 0.0) + alpha * one for n, one in enumerate(direction)
        ]
        if iteration == last:
            break
        moved = []
        for n in range(len(direction) + 1):
            value = None
            if n < len(direction) and NEWTON[n]:
                value = NEWTON[n] * direction[n]
            if n > 0:
                value = direction[n - 1] if value is None else value + direction[n - 1]
            moved.append(value)
        fresh_precond = []
        for n, one in enumerate(moved):
            old = precond[n] if n < len(precond) else None
            if one is None:
                fresh_precond.append(old)
            else:
                fresh_precond.append(-alpha * one if old is None else old - alpha * one)
        precond = fresh_precond
        fresh = product(gram, precond, precond)
        beta = fresh / rz
        direction = [
            one + beta * direction[n] if n < len(direction) else one for n, one in enumerate(precond)
        ]
        rz = fresh
    return pressure


def finish(dots, velocity, inv, columns, *refs):
    spans = refs[:ITERS]
    sides = refs[ITERS]
    pressure, corrected, keep, keep_more, send, p, cut = refs[ITERS + 1 :]
    nx, ny, nz = inv.shape
    shape = (ny, nz)
    lane = lanes(shape)
    total = dots[0]
    for n in range(1, dots.shape[0]):
        total = total + dots[n]
    weights = coefficients(total)
    mixed = jnp.zeros((1, nz), F32)
    for k, one in enumerate(weights):
        mixed = jnp.where(lanes((1, nz)) // 2 == k, one, mixed)

    def combine(x, carry):
        value = weights[0] * spans[0][x]
        for k in range(1, ITERS):
            value = value + weights[k] * spans[k][x]
        p[x] = value
        return carry

    lax.fori_loop(0, nx + 2, combine, 0)
    mine = slice(WIDE, WIDE + ny)
    half = columns.shape[0] // 2
    ranks = half // 2

    def pair(n, carry):
        for which in range(2):
            x = 2 * n + which
            centre = p[x + 1, mine, :]
            gap = sides[x + 1] * mixed
            step = 2
            while step < 2 * ITERS:
                gap = gap + pltpu.roll(gap, nz - step, 1)
                step *= 2
            before = jnp.where(lane == 0, gap, pltpu.roll(centre, 1, 1))
            after = jnp.where(lane == nz - 1, pltpu.roll(gap, nz - 2, 1), pltpu.roll(centre, nz - 1, 1))
            pressure[x] = centre
            half_inv = 0.5 * inv[x]
            slopes = (
                p[x + 2, mine, :] - p[x, mine, :],
                p[x + 1, WIDE + 1 : WIDE + 1 + ny, :] - p[x + 1, WIDE - 1 : WIDE - 1 + ny, :],
                after - before,
            )
            fields = [velocity[d, x] - half_inv * slopes[d] for d in range(3)] + [centre]
            for d in range(3):
                corrected[d, x] = fields[d]
            for f, field in enumerate(fields):
                high = field.astype(BF16)
                low = (field - high.astype(F32)).astype(BF16)
                cut[f, which * ny : (which + 1) * ny, 0:nz] = high
                cut[f, which * ny : (which + 1) * ny, nz : 2 * nz] = low
        for f in range(4):
            out = lax.dot_general(
                columns[...], cut[f], (((1,), (1,)), ((), ())), preferred_element_type=F32
            )
            out = out[:half] + out[half:]
            block = f * (nx // 2) + n
            quarter = half // 4
            keep[block] = out[0:quarter]
            keep_more[block] = out[quarter : 2 * quarter]
            send[0, block] = out[2 * quarter : 3 * quarter]
            send[1, block] = out[3 * quarter :]
        return carry

    lax.fori_loop(0, nx // 2, pair, 0)


def split(value):
    high = value.astype(BF16)
    return high, (value - high.astype(F32)).astype(BF16)


def split_table(value):
    high = lax.reduce_precision(value, exponent_bits=8, mantissa_bits=7)
    return high.astype(BF16), (value - high).astype(BF16)


def three(a, b, dims=(((1,), (0,)), ((), ()))):
    dot = functools.partial(lax.dot_general, dimension_numbers=dims, preferred_element_type=F32)
    (ah, al), (bh, bl) = a, b
    return dot(ah, bh) + (dot(al, bh) + dot(ah, bl))


def rank_y(kept, came, wide_high, wide_low, keep, keep_more, send):
    blocks, ranks, nz = kept.shape
    group = wide_high.shape[0] // nz
    parts = []
    for n in range(blocks // group):
        parts.append(
            jnp.concatenate(
                [kept[n * group + q] + came[n * group + q] for q in range(group)], axis=1
            )
        )
    x = jnp.concatenate(parts, axis=0)
    out = three(split(x), (wide_high[...], wide_low[...]))
    quarter = out.shape[1] // 4
    keep[...] = out[:, 0:quarter]
    keep_more[...] = out[:, quarter : 2 * quarter]
    send[0] = out[:, 2 * quarter : 3 * quarter]
    send[1] = out[:, 3 * quarter :]


def rank_x(ranks, kept, came, wide_high, wide_low, *outs):
    u = kept[...] + came[...]
    rows, nz = u.shape
    group = wide_high.shape[0] // nz
    parts = []
    for f in range(rows // ranks // group):
        parts.append(
            jnp.concatenate(
                [u[(f * group + q) * ranks : (f * group + q + 1) * ranks] for q in range(group)], axis=1
            )
        )
    x = jnp.concatenate(parts, axis=0)
    out = three(split(x), (wide_high[...], wide_low[...]))
    width = out.shape[1] // len(outs)
    for n, ref in enumerate(outs):
        ref[...] = out[:, n * width : (n + 1) * width]


def last_core(kept, came, core):
    ranks_x, fields, ranks_y, ranks_z = core.shape
    z = jnp.transpose(kept[...] + came[...])
    for f in range(fields):
        core[:, f] = z[:, f * ranks_z : (f + 1) * ranks_z].reshape(ranks_x, ranks_y, ranks_z)


def relative(factor, axis):
    count = lax.axis_size(axis)
    order = [0]
    step = 1
    while step < count:
        order = order + [n + step for n in order]
        step *= 2
    bits = count.bit_length() - 1
    order = [sum(((n >> b) & 1) << (bits - 1 - b) for b in range(bits)) for n in range(count)]
    blocks = factor.reshape(factor.shape[0], count, factor.shape[1] // count)
    here = lax.axis_index(axis)
    picked = [
        lax.dynamic_index_in_dim(blocks, jnp.bitwise_xor(here, n), axis=1, keepdims=False) for n in order
    ]
    return jnp.stack(picked, axis=1)


def swap(value, axis, mask):
    count = lax.axis_size(axis)
    return lax.ppermute(value, axis, [(i, i ^ mask) for i in range(count)])


def per_device(velocity, inv_density, factor_x, factor_y, factor_z):
    nx, ny, nz = inv_density.shape
    wide, rows = nx + 2 * LAYERS, ny + 2 * WIDE
    devices = lax.axis_size("gx") * lax.axis_size("gy") * lax.axis_size("gz")
    group = nz // SLOT
    cells = (nx, ny, nz)

    message = (((REACH + 1 + LAYERS + 1) * ny + 2 * REACH), nz)
    rhs, up, down = call(pack_x, [cells, message, message], [velocity, inv_density])
    below, above = exchange(up, down, "gx")
    message = (wide // 2, ROWS, nz)
    up, down = call(pack_y, [message, message], [velocity, inv_density, rhs, below, above])
    before, after = exchange(up, down, "gy")
    message = (-(-wide // group), rows, nz)
    whole = (wide, rows, nz)
    rhs_wide, inv_wide, up, down, ends = call(
        pack_z,
        [whole, whole, message, message, whole],
        [velocity, inv_density, rhs, below, above, before, after],
    )
    before, after = exchange(up, down, "gz")
    span = (nx + 2, rows, nz)
    slots = (devices, 2 * WIDE, nz)
    *spans, dots = call(
        basis,
        [span] * ITERS + [(nx + 2, ny, nz), slots],
        [rhs_wide, inv_wide, ends, before, after],
        scratch=[whole] * 10 + [(ITERS,) + whole] * 2,
        limit=60,
    )
    dots = lax.all_to_all(dots, AXES, 0, 0, tiled=True)

    columns = relative(factor_z, "gz")
    count_z = lax.axis_size("gz")
    columns = jnp.transpose(columns.reshape(nz, -1))
    high, low = split_table(columns)
    columns = jnp.concatenate(
        [jnp.concatenate([high, high], axis=1), jnp.concatenate([low, low], axis=1)], axis=0
    )
    rank = factor_z.shape[1]
    ranks_z = rank // count_z
    blocks = 4 * nx // 2
    piece = (blocks, ranks_z, nz)
    pressure, corrected, keep, keep_more, send = pl.pallas_call(
        finish,
        out_shape=[
            jax.ShapeDtypeStruct(shape, F32)
            for shape in (cells, (3,) + cells, piece, piece, (2,) + piece)
        ],
        in_specs=[VMEM] * (4 + ITERS + 1),
        out_specs=[VMEM] * 5,
        scratch_shapes=[pltpu.VMEM(span, F32), pltpu.VMEM((4, 2 * ny, 2 * nz), BF16)],
        compiler_params=pltpu.CompilerParams(vmem_limit_bytes=56 * 2**20),
    )(dots, velocity, inv_density, columns, *spans)

    came = swap(send, "gz", 1)
    send = keep_more + came[1]
    keep = keep + came[0]
    came = swap(send, "gz", 2)

    group_y = nz // 16
    count_y = lax.axis_size("gy")
    ranks_y = rank // count_y
    planes = nz // ranks_y
    table = relative(factor_y, "gy")
    eye = jnp.eye(planes, dtype=F32)
    table = (eye[:, None, None, :, None] * table[None, :, :, None, :]).reshape(planes * ny, count_y * nz)
    keep, keep_more, send = call(
        rank_y,
        [(4 * nx // planes * ranks_z, nz)] * 2 + [(2, 4 * nx // planes * ranks_z, nz)],
        [keep, came, *split_table(table)],
    )
    came = swap(send, "gy", 1)
    send = keep_more + came[1]
    keep = keep + came[0]
    came = swap(send, "gy", 2)

    count_x = lax.axis_size("gx")
    table = relative(factor_x, "gx")
    eye = jnp.eye(ranks_y, dtype=F32)
    table = (table.reshape(nx, 1, rank, 1) * eye[None, :, None, :]).reshape(nx * ranks_y, rank * ranks_y)
    pieces = 2 if count_x > 1 else 1
    half = (4 * ranks_z, rank * ranks_y // 2)
    keep, send = call(
        functools.partial(rank_x, ranks_z), [half] * 2, [keep, came, *split_table(table)]
    )
    mask = 1
    while True:
        came = swap(send, "gx", mask)
        mask *= 2
        if mask >= count_x:
            break
        total = keep + came
        width = total.shape[1] // 2
        keep, send = total[:, :width], total[:, width:]
    core, = call(last_core, [(rank // count_x, 4, ranks_y, ranks_z)], [keep, came])
    return pressure, corrected, core


def solution(mesh):
    placed = (
        P(None, "gx", "gy", "gz"),
        P("gx", "gy", "gz"),
        P("gx", None),
        P("gy", None),
        P("gz", None),
    )
    return jax.shard_map(
        per_device,
        mesh=mesh,
        in_specs=placed,
        out_specs=(P("gx", "gy", "gz"), P(None, "gx", "gy", "gz"), P("gx", None, "gy", "gz")),
        check_vma=False,
    )
```

time: 683 us -> 208 us (0.30); the launches traced: 674 us -> 208 us
  blocking collectives: 283 us -> 0 us
  Pallas kernels: 0 us -> 91.9 us
  waiting for transfers between devices: 126 us -> 53.8 us
  other arithmetic: 73.7 us -> 13.6 us
  local copies, waits for them, and re-layouts: 77 us -> 22 us
  starting transfers between devices: 80.5 us -> 25.7 us
  between operations: 24.3 us -> 0.89 us
  matrix products: 10 us -> 0 us
    psum x7 -> x0, blocking collectives: 283 us -> none  [the longest x4 166 us: residual_product(): return lax.psum(jnp.sum(residual * precond), ('gx', 'gy', 'gz'))]
    pallas_call x0 -> x8, Pallas kernels: none -> 91.9 us  [the longest x7 76.3 us: call(): pl.pallas_call(body, out_shape=[jax.ShapeDtypeStruct(shape, F32) for shap...]
    ppermute x36 -> x11, starting transfers between devices: 80.1 us -> 18.5 us  [the longest x3 9.63 us: exchange(): below = lax.ppermute(up, axis, [(i, i + 1) for i in range(ends)])]
    unnamed x5 -> x0, waiting for transfers between devices: 49.9 us -> none
    reduce_sum x7 -> x0, other arithmetic: 42.5 us -> none  [the longest x4 32.1 us: per_device(): alpha = product / lax.psum(jnp.sum(direction * image), ('gx', 'gy', 'gz'))]
    slice x23 -> x0, local copies, waits for them, and re-layouts: 35.7 us -> none  [the longest x11 20.7 us: padded_2(): head = lax.slice_in_dim(cells, 0, width, axis=dim)]
    ppermute x12 -> x0, local copies, waits for them, and re-layouts: 21.8 us -> none  [the longest x6 11 us: padded_2(): lax.ppermute(tail, axis, [(i, (i + 1) % count) for i in range(ends)])]
    reduce_scatter x1 -> x0, waiting for transfers between devices: 20.2 us -> none  [per_device(): lax.psum_scatter(jnp.einsum('cfij,ia->acfj', shaped_z, columns, precision...]
  transfers between devices with their start and end apart: 39 -> 12, of which waited for: 29 -> 10; matrix products, arithmetic and copies ran while one was open for 4% -> 13% of each run, Pallas kernels for 0% -> 0%
where the time goes in v1:
time: 208 us
  Pallas kernels  91.9 us (44%)
  waiting for transfers between devices  53.8 us (26%)
  starting transfers between devices  25.7 us (12%)
  local copies, waits for them, and re-layouts  22 us (11%)
  other arithmetic  13.6 us (7%)
    pallas_call x7, Pallas kernels, call(): pl.pallas_call(body, out_shape=[jax.ShapeDtypeStruct(shape, F32) for shap...  76.3 us
    ppermute x5, waiting for transfers between devices, swap(): return lax.ppermute(value, axis, [(i, i ^ mask) for i in range(count)])  22.1 us
    pallas_call x1, Pallas kernels, per_device(): pl.pallas_call(finish, out_shape=[jax.ShapeDtypeStruct(shape, F32) for sh...  15.6 us
    mul x2, local copies, waits for them, and re-layouts, per_device(): table.reshape(nx, 1, rank, 1) * eye[None, :, None, :]  14.3 us
    ppermute x3, waiting for transfers between devices, exchange(): above = lax.ppermute(down, axis, [(i + 1, i) for i in range(ends)])  12.1 us
    ppermute x3, waiting for transfers between devices, exchange(): below = lax.ppermute(up, axis, [(i, i + 1) for i in range(ends)])  10 us
    ppermute x3, starting transfers between devices, exchange(): below = lax.ppermute(up, axis, [(i, i + 1) for i in range(ends)])  9.63 us
    all_to_all x1, waiting for transfers between devices, per_device(): dots = lax.all_to_all(dots, AXES, 0, 0, tiled=True)  9.6 us
  transfers between devices with their start and end apart: 12, of which 10 were waited for; matrix products, arithmetic and copies ran while one was open for 13% of the time, Pallas kernels for 0%

profile of v1, /device:TPU:0, one launch (start us, length us, event | category | flops | bytes accessed | tf_op | source)
XLA Modules:
  0.0 207.9 jit_solution(16967541272527382394)
XLA Ops:
  0.6 6.2 %shard_map.76 = (f32[32,64,128]{2,1,0:T(8,128)}, f32[712,128]{1,0:T(8,128)}, f32[712,128]{1,0:T(8,128)}) custom-call(f32[3,32,64,128]{3,2,1,0:T(8,128)} %velocity.7, f32[32,64,128]{2,1,0:T(8,128)} %inv.7), custom_call_target="tpu_custom_call" | custom-call | tf_op jit(solution)/shard_map/pallas_call | solution.py:28
  6.8 4.9 %collective-permute-start = (f32[712,128]{1,0:T(8,128)}, f32[712,128]{1,0:T(8,128)S(1)}, u32[]{:S(2)}, u32[]{:S(2)}) collective-permute-start(f32[712,128]{1,0:T(8,128)} %get-tuple-element.30), channel_id=1, source_target_pairs={{0,16},{1,17},{2,18},{3,19},{4,20},{5,21},{6,22},{7,23},{8,24},{9,... | collective-permute-start | bytes 1093640 | tf_op jit(solution)/shard_map/ppermute | solution.py:49
  11.6 1.3 collective-permute-start.1
  12.9 6.7 %collective-permute-done.below = f32[712,128]{1,0:T(8,128)S(1)} collective-permute-done((f32[712,128]{1,0:T(8,128)}, f32[712,128]{1,0:T(8,128)S(1)}, u32[]{:S(2)}, u32[]{:S(2)}) %collective-permute-start) | collective-permute-done | bytes 364576 | tf_op jit(solution)/shard_map/ppermute | solution.py:49
  19.7 4.0 %collective-permute-done.1.above = f32[712,128]{1,0:T(8,128)S(1)} collective-permute-done((f32[712,128]{1,0:T(8,128)}, f32[712,128]{1,0:T(8,128)S(1)}, u32[]{:S(2)}, u32[]{:S(2)}) %collective-permute-start.1) | collective-permute-done | bytes 364576 | tf_op jit(solution)/shard_map/ppermute | solution.py:50
  24.5 4.9 %shard_map.77 = (f32[21,24,128]{2,1,0:T(8,128)}, f32[21,24,128]{2,1,0:T(8,128)}) custom-call(f32[3,32,64,128]{3,2,1,0:T(8,128)} %velocity.7, f32[32,64,128]{2,1,0:T(8,128)} %inv.7, f32[32,64,128]{2,1,0:T(8,128)} %get-tuple-element.29.rhs, f32[712,128]{1,0:T(8,128)} %copy-done, f32[712,128]{1,0:T(8,128)} %copy-done.1), custom_call_target="tpu_custom_call" | custom-call | tf_op jit(solution)/shard_map/pallas_call | solution.py:28
  29.3 3.5 %collective-permute-start.2 = (f32[21,24,128]{2,1,0:T(8,128)}, f32[21,24,128]{2,1,0:T(8,128)S(1)}, u32[]{:S(2)}, u32[]{:S(2)}) collective-permute-start(f32[21,24,128]{2,1,0:T(8,128)} %get-tuple-element.32), channel_id=1, source_target_pairs={{0,4},{4,8},{8,12},{1,5},{5,9},{9,13},{2,6},{6,10},{10,14},{3,7},{... | collective-permute-start | bytes 774152 | tf_op jit(solution)/shard_map/ppermute | solution.py:49
  32.8 1.3 collective-permute-start.3
  34.1 3.3 %collective-permute-done.2.before = f32[21,24,128]{2,1,0:T(8,128)S(1)} collective-permute-done((f32[21,24,128]{2,1,0:T(8,128)}, f32[21,24,128]{2,1,0:T(8,128)S(1)}, u32[]{:S(2)}, u32[]{:S(2)}) %collective-permute-start.2) | collective-permute-done | bytes 258080 | tf_op jit(solution)/shard_map/ppermute | solution.py:49
  37.4 4.0 %collective-permute-done.3.after = f32[21,24,128]{2,1,0:T(8,128)S(1)} collective-permute-done((f32[21,24,128]{2,1,0:T(8,128)}, f32[21,24,128]{2,1,0:T(8,128)S(1)}, u32[]{:S(2)}, u32[]{:S(2)}) %collective-permute-start.3) | collective-permute-done | bytes 258080 | tf_op jit(solution)/shard_map/ppermute | solution.py:50
  42.1 13.6 %shard_map.78 = (f32[42,80,128]{2,1,0:T(8,128)}, f32[42,80,128]{2,1,0:T(8,128)}, f32[6,80,128]{2,1,0:T(8,128)}, f32[6,80,128]{2,1,0:T(8,128)}, f32[42,80,128]{2,1,0:T(8,128)}) custom-call(f32[3,32,64,128]{3,2,1,0:T(8,128)} %velocity.7, f32[32,64,128]{2,1,0:T(8,128)} %inv.7, f32[32,64,128]{2,1,0:T(8,128)} %get-tuple-element.29.rhs, f32[712,128]{1,0:T(8,128)} %copy-done, ...), custom_call_target="tpu_custom_call" | custom-call | tf_op jit(solution)/shard_map/pallas_call | solution.py:28
  55.7 1.3 collective-permute-start.4
  57.0 1.3 collective-permute-start.5
  58.3 4.0 %collective-permute-done.5.after = f32[6,80,128]{2,1,0:T(8,128)S(1)} collective-permute-done((f32[6,80,128]{2,1,0:T(8,128)}, f32[6,80,128]{2,1,0:T(8,128)S(1)}, u32[]{:S(2)}, u32[]{:S(2)}) %collective-permute-start.5) | collective-permute-done | bytes 245792 | tf_op jit(solution)/shard_map/ppermute | solution.py:50
  63.0 43.6 %shard_map.79 = (f32[34,80,128]{2,1,0:T(8,128)}, f32[34,80,128]{2,1,0:T(8,128)}, f32[34,80,128]{2,1,0:T(8,128)}, f32[34,80,128]{2,1,0:T(8,128)}, f32[34,64,128]{2,1,0:T(8,128)}, /*index=5*/f32[32,16,128]{2,1,0:T(8,128)}) custom-call(f32[42,80,128]{2,1,0:T(8,128)} %get-tuple-element.34.rhs_wide, f32[42,80,128]{2,1,0:T(8,128)} %get-tuple-element.35.inv_wide, ...), custom_call_target="tpu_custom_call" | custom-call | tf_op jit(solution)/shard_map/pallas_call | solution.py:28
  106.6 7.2 %all-to-all-start = ((f32[32,16,128]{2,1,0:T(8,128)}), f32[32,16,128]{2,1,0:T(8,128)S(1)}, u32[]{:S(2)}, u32[]{:S(2)}) async-start(f32[32,16,128]{2,1,0:T(8,128)} %get-tuple-element.39), calls=%async_computation | async-start | bytes 524288 | tf_op jit(solution)/shard_map/all_to_all | solution.py:677
  114.4 9.6 %all-to-all-done.dots = f32[32,16,128]{2,1,0:T(8,128)S(1)} async-done(((f32[32,16,128]{2,1,0:T(8,128)}), f32[32,16,128]{2,1,0:T(8,128)S(1)}, u32[]{:S(2)}, u32[]{:S(2)}) %all-to-all-start) | async-done | bytes 262176 | tf_op jit(solution)/shard_map/all_to_all | solution.py:677
  124.7 15.6 %shard_map.80 = (f32[32,64,128]{2,1,0:T(8,128)}, f32[3,32,64,128]{3,2,1,0:T(8,128)}, f32[64,16,128]{2,1,0:T(8,128)}, f32[64,16,128]{2,1,0:T(8,128)}, f32[2,64,16,128]{3,2,1,0:T(8,128)}) custom-call(f32[32,16,128]{2,1,0:T(8,128)} %copy-done.2, f32[3,32,64,128]{3,2,1,0:T(8,128)} %velocity.7, f32[32,64,128]{2,1,0:T(8,128)} %inv.7, ...), custom_call_target="tpu_custom_call" | custom-call | tf_op jit(solution)/shard_map/pallas_call | solution.py:690
  141.2 2.0 collective-permute-done.6
  144.3 1.5 collective-permute-start.7
  146.8 1.1 fusion.1
  147.9 10.8 %collective-permute-done.7.came = f32[64,16,128]{2,1,0:T(8,128)} collective-permute-done((f32[64,16,128]{2,1,0:T(8,128)}, f32[64,16,128]{2,1,0:T(8,128)}, u32[]{:S(2)}, u32[]{:S(2)}) %collective-permute-start.7) | collective-permute-done | bytes 524320 | tf_op jit(solution)/shard_map/ppermute | solution.py:644
  158.7 2.9 %shard_map.81 = (f32[256,128]{1,0:T(8,128)}, f32[256,128]{1,0:T(8,128)}, f32[2,256,128]{2,1,0:T(8,128)}) custom-call(f32[64,16,128]{2,1,0:T(8,128)} %get-tuple-element.66.kept, f32[64,16,128]{2,1,0:T(8,128)} %collective-permute-done.7.came, bf16[512,512]{1,0:T(8,128)(2,1)} %get-tuple-element.64.wide_high, bf16[512,512]{1,0:T(8,128)(2,1)} %get-tuple-element.63.wide_low), custom_call_target="tpu_custom_call" | custom-call | tf_op jit(solution)/shard_map/pallas_call | solution.py:28
  162.6 8.0 %broadcast_multiply_fusion = f32[32,16,64,16]{3,2,1,0:T(8,128)} fusion(f32[16,16]{1,0:T(8,128)S(1)} %fusion.7, f32[32,64]{1,0:T(8,128)S(1)} %mul.40), kind=kLoop, calls=%fused_computation | loop fusion | flops 524288 | bytes 2106368 | tf_op jit(solution)/shard_map/mul | solution.py:727
  170.5 14.2 %mul.44 = f32[512,1024]{1,0:T(8,128)S(1)} reshape(f32[32,16,64,16]{3,2,1,0:T(8,128)} %broadcast_multiply_fusion) | data formatting | bytes 4194304 | tf_op jit(solution)/shard_map/mul | solution.py:727
  185.5 1.4 collective-permute-start.9
  186.9 1.8 fusion
  188.7 4.9 %collective-permute-done.9.came = f32[256,128]{1,0:T(8,128)S(1)} collective-permute-done((f32[256,128]{1,0:T(8,128)S(1)}, f32[256,128]{1,0:T(8,128)S(1)}, u32[]{:S(2)}, u32[]{:S(2)}) %collective-permute-start.9) | collective-permute-done | bytes 131104 | tf_op jit(solution)/shard_map/ppermute | solution.py:644
  194.2 3.0 %shard_map.82 = (f32[64,512]{1,0:T(8,128)}, f32[64,512]{1,0:T(8,128)}) custom-call(f32[256,128]{1,0:T(8,128)} %get-tuple-element.68.kept, f32[256,128]{1,0:T(8,128)} %copy-done.9, bf16[512,1024]{1,0:T(8,128)(2,1)} %get-tuple-element.62.wide_high, bf16[512,1024]{1,0:T(8,128)(2,1)} %get-tuple-element.61.wide_low), custom_call_target="tpu_custom_call" | custom-call | tf_op jit(solution)/shard_map/pallas_call | solution.py:28
  198.1 4.3 %collective-permute-done.10.came = f32[64,512]{1,0:T(8,128)S(1)} collective-permute-done((f32[64,512]{1,0:T(8,128)}, f32[64,512]{1,0:T(8,128)S(1)}, u32[]{:S(2)}, u32[]{:S(2)}) %collective-permute-start.10) | collective-permute-done | bytes 131104 | tf_op jit(solution)/shard_map/ppermute | solution.py:644
  203.1 2.3 %shard_map.83 = f32[32,4,16,16]{3,2,1,0:T(8,128)} custom-call(f32[64,512]{1,0:T(8,128)} %get-tuple-element.53.kept, f32[64,512]{1,0:T(8,128)} %copy-done.10), custom_call_target="tpu_custom_call" | custom-call | tf_op jit(solution)/shard_map/pallas_call | solution.py:28
  205.4 2.5 %copy.12 = f32[32,4,16,16]{0,3,2,1:T(8,128)} copy(f32[32,4,16,16]{3,2,1,0:T(8,128)} %shard_map.83) | data formatting | bytes 262144
  (55 shorter events, 10.2 us)
Async XLA Ops:
  6.8 12.9 %collective-permute-start = (f32[712,128]{1,0:T(8,128)}, f32[712,128]{1,0:T(8,128)S(1)}, u32[]{:S(2)}, u32[]{:S(2)}) collective-permute-start(f32[712,128]{1,0:T(8,128)} %get-tuple-element.30), channel_id=1, source_target_pairs={{0,16},{1,17},{2,18},{3,19},{4,20},{5,21},{6,22},{7,23},{8,24},{9,... | collective-permute-start | bytes 1093640 | tf_op jit(solution)/shard_map/ppermute | solution.py:49
  11.6 12.1 %collective-permute-start.1 = (f32[712,128]{1,0:T(8,128)}, f32[712,128]{1,0:T(8,128)S(1)}, u32[]{:S(2)}, u32[]{:S(2)}) collective-permute-start(f32[712,128]{1,0:T(8,128)} %get-tuple-element.31), channel_id=1, source_target_pairs={{16,0},{17,1},{18,2},{19,3},{20,4},{21,5},{22,6},{23,7},{24,8},{25... | collective-permute-start | bytes 1093640 | tf_op jit(solution)/shard_map/ppermute | solution.py:50
  19.7 4.0 %copy-start = (f32[712,128]{1,0:T(8,128)}, f32[712,128]{1,0:T(8,128)S(1)}, u32[]{:S(2)}) copy-start(f32[712,128]{1,0:T(8,128)S(1)} %collective-permute-done.below) | copy-start | bytes 1093636
  23.7 0.7 copy-start.1
  29.3 8.1 %collective-permute-start.2 = (f32[21,24,128]{2,1,0:T(8,128)}, f32[21,24,128]{2,1,0:T(8,128)S(1)}, u32[]{:S(2)}, u32[]{:S(2)}) collective-permute-start(f32[21,24,128]{2,1,0:T(8,128)} %get-tuple-element.32), channel_id=1, source_target_pairs={{0,4},{4,8},{8,12},{1,5},{5,9},{9,13},{2,6},{6,10},{10,14},{3,7},{... | collective-permute-start | bytes 774152 | tf_op jit(solution)/shard_map/ppermute | solution.py:49
  32.8 8.6 %collective-permute-start.3 = (f32[21,24,128]{2,1,0:T(8,128)}, f32[21,24,128]{2,1,0:T(8,128)S(1)}, u32[]{:S(2)}, u32[]{:S(2)}) collective-permute-start(f32[21,24,128]{2,1,0:T(8,128)} %get-tuple-element.33), channel_id=1, source_target_pairs={{4,0},{8,4},{12,8},{5,1},{9,5},{13,9},{6,2},{10,6},{14,10},{7,3},{... | collective-permute-start | bytes 774152 | tf_op jit(solution)/shard_map/ppermute | solution.py:50
  37.4 4.0 %copy-start.5 = (f32[21,24,128]{2,1,0:T(8,128)}, f32[21,24,128]{2,1,0:T(8,128)S(1)}, u32[]{:S(2)}) copy-start(f32[21,24,128]{2,1,0:T(8,128)S(1)} %collective-permute-done.2.before) | copy-start | bytes 774148
  41.4 0.7 copy-start.6
  55.7 2.6 %collective-permute-start.4 = (f32[6,80,128]{2,1,0:T(8,128)}, f32[6,80,128]{2,1,0:T(8,128)S(1)}, u32[]{:S(2)}, u32[]{:S(2)}) collective-permute-start(f32[6,80,128]{2,1,0:T(8,128)} %get-tuple-element.37), channel_id=1, source_target_pairs={{0,1},{1,2},{2,3},{4,5},{5,6},{6,7},{8,9},{9,10},{10,11},{12,13},{... | collective-permute-start | bytes 737288 | tf_op jit(solution)/shard_map/ppermute | solution.py:49
  57.0 5.4 %collective-permute-start.5 = (f32[6,80,128]{2,1,0:T(8,128)}, f32[6,80,128]{2,1,0:T(8,128)S(1)}, u32[]{:S(2)}, u32[]{:S(2)}) collective-permute-start(f32[6,80,128]{2,1,0:T(8,128)} %get-tuple-element.38), channel_id=1, source_target_pairs={{1,0},{2,1},{3,2},{5,4},{6,5},{7,6},{9,8},{10,9},{11,10},{13,12},{... | collective-permute-start | bytes 737288 | tf_op jit(solution)/shard_map/ppermute | solution.py:50
  58.3 4.0 %copy-start.7 = (f32[6,80,128]{2,1,0:T(8,128)}, f32[6,80,128]{2,1,0:T(8,128)S(1)}, u32[]{:S(2)}) copy-start(f32[6,80,128]{2,1,0:T(8,128)S(1)} %collective-permute-done.4.before) | copy-start | bytes 737284
  62.4 0.7 copy-start.8
  63.0 50.7 %copy-start.13 = (f32[128,64]{0,1:T(8,128)S(1)}, f32[128,64]{0,1:T(8,128)}, u32[]{:S(2)}) copy-start(f32[128,64]{0,1:T(8,128)} %param.9) | copy-start | bytes 98308
  106.6 17.4 %all-to-all-start = ((f32[32,16,128]{2,1,0:T(8,128)}), f32[32,16,128]{2,1,0:T(8,128)S(1)}, u32[]{:S(2)}, u32[]{:S(2)}) async-start(f32[32,16,128]{2,1,0:T(8,128)} %get-tuple-element.39), calls=%async_computation | async-start | bytes 524288 | tf_op jit(solution)/shard_map/all_to_all | solution.py:677
  124.0 0.7 copy-start.2
  124.7 15.9 %copy-start.15 = (f32[32,64]{1,0:T(8,128)S(1)}, f32[32,64]{1,0:T(8,128)}, u32[]{:S(2)}) copy-start(f32[32,64]{1,0:T(8,128)} %param.7) | copy-start | bytes 24580
  124.7 16.0 %copy-start.14 = (f32[64,64]{1,0:T(8,128)S(1)}, f32[64,64]{1,0:T(8,128)}, u32[]{:S(2)}) copy-start(f32[64,64]{1,0:T(8,128)} %param.8) | copy-start | bytes 49156
  140.3 2.9 %collective-permute-start.6 = (f32[2,64,16,128]{3,2,1,0:T(8,128)}, f32[2,64,16,128]{3,2,1,0:T(8,128)S(1)}, u32[]{:S(2)}, u32[]{:S(2)}) collective-permute-start(f32[2,64,16,128]{3,2,1,0:T(8,128)} %get-tuple-element.48), channel_id=1, source_target_pairs={{0,1},{1,0},{2,3},{3,2},{4,5},{5,4},{6,7},{7,6},{8,9},{9,8},{10,11... | collective-permute-start | bytes 3145736 | tf_op jit(solution)/shard_map/ppermute | solution.py:644
  140.8 2.4 %copy-start.3 = (f32[64,16,128]{2,1,0:T(8,128)S(1)}, f32[64,16,128]{2,1,0:T(8,128)}, u32[]{:S(2)}) copy-start(f32[64,16,128]{2,1,0:T(8,128)} %get-tuple-element.47) | copy-start | bytes 1572868
  140.8 2.4 %copy-start.4 = (f32[64,16,128]{2,1,0:T(8,128)S(1)}, f32[64,16,128]{2,1,0:T(8,128)}, u32[]{:S(2)}) copy-start(f32[64,16,128]{2,1,0:T(8,128)} %get-tuple-element.49) | copy-start | bytes 1572868
  144.3 14.5 %collective-permute-start.7 = (f32[64,16,128]{2,1,0:T(8,128)}, f32[64,16,128]{2,1,0:T(8,128)}, u32[]{:S(2)}, u32[]{:S(2)}) collective-permute-start(f32[64,16,128]{2,1,0:T(8,128)} %get-tuple-element.65), channel_id=1, source_target_pairs={{0,2},{1,3},{2,0},{3,1},{4,6},{5,7},{6,4},{7,5},{8,10},{9,11},{10,... | collective-permute-start | bytes 1572872 | tf_op jit(solution)/shard_map/ppermute | solution.py:644
  161.6 23.1 %collective-permute-start.8 = (f32[2,256,128]{2,1,0:T(8,128)}, f32[2,256,128]{2,1,0:T(8,128)S(1)}, u32[]{:S(2)}, u32[]{:S(2)}) collective-permute-start(f32[2,256,128]{2,1,0:T(8,128)} %get-tuple-element.51), channel_id=1, source_target_pairs={{0,4},{4,0},{8,12},{12,8},{1,5},{5,1},{9,13},{13,9},{2,6},{6,2},{1... | collective-permute-start | bytes 786440 | tf_op jit(solution)/shard_map/ppermute | solution.py:644
  170.5 14.2 %copy-start.11 = (f32[256,128]{1,0:T(8,128)S(1)}, f32[256,128]{1,0:T(8,128)}, u32[]{:S(2)}) copy-start(f32[256,128]{1,0:T(8,128)} %get-tuple-element.50) | copy-start | bytes 393220
  170.5 14.2 %copy-start.12 = (f32[256,128]{1,0:T(8,128)S(1)}, f32[256,128]{1,0:T(8,128)}, u32[]{:S(2)}) copy-start(f32[256,128]{1,0:T(8,128)} %get-tuple-element.52) | copy-start | bytes 393220
  185.5 8.1 %collective-permute-start.9 = (f32[256,128]{1,0:T(8,128)S(1)}, f32[256,128]{1,0:T(8,128)S(1)}, u32[]{:S(2)}, u32[]{:S(2)}) collective-permute-start(f32[256,128]{1,0:T(8,128)S(1)} %get-tuple-element.67), channel_id=1, source_target_pairs={{0,8},{4,12},{8,0},{12,4},{1,9},{5,13},{9,1},{13,5},{2,10},{6,14},... | collective-permute-start | bytes 393224 | tf_op jit(solution)/shard_map/ppermute | solution.py:644
  193.6 0.7 copy-start.9
  197.2 5.2 %collective-permute-start.10 = (f32[64,512]{1,0:T(8,128)}, f32[64,512]{1,0:T(8,128)S(1)}, u32[]{:S(2)}, u32[]{:S(2)}) collective-permute-start(f32[64,512]{1,0:T(8,128)} %get-tuple-element.54), channel_id=1, source_target_pairs={{0,16},{16,0},{1,17},{17,1},{2,18},{18,2},{3,19},{19,3},{4,20},{20... | collective-permute-start | bytes 393224 | tf_op jit(solution)/shard_map/ppermute | solution.py:644
  202.4 0.7 copy-start.10

commit v2 on v1

v2 whole, which is shorter than its diff:
```python
import functools
import math

import jax
import jax.numpy as jnp
from jax import lax
from jax.experimental import pallas as pl
from jax.experimental.pallas import tpu as pltpu
from jax.sharding import PartitionSpec as P

ITERS = 4
SHIFT = 0.1
AXES = ("gx", "gy", "gz")

REACH = ITERS
LAYERS = ITERS + 1
WIDE = 8
SLOT = 16
STRIP = 2 * LAYERS
SPAN = 32
ROWS = 24
NEWTON = (0.5, 0.5, 0.5)
PAIRS = [(a, b) for a in range(ITERS) for b in range(a, ITERS)]
VMEM = pl.BlockSpec(memory_space=pltpu.VMEM)
SMEM = pl.BlockSpec(memory_space=pltpu.SMEM)
HBM = pl.BlockSpec(memory_space=pltpu.HBM)
F32 = jnp.float32
BF16 = jnp.bfloat16


def call(body, outs, operands, scratch=(), smem=0, limit=12, cost=None, far_in=(), far_out=(), sems=0):
    scratch = [pltpu.VMEM(shape, F32) if isinstance(shape, tuple) else shape for shape in scratch]
    return pl.pallas_call(
        body,
        out_shape=[
            pltpu.HBM(shape, F32) if n in far_out else jax.ShapeDtypeStruct(shape, F32)
            for n, shape in enumerate(outs)
        ],
        in_specs=[SMEM if n < smem else HBM if n in far_in else VMEM for n in range(len(operands))],
        out_specs=[HBM if n in far_out else VMEM for n in range(len(outs))],
        scratch_shapes=scratch + ([pltpu.SemaphoreType.DMA((sems,))] if sems else []),
        compiler_params=pltpu.CompilerParams(vmem_limit_bytes=limit * 2**20),
        cost_estimate=cost
        and pl.CostEstimate(flops=cost[0], bytes_accessed=cost[1], transcendentals=0),
    )(
        *(
            pltpu.with_memory_space_constraint(one, pltpu.HBM) if n in far_in else one
            for n, one in enumerate(operands)
        )
    )


def cost_of(shape):
    return 4 * math.prod(shape)


def lanes(shape):
    return lax.broadcasted_iota(jnp.int32, shape, len(shape) - 1)


def sublanes(shape):
    return lax.broadcasted_iota(jnp.int32, shape, len(shape) - 2)


def exchange(up, down, axis):
    count = lax.axis_size(axis)
    ends = count - 1
    below = lax.ppermute(up, axis, [(i, i + 1) for i in range(ends)])
    above = lax.ppermute(down, axis, [(i + 1, i) for i in range(ends)])
    return below, above


def source(velocity, x, nx):
    ny, nz = velocity.shape[2:]
    shape = (ny, nz)
    before = jnp.where(x == 0, 0.0, velocity[0, jnp.maximum(x - 1, 0)])
    after = jnp.where(x == nx - 1, 0.0, velocity[0, jnp.minimum(x + 1, nx - 1)])
    along_y = velocity[1, x]
    along_z = velocity[2, x]
    total = after - before
    total = total + jnp.where(sublanes(shape) == ny - 1, 0.0, pltpu.roll(along_y, ny - 1, 0))
    total = total - jnp.where(sublanes(shape) == 0, 0.0, pltpu.roll(along_y, 1, 0))
    total = total + jnp.where(lanes(shape) == nz - 1, 0.0, pltpu.roll(along_z, nz - 1, 1))
    total = total - jnp.where(lanes(shape) == 0, 0.0, pltpu.roll(along_z, 1, 1))
    return -0.5 * total


def sources(velocity, rhs):
    nx = rhs.shape[0]

    def plane(x, carry):
        rhs[x] = source(velocity, x, nx)
        return carry

    lax.fori_loop(0, nx, plane, 0)


def pack_x(index, velocity_far, inv_far, *refs):
    velocity, inv, sems = refs[-3:]
    messages = refs[:-3]
    layers, ny, nz = inv.shape[1:]
    far = inv_far.shape[0] - layers
    shape = (ny, nz)
    only = len(messages) == 1
    first = index[0] == 0

    def copies(n):
        start = jnp.where(first, far, 0) if only else (far, 0)[n]
        part = pl.ds(start, layers)
        yield pltpu.make_async_copy(inv_far.at[part], inv.at[n], sems.at[4 * n])
        for d in range(3):
            yield pltpu.make_async_copy(velocity_far.at[d, part], velocity.at[n, d], sems.at[4 * n + d + 1])

    for n in range(len(messages)):
        for copy in copies(n):
            copy.start()

    def fill(n, start, own, sign):
        message, near = messages[n], velocity.at[n]
        for k in range(REACH):
            message[k * ny : (k + 1) * ny, :] = source(near, start + k, layers)
        base = REACH * ny
        message[base : base + ny, :] = sign * near[0, own]
        base += ny
        for k in range(LAYERS):
            message[base : base + ny, :] = inv[n, k]
            base += ny
        ends = jnp.zeros(shape, F32)
        for k in range(REACH):
            plane_z = near[2, start + k]
            ends = jnp.where(lanes(shape) == 2 * k, plane_z[:, 0:1], ends)
            ends = jnp.where(lanes(shape) == 2 * k + 1, plane_z[:, nz - 1 : nz], ends)
        message[base : base + ny, :] = ends
        base += ny
        for k in range(REACH):
            message[base + 2 * k : base + 2 * k + 1, :] = near[1, start + k, 0:1, :]
            message[base + 2 * k + 1 : base + 2 * k + 2, :] = near[1, start + k, ny - 1 : ny, :]

    for n in range(len(messages)):
        for copy in copies(n):
            copy.wait()
    upper = (1, layers - 1, 0.5)
    lower = (0, 0, -0.5)
    if only:
        fill(0, *(jnp.where(first, one, two) for one, two in zip(upper, lower)))
    else:
        fill(0, *upper)
        fill(1, *lower)


class Scaled:
    def __init__(self, ref, factor):
        self.ref, self.factor = ref, factor

    def __getitem__(self, where):
        return self.ref[where] * self.factor


def sides_x(index, messages):
    if len(messages) == 2:
        return messages
    first = jnp.where(index[0] == 0, 1.0, 0.0)
    return Scaled(messages[0], 1.0 - first), Scaled(messages[0], first)


def pack_y(index, velocity, inv, rhs, *refs):
    (below, above), (up, down) = sides_x(index, refs[:-2]), refs[-2:]
    nx, ny, nz = inv.shape
    each = REACH + 1 + LAYERS + 1

    def put(pair, parity, rows_rhs, ghost, rows_inv, first, last):
        offset = parity * each
        for message, part in ((up, 1), (down, 0)):
            message[pair, pl.ds(offset, REACH), :] = rows_rhs[part]
            message[pair, pl.ds(offset + REACH, 1), :] = (0.5 if part else -0.5) * ghost[part]
            message[pair, pl.ds(offset + REACH + 1, LAYERS), :] = rows_inv[part]
            ends = jnp.zeros((1, nz), F32)
            for k in range(REACH):
                ends = jnp.where(lanes((1, nz)) == 2 * k, first[part][k : k + 1], ends)
                ends = jnp.where(lanes((1, nz)) == 2 * k + 1, last[part][k : k + 1], ends)
            message[pair, pl.ds(offset + each - 1, 1), :] = ends

    def halo(x, message, k_rhs, k_inv, extra):
        base = (REACH + 1 + k_inv) * ny
        rows_inv = (message[pl.ds(base, LAYERS), :], message[pl.ds(base + ny - LAYERS, LAYERS), :])
        zero_row = jnp.zeros((1, nz), F32)
        zero = jnp.zeros((REACH, nz), F32)
        if k_rhs is None:
            column = jnp.zeros((REACH, 1), F32)
            put(x // 2, x % 2, (zero, zero), (zero_row, zero_row), rows_inv, (column, column), (column, column))
            return
        low, high = message[pl.ds(k_rhs * ny, REACH), :], message[pl.ds((k_rhs + 1) * ny - REACH, REACH), :]
        if extra is not None:
            sign, source = extra
            low = low + sign * velocity[0, source, 0:REACH, :]
            high = high + sign * velocity[0, source, ny - REACH : ny, :]
        ends = (REACH + 1 + LAYERS) * ny
        lines = ends + ny + 2 * k_rhs
        ghost = (message[pl.ds(lines, 1), :], message[pl.ds(lines + 1, 1), :])
        head, tail = message[pl.ds(ends, REACH), :], message[pl.ds(ends + ny - REACH, REACH), :]
        first = (head[:, 2 * k_rhs : 2 * k_rhs + 1], tail[:, 2 * k_rhs : 2 * k_rhs + 1])
        last = (head[:, 2 * k_rhs + 1 : 2 * k_rhs + 2], tail[:, 2 * k_rhs + 1 : 2 * k_rhs + 2])
        put(x // 2, x % 2, (low, high), ghost, rows_inv, first, last)

    for k in range(LAYERS):
        halo(k, below, k - 1 if k else None, k, (-0.5, 0) if k == LAYERS - 1 else None)
        halo(
            nx + LAYERS + k,
            above,
            k if k < REACH else None,
            k,
            (0.5, nx - 1) if k == 0 else None,
        )

    def own(x, pair, parity, extra):
        low, high = rhs[x, 0:REACH, :], rhs[x, ny - REACH : ny, :]
        if extra is not None:
            low = low + extra[pl.ds(REACH * ny, REACH), :]
            high = high + extra[pl.ds((REACH + 1) * ny - REACH, REACH), :]
        ghost = (velocity[1, x, 0:1, :], velocity[1, x, ny - 1 : ny, :])
        rows_inv = (inv[x, 0:LAYERS, :], inv[x, ny - LAYERS : ny, :])
        head, tail = velocity[2, x, 0:REACH, :], velocity[2, x, ny - REACH : ny, :]
        first = (head[:, 0:1], tail[:, 0:1])
        last = (head[:, nz - 1 : nz], tail[:, nz - 1 : nz])
        put(pair, parity, (low, high), ghost, rows_inv, first, last)

    def at(x, extra):
        own(x, (x + LAYERS) // 2, (x + LAYERS) % 2, extra)

    at(0, below)
    at(nx - 1, above)
    begin = 1 + (1 + LAYERS) % 2
    finish = begin + (nx - 1 - begin) // 2 * 2
    for x in (*range(1, begin), *range(finish, nx - 1)):
        at(x, None)

    def planes(n, carry):
        for parity in range(2):
            own(begin + 2 * n + parity, (begin + LAYERS) // 2 + n, parity, None)
        return carry

    lax.fori_loop(0, (finish - begin) // 2, planes, 0)


def pack_z(index, velocity, inv, rhs, *refs):
    (below, above), before, after = sides_x(index, refs[:-14]), refs[-14], refs[-13]
    rhs_far, inv_far, up, down, strip_rhs_far, strip_inv_far = refs[-12:-6]
    rhs_wide, inv_wide, ends, strip_rhs, strip_inv, sems = refs[-6:]
    nx, ny, nz = inv.shape
    wide = nx + 2 * LAYERS
    rows = ny + 2 * WIDE
    each = REACH + 1 + LAYERS + 1
    mine = pl.ds(WIDE, ny)
    edge = (WIDE, nz)
    groups = strip_rhs.shape[0]

    for k in range(LAYERS):
        for message, x, layer in ((below, k, k - 1), (above, nx + LAYERS + k, k if k < REACH else -1)):
            base = (REACH + 1 + k) * ny
            inv_wide[x, mine, :] = message[pl.ds(base, ny), :]
            if layer < 0:
                rhs_wide[x, mine, :] = jnp.zeros((ny, nz), F32)
                ends[x, mine, :] = jnp.zeros((ny, nz), F32)
                continue
            part = message[pl.ds(layer * ny, ny), :]
            if x == LAYERS - 1:
                part = part - 0.5 * velocity[0, 0]
            if x == nx + LAYERS:
                part = part + 0.5 * velocity[0, nx - 1]
            rhs_wide[x, mine, :] = part
            line = message[pl.ds((REACH + 1 + LAYERS) * ny, ny), :]
            ends[x, mine, :] = jnp.where(
                lanes((ny, nz)) == 0, line[:, 2 * layer : 2 * layer + 1], line[:, 2 * layer + 1 : 2 * layer + 2]
            )

    def plane(x, carry):
        inv_wide[x + LAYERS, mine, :] = inv[x]
        rhs_wide[x + LAYERS, mine, :] = rhs[x]
        ends[x + LAYERS, mine, :] = velocity[2, x]
        return carry

    lax.fori_loop(0, nx, plane, 0)
    rhs_wide[LAYERS, mine, :] += below[pl.ds(REACH * ny, ny), :]
    rhs_wide[LAYERS + nx - 1, mine, :] += above[pl.ds(REACH * ny, ny), :]
    for ref in (rhs_wide, inv_wide, ends):
        for x in range(wide, ref.shape[0]):
            ref[x] = jnp.zeros((rows, nz), F32)

    def finish(x, ghost_low, ghost_high):
        low, high = before[x // 2], after[x // 2]
        low = jnp.where(x % 2 == 0, low, pltpu.roll(low, ROWS - each, 0))[0:SLOT]
        high = jnp.where(x % 2 == 0, high, pltpu.roll(high, ROWS - each, 0))[0:SLOT]
        part = pltpu.roll(low, WIDE - REACH, 0)[0:WIDE]
        part = jnp.where(sublanes(edge) >= WIDE - REACH, part, 0.0)
        part = part - jnp.where(sublanes(edge) == WIDE - 1, 0.5 * ghost_low, 0.0)
        rhs_wide[x, 0:WIDE, :] = part
        part = pltpu.roll(low, SLOT - (REACH + 1) + WIDE - LAYERS, 0)[0:WIDE]
        inv_wide[x, 0:WIDE, :] = jnp.where(sublanes(edge) >= WIDE - LAYERS, part, 0.0)
        part = jnp.where(sublanes(edge) < REACH, high[0:WIDE], 0.0)
        part = part + jnp.where(sublanes(edge) == 0, 0.5 * ghost_high, 0.0)
        rhs_wide[x, WIDE + ny : rows, :] = part
        part = pltpu.roll(high, SLOT - (REACH + 1), 0)[0:WIDE]
        inv_wide[x, WIDE + ny : rows, :] = jnp.where(sublanes(edge) < LAYERS, part, 0.0)
        head = rhs_wide[x, WIDE : 2 * WIDE, :]
        rhs_wide[x, WIDE : 2 * WIDE, :] = head + jnp.where(sublanes(edge) == 0, low[REACH : REACH + 1], 0.0)
        tail = rhs_wide[x, ny : WIDE + ny, :]
        rhs_wide[x, ny : WIDE + ny, :] = tail + jnp.where(
            sublanes(edge) == WIDE - 1, high[REACH : REACH + 1], 0.0
        )
        for message, start, place in ((low, WIDE - REACH, 0), (high, 0, WIDE + ny)):
            line = message[each - 1 : each]
            one = jnp.zeros(edge, F32)
            two = jnp.zeros(edge, F32)
            for k in range(REACH):
                here = sublanes(edge) == start + k
                one = jnp.where(here, line[:, 2 * k : 2 * k + 1], one)
                two = jnp.where(here, line[:, 2 * k + 1 : 2 * k + 2], two)
            ends[x, place : place + WIDE, :] = jnp.where(lanes(edge) == 0, one, two)

    for k in range(LAYERS):
        for message, x, layer in ((below, k, k - 1), (above, nx + LAYERS + k, k if k < REACH else -1)):
            lines = (REACH + 1 + LAYERS + 1) * ny + 2 * layer
            if layer < 0:
                zero = jnp.zeros((1, nz), F32)
                finish(x, zero, zero)
            else:
                finish(x, message[pl.ds(lines, 1), :], message[pl.ds(lines + 1, 1), :])

    def middle(x, carry):
        finish(x + LAYERS, velocity[1, x, 0:1, :], velocity[1, x, ny - 1 : ny, :])
        return carry

    lax.fori_loop(0, nx, middle, 0)
    copies = [
        pltpu.make_async_copy(ref.at[pl.ds(0, wide)], far, sems.at[n])
        for n, (ref, far) in enumerate(((rhs_wide, rhs_far), (inv_wide, inv_far)))
    ]
    for copy in copies:
        copy.start()

    whole = (rows, nz)
    lane = lanes(whole)
    place = lane % SPAN

    def back(value, step):
        return pltpu.roll(value, nz - step, 1)

    def gather(ref, g):
        value = None
        for n in range(nz // SPAN):
            moved = pltpu.roll(ref[g + n * groups], n * SPAN + STRIP, 1)
            value = moved if value is None else jnp.where(lane >= n * SPAN, moved, value)
        return value

    def pack(g):
        r, i, e = gather(rhs_wide, g), gather(inv_wide, g), gather(ends, g)
        apart = SPAN - 2 * STRIP
        for ref, value in ((strip_rhs, r), (strip_inv, i)):
            out = jnp.where(place < STRIP, value, 0.0)
            ref[g] = jnp.where(place >= SPAN - STRIP, pltpu.roll(value, apart, 1), out)
        ghost = jnp.where(place == STRIP, 0.5 * pltpu.roll(e, 1, 1), 0.0)
        ghost = jnp.where(place == SPAN - STRIP - 1, -0.5 * pltpu.roll(e, apart - 1, 1), ghost)
        strip_rhs[g] += ghost
        out = jnp.where(place < REACH, back(r, STRIP - REACH), 0.0)
        out = jnp.where(place == REACH, 0.5 * back(e, STRIP - 1 - REACH), out)
        here = (place > REACH) & (place <= REACH + LAYERS)
        higher = jnp.where(here, pltpu.roll(i, (nz + REACH + 1 + LAYERS - STRIP) % nz, 1), out)
        out = jnp.where(place < REACH, back(r, STRIP), 0.0)
        out = jnp.where(place == REACH, -0.5 * back(e, STRIP - REACH), out)
        return higher, jnp.where(here, back(i, STRIP - REACH - 1), out)

    halves = up.shape[0]

    def both(n, carry):
        one, two = pack(n)
        up[n] = one
        down[n] = two
        return carry

    lax.fori_loop(0, halves, both, 0)

    def more(n, carry):
        one, two = pack(n + halves)
        up[n] += pltpu.roll(one, SPAN // 2, 1)
        down[n] += pltpu.roll(two, SPAN // 2, 1)
        return carry

    lax.fori_loop(0, groups - halves, more, 0)
    for ref, far in ((strip_rhs, strip_rhs_far), (strip_inv, strip_inv_far)):
        copies.append(pltpu.make_async_copy(ref, far, sems.at[len(copies)]))
        copies[-1].start()
    for copy in copies:
        copy.wait()


def shifted(ref, x, t, step):
    rows = ref.shape[1]
    start = t * WIDE + step
    if start < 0:
        return pltpu.roll(ref[x, 0:WIDE, :], 1, 0)
    if start + WIDE > rows:
        return pltpu.roll(ref[x, rows - WIDE : rows, :], WIDE - 1, 0)
    return ref[x, start : start + WIDE, :]


class Stencil:
    def __init__(self, inv, root, ax, ay, az, vs, planes, edges=None):
        self.inv, self.root, self.ax, self.ay, self.az, self.vs = inv, root, ax, ay, az, vs
        self.planes, self.edges = planes, edges or (lambda ref: None)
        self.count, self.rows, self.nz = inv.shape
        self.tiles = self.rows // WIDE

    def here(self, t):
        return slice(t * WIDE, (t + 1) * WIDE)

    def right(self, value):
        return pltpu.roll(value, self.nz - 1, 1)

    def left(self, value):
        return pltpu.roll(value, 1, 1)

    def prepare(self, rhs):
        inv, root = self.inv, self.root
        self.edges(inv)

        def scales(x, carry):
            writes = []
            for t in range(self.tiles):
                here = self.here(t)
                c = inv[x, here, :]
                total = (inv[x + 1, here, :] + inv[x - 1, here, :]) + (self.right(c) + self.left(c))
                total = total + (shifted(inv, x, t, 1) + shifted(inv, x, t, -1))
                value = jnp.where(c > 0.0, lax.rsqrt(SHIFT + 0.5 * (6.0 * c + total)), 0.0)
                writes.append((here, value, rhs[x, here, :] * value))
            for here, one, two in writes:
                root[x, here, :] = one
                self.vs[0][x, here, :] = two
            return carry

        lax.fori_loop(1, self.count - 1, scales, 0)
        zero = jnp.zeros((self.rows, self.nz), F32)
        for ref in (root, self.vs[0]):
            ref[0] = zero
            ref[self.count - 1] = zero
            self.edges(ref)

        def couplings(x, carry):
            writes = []
            for t in range(self.tiles):
                here = self.here(t)
                c, d = inv[x, here, :], root[x, here, :]
                half = 0.5 * d
                writes.append(
                    (
                        here,
                        (c + inv[x + 1, here, :]) * (half * root[x + 1, here, :]),
                        (c + shifted(inv, x, t, 1)) * (half * shifted(root, x, t, 1)),
                        (c + self.right(c)) * (half * self.right(d)),
                    )
                )
            for here, x_face, y_face, z_face in writes:
                self.ax[x, here, :] = x_face
                self.ay[x, here, :] = y_face
                self.az[x, here, :] = z_face
            return carry

        lax.fori_loop(1, self.count - 1, couplings, 0)
        self.ax[0] = zero
        self.edges(self.ax)

    def couple(self, k, x, t):
        here = self.here(t)
        v, ax, ay = self.vs[k], self.ax, self.ay
        c, f = v[x, here, :], self.az[x, here, :]
        total = ax[x, here, :] * v[x + 1, here, :] + ax[x - 1, here, :] * v[x - 1, here, :]
        total = total + (f * self.right(c) + self.left(f * c))
        total = total + ay[x, here, :] * shifted(v, x, t, 1)
        return c, total + shifted(ay, x, t, -1) * shifted(v, x, t, -1)

    def extend(self, k):
        scale = 1.0 - NEWTON[k]

        def step(x, carry):
            writes = []
            for t in range(self.tiles):
                c, total = self.couple(k, x, t)
                writes.append((t, scale * c - total if scale else -total))
            for t, value in writes:
                self.vs[k + 1][x, self.here(t), :] = value
            return carry

        start, stop = self.planes(k)
        lax.fori_loop(start, stop, step, 0)
        self.edges(self.vs[k + 1])

    def products(self, start, stop, mask):
        def measure(x, sums):
            sums = list(sums)
            for t in range(1, self.tiles - 1):
                keep = mask(x)
                v = [self.vs[k][x, self.here(t), :] for k in range(ITERS)]
                own, total = self.couple(ITERS - 1, x, t)
                kept = [jnp.where(keep, one, 0.0) for one in v]
                for n, (a, b) in enumerate(PAIRS):
                    sums[n] = sums[n] + v[a] * kept[b]
                sums[-1] = sums[-1] + kept[-1] * (own - total)
            return tuple(sums)

        zero = jnp.zeros((WIDE, self.nz), F32)
        return lax.fori_loop(start, stop, measure, (zero,) * (len(PAIRS) + 1))


def basis_main(far_rhs, far_inv, *refs):
    outs, sums = refs[: ITERS + 1], refs[ITERS + 1]
    rhs, inv, root, ax, ay, az = refs[ITERS + 2 : ITERS + 8]
    vs, sems = refs[ITERS + 8 : -1], refs[-1]
    wide, rows, nz = ax.shape
    nx = wide - 2 * LAYERS
    loads = [
        pltpu.make_async_copy(far, ref, sems.at[n]) for n, (far, ref) in enumerate(((far_rhs, rhs), (far_inv, inv)))
    ]
    for load in loads:
        load.start()
    for load in loads:
        load.wait()
    stencil = Stencil(inv, root, ax, ay, az, vs, lambda k: (2 + k, wide - 2 - k))
    copies = []

    def send(n, ref):
        copy = pltpu.make_async_copy(ref.at[pl.ds(LAYERS - 1, nx + 2)], outs[n], sems.at[2 + n])
        copy.start()
        copies.append(copy)

    stencil.prepare(rhs)
    send(ITERS, root)
    send(0, vs[0])
    for k in range(ITERS - 1):
        stencil.extend(k)
        send(k + 1, vs[k + 1])
    lane = lanes((WIDE, nz))
    inner = (lane > REACH) & (lane < nz - 1 - REACH)
    for n, one in enumerate(stencil.products(LAYERS, LAYERS + nx, lambda x: inner)):
        sums[n] = one
    for copy in copies:
        copy.wait()


def basis_strips(nx, rhs_far, inv_far, before, after, sums, *refs):
    outs, dots = refs[:ITERS], refs[ITERS]
    rhs, inv, root, ax, ay, az = refs[ITERS + 1 : ITERS + 7]
    vs, strip_rhs, strip_inv, sems = refs[ITERS + 7 : -3], *refs[-3:]
    groups, rows, nz = strip_inv.shape
    loads = [
        pltpu.make_async_copy(far, ref, sems.at[ITERS + n])
        for n, (far, ref) in enumerate(((rhs_far, strip_rhs), (inv_far, strip_inv)))
    ]
    for load in loads:
        load.start()
    for load in loads:
        load.wait()
    halves = before.shape[0]
    whole = (rows, nz)
    place = lanes(whole) % SPAN

    def edges(ref):
        ref[0] = pltpu.roll(ref[groups], SPAN, 1)
        ref[groups + 1] = pltpu.roll(ref[1], nz - SPAN, 1)

    def receive(g, low, high):
        start = SPAN - STRIP - LAYERS
        moved = pltpu.roll(low, start + 1, 1)
        r = strip_rhs[g] + jnp.where((place > start) & (place <= SPAN - STRIP), moved, 0.0)
        moved = pltpu.roll(low, start - REACH - 1, 1)
        i = strip_inv[g] + jnp.where((place >= start) & (place < SPAN - STRIP), moved, 0.0)
        moved = pltpu.roll(high, STRIP, 1)
        r = r + jnp.where((place >= STRIP) & (place < STRIP + REACH), moved, 0.0)
        moved = pltpu.roll(high, STRIP - REACH - 1, 1)
        r = r + jnp.where(place == STRIP - 1, moved, 0.0)
        i = i + jnp.where((place >= STRIP) & (place < STRIP + LAYERS), moved, 0.0)
        rhs[g + 1] = r
        inv[g + 1] = i

    def first(n, carry):
        receive(n, before[n], after[n])
        return carry

    def second(n, carry):
        half = nz - SPAN // 2
        receive(n + halves, pltpu.roll(before[n], half, 1), pltpu.roll(after[n], half, 1))
        return carry

    lax.fori_loop(0, halves, first, 0)
    lax.fori_loop(0, groups - halves, second, 0)
    stencil = Stencil(inv, root, ax, ay, az, vs, lambda k: (1, groups + 1), edges)
    stencil.prepare(rhs)
    for k in range(ITERS - 1):
        stencil.extend(k)
    lane = lanes((WIDE, nz))
    part = lane // SPAN
    spot = lane % SPAN
    ends = ((spot >= STRIP - LAYERS) & (spot < STRIP)) | (
        (spot >= SPAN - STRIP) & (spot < SPAN - STRIP + LAYERS)
    )

    def mask(x):
        plane = x - 1 + part * groups
        return ends & (plane >= LAYERS) & (plane < LAYERS + nx)

    totals = []
    for n, one in enumerate(stencil.products(1, groups + 1, mask)):
        line = jnp.sum(one + sums[n], axis=0, keepdims=True)
        totals.append(line + pltpu.roll(line, nz // 2, 1))
    row = sublanes((WIDE, nz))
    message = jnp.zeros((WIDE, nz), F32)
    for n, line in enumerate(totals):
        half = lane < nz // 2 if n < WIDE else lane >= nz // 2
        message = jnp.where((row == n % WIDE) & half, line, message)

    def send(n, carry):
        dots[n] = message
        return carry

    lax.fori_loop(0, dots.shape[0], send, 0)

    def result(g, carry):
        for k in range(ITERS):
            vs[k][g] = vs[k][g] * root[g]
        return carry

    lax.fori_loop(1, groups + 1, result, 0)
    copies = [pltpu.make_async_copy(vs[k].at[pl.ds(1, groups)], outs[k], sems.at[k]) for k in range(ITERS)]
    for copy in copies:
        copy.start()
    for copy in copies:
        copy.wait()


def coefficients(dots):
    half = lanes(dots.shape) < dots.shape[1] // 2
    one = jnp.sum(jnp.where(half, dots, 0.0), axis=1, keepdims=True)
    two = jnp.sum(jnp.where(half, 0.0, dots), axis=1, keepdims=True)

    def entry(n):
        return one[n : n + 1] if n < WIDE else two[n - WIDE : n - WIDE + 1]

    gram = {}
    for n, (a, b) in enumerate(PAIRS):
        gram[a, b] = gram[b, a] = entry(n)
    last = ITERS - 1
    image = {}
    for b in range(last):
        for a in range(ITERS):
            image[a, b] = gram[a, b + 1]
            if NEWTON[b]:
                image[a, b] = image[a, b] + NEWTON[b] * gram[a, b]
    for a in range(last):
        image[a, last] = image[last, a]
    image[last, last] = entry(len(PAIRS))

    def product(table, one, two):
        total = None
        for a, left in enumerate(one):
            for b, right in enumerate(two):
                term = left * right * table[a, b]
                total = term if total is None else total + term
        return total

    unit = jnp.ones((1, 1), F32)
    pressure = []
    precond = [unit]
    direction = [unit]
    rz = gram[0, 0]
    for iteration in range(ITERS):
        alpha = rz / product(image, direction, direction)
        pressure = [
            (pressure[n] if n < len(pressure) else 0.0) + alpha * one for n, one in enumerate(direction)
        ]
        if iteration == last:
            break
        moved = []
        for n in range(len(direction) + 1):
            value = None
            if n < len(direction) and NEWTON[n]:
                value = NEWTON[n] * direction[n]
            if n > 0:
                value = direction[n - 1] if value is None else value + direction[n - 1]
            moved.append(value)
        fresh_precond = []
        for n, one in enumerate(moved):
            old = precond[n] if n < len(precond) else None
            if one is None:
                fresh_precond.append(old)
            else:
                fresh_precond.append(-alpha * one if old is None else old - alpha * one)
        precond = fresh_precond
        fresh = product(gram, precond, precond)
        beta = fresh / rz
        direction = [
            one + beta * direction[n] if n < len(direction) else one for n, one in enumerate(precond)
        ]
        rz = fresh
    return pressure


def finish(dots, columns, *refs):
    inputs = 2 * ITERS + 3
    pressure_far, corrected_far, keep, keep_more, send, p, gaps, mixed, cut, pressure, corrected = refs[inputs : inputs + 11]
    held, sems = refs[inputs + 11 : -1], refs[-1]
    loads = [pltpu.make_async_copy(far, ref, sems.at[n]) for n, (far, ref) in enumerate(zip(refs, held))]
    for load in loads:
        load.start()
    strips, spans, roots = held[:ITERS], held[ITERS : 2 * ITERS], held[2 * ITERS]
    velocity, inv = held[2 * ITERS + 1 :]
    nx, ny, nz = inv.shape
    shape = (ny, nz)
    groups = mixed.shape[0]
    total = dots[0]
    for n in range(1, dots.shape[0]):
        total = total + dots[n]
    weights = coefficients(total)

    def strip(g, carry):
        value = weights[0] * strips[0][g]
        for k in range(1, ITERS):
            value = value + weights[k] * strips[k][g]
        mixed[g] = value
        return carry

    for load in loads[:ITERS]:
        load.wait()
    lax.fori_loop(0, groups, strip, 0)
    for load in loads[ITERS : 2 * ITERS + 1]:
        load.wait()
    mine = slice(WIDE, WIDE + ny)
    lane = lanes(spans[0].shape[1:])

    def combine(x, carry):
        value = weights[0] * spans[0][x]
        for k in range(1, ITERS):
            value = value + weights[k] * spans[k][x]
        value = value * roots[x]
        plane = x + LAYERS - 1
        ends = mixed[plane % groups]
        start = plane // groups * SPAN
        last = pltpu.roll(ends, lax.rem(2 * nz - STRIP - start, nz), 1)
        first = pltpu.roll(ends, lax.rem(nz + STRIP - SPAN - start + nz, nz), 1)
        value = jnp.where(lane < LAYERS, first, jnp.where(lane >= nz - LAYERS, last, value))
        p[x] = value
        after = pltpu.roll(jnp.where(lane == 0, last, value), nz - 1, 1)
        before = pltpu.roll(jnp.where(lane == nz - 1, first, value), 1, 1)
        gaps[x] = (after - before)[mine]
        return carry

    lax.fori_loop(0, nx + 2, combine, 0)
    half = columns.shape[0] // 2
    for load in loads[2 * ITERS + 1 :]:
        load.wait()
    batch = 4
    each = nx // batch
    stores = []

    def pair(n, carry):
        for which in range(2):
            x = 2 * n + which
            centre = p[x + 1, mine, :]
            pressure[x] = centre
            half_inv = 0.5 * inv[x]
            slopes = (
                p[x + 2, mine, :] - p[x, mine, :],
                p[x + 1, WIDE + 1 : WIDE + 1 + ny, :] - p[x + 1, WIDE - 1 : WIDE - 1 + ny, :],
                gaps[x + 1],
            )
            fields = [velocity[d, x] - half_inv * slopes[d] for d in range(3)] + [centre]
            for d in range(3):
                corrected[d, x] = fields[d]
            for f, field in enumerate(fields):
                high = field.astype(BF16)
                low = (field - high.astype(F32)).astype(BF16)
                cut[f, which * ny : (which + 1) * ny, 0:nz] = high
                cut[f, which * ny : (which + 1) * ny, nz : 2 * nz] = low
        for f in range(4):
            out = lax.dot_general(
                columns[...], cut[f], (((1,), (1,)), ((), ())), preferred_element_type=F32
            )
            out = out[:half] + out[half:]
            block = f * (nx // 2) + n
            quarter = half // 4
            keep[block] = out[0:quarter]
            keep_more[block] = out[quarter : 2 * quarter]
            send[0, block] = out[2 * quarter : 3 * quarter]
            send[1, block] = out[3 * quarter :]
        return carry

    for n in range(batch):
        lax.fori_loop(n * each // 2, (n + 1) * each // 2, pair, 0)
        part = pl.ds(n * each, each)
        for ref, far in [(pressure.at[part], pressure_far.at[part])] + [
            (corrected.at[d, part], corrected_far.at[d, part]) for d in range(3)
        ]:
            store = pltpu.make_async_copy(ref, far, sems.at[len(loads) + len(stores)])
            store.start()
            stores.append(store)
    for store in stores:
        store.wait()


def tables(factor_y, factor_x, y_high, y_low, x_high, x_low, spread_high, spread_low):
    ny, rank = factor_y.shape
    nx = factor_x.shape[0]
    planes = y_high.shape[0] // ny
    nz = x_high.shape[1] // rank * planes
    count = y_high.shape[1] // nz
    ranks = rank // count
    wide = jnp.concatenate([factor_y[...], jnp.zeros((ny, nz - rank), F32)], axis=1)
    lane = lanes((ny, nz))
    for h in range(count):
        value = pltpu.roll(wide, (nz - h * ranks) % nz, 1)
        value = jnp.where(lane < ranks, value, 0.0)
        step = ranks
        while step < nz:
            value = value + pltpu.roll(value, step, 1)
            step *= 2
        for n in range(planes):
            high, low = split(jnp.where(lane // ranks == n, value, 0.0))
            y_high[n * ny : (n + 1) * ny, h * nz : (h + 1) * nz] = high
            y_low[n * ny : (n + 1) * ny, h * nz : (h + 1) * nz] = low
    width = x_high.shape[1]
    shape = (rank, width)
    copy = jnp.where(lanes(shape) // ranks == sublanes(shape), 1.0, 0.0).astype(BF16)
    for ref, value in zip((spread_high, spread_low), split(factor_x[...])):
        ref[...] = jnp.dot(value, copy, preferred_element_type=F32)
    shape = (ranks, width)
    here = lanes(shape) % ranks == sublanes(shape)

    def row(i, carry):
        at = pl.ds(pl.multiple_of(i * ranks, ranks), ranks)
        x_high[at, :] = jnp.where(here, spread_high[pl.ds(i, 1), :], 0.0).astype(BF16)
        x_low[at, :] = jnp.where(here, spread_low[pl.ds(i, 1), :], 0.0).astype(BF16)
        return carry

    lax.fori_loop(0, nx, row, 0)


def split(value):
    high = value.astype(BF16)
    return high, (value - high.astype(F32)).astype(BF16)


def split_table(value):
    high = lax.reduce_precision(value, exponent_bits=8, mantissa_bits=7)
    return high.astype(BF16), (value - high).astype(BF16)


def three(a, b, dims=(((1,), (0,)), ((), ()))):
    dot = functools.partial(lax.dot_general, dimension_numbers=dims, preferred_element_type=F32)
    (ah, al), (bh, bl) = a, b
    return dot(ah, bh) + (dot(al, bh) + dot(ah, bl))


def rank_y(kept, came, wide_high, wide_low, keep, keep_more, send):
    blocks, ranks, nz = kept.shape
    group = wide_high.shape[0] // nz
    parts = []
    for n in range(blocks // group):
        parts.append(
            jnp.concatenate(
                [kept[n * group + q] + came[n * group + q] for q in range(group)], axis=1
            )
        )
    x = jnp.concatenate(parts, axis=0)
    out = three(split(x), (wide_high[...], wide_low[...]))
    quarter = out.shape[1] // 4
    keep[...] = out[:, 0:quarter]
    keep_more[...] = out[:, quarter : 2 * quarter]
    send[0] = out[:, 2 * quarter : 3 * quarter]
    send[1] = out[:, 3 * quarter :]


def rank_x(ranks, kept, came, wide_high, wide_low, *outs):
    u = kept[...] + came[...]
    rows, nz = u.shape
    group = wide_high.shape[0] // nz
    parts = []
    for f in range(rows // ranks // group):
        parts.append(
            jnp.concatenate(
                [u[(f * group + q) * ranks : (f * group + q + 1) * ranks] for q in range(group)], axis=1
            )
        )
    x = jnp.concatenate(parts, axis=0)
    out = three(split(x), (wide_high[...], wide_low[...]))
    width = out.shape[1] // len(outs)
    for n, ref in enumerate(outs):
        ref[...] = out[:, n * width : (n + 1) * width]


def last_core(kept, came, core):
    ranks_x, fields, ranks_y, ranks_z = core.shape
    z = jnp.transpose(kept[...] + came[...])
    for f in range(fields):
        core[:, f] = z[:, f * ranks_z : (f + 1) * ranks_z].reshape(ranks_x, ranks_y, ranks_z)


def relative(factor, axis):
    count = lax.axis_size(axis)
    order = [0]
    step = 1
    while step < count:
        order = order + [n + step for n in order]
        step *= 2
    bits = count.bit_length() - 1
    order = [sum(((n >> b) & 1) << (bits - 1 - b) for b in range(bits)) for n in range(count)]
    blocks = factor.reshape(factor.shape[0], count, factor.shape[1] // count)
    here = lax.axis_index(axis)
    picked = [
        lax.dynamic_index_in_dim(blocks, jnp.bitwise_xor(here, n), axis=1, keepdims=False) for n in order
    ]
    return jnp.stack(picked, axis=1)


def swap(value, axis, mask):
    count = lax.axis_size(axis)
    return lax.ppermute(value, axis, [(i, i ^ mask) for i in range(count)])


def per_device(velocity, inv_density, factor_x, factor_y, factor_z):
    nx, ny, nz = inv_density.shape
    wide, rows = nx + 2 * LAYERS, ny + 2 * WIDE
    count_x, count_y, count_z = (lax.axis_size(axis) for axis in AXES)
    devices = count_x * count_y * count_z
    cells = (nx, ny, nz)
    rank = factor_x.shape[1]
    index = lax.axis_index("gx").reshape(1)

    shape = (((REACH + 1 + LAYERS + 1) * ny + 2 * REACH), nz)
    number = 1 if count_x == 2 else 2
    sent = call(
        pack_x,
        [shape] * number,
        [index, velocity, inv_density],
        scratch=[(number, 3, LAYERS, ny, nz), (number, LAYERS, ny, nz)],
        smem=1,
        far_in=(1, 2),
        sems=4 * number,
    )
    near = [swap(sent[0], "gx", 1)] if count_x == 2 else list(exchange(*sent, "gx"))
    rhs, = call(sources, [cells], [velocity], cost=(nx * ny * nz * 10, 4 * cost_of(cells)))
    shape = (wide // 2, ROWS, nz)
    up, down = call(pack_y, [shape, shape], [index, velocity, inv_density, rhs, *near], smem=1)
    before, after = exchange(up, down, "gy")
    parts = nz // SPAN
    groups = -(-wide // parts)
    message = (-(-groups // 2), rows, nz)
    whole = (groups * parts, rows, nz)
    strip = (groups, rows, nz)
    rhs_wide, inv_wide, up, down, strip_rhs, strip_inv = call(
        pack_z,
        [(wide, rows, nz)] * 2 + [message, message, strip, strip],
        [index, velocity, inv_density, rhs, *near, before, after],
        scratch=[whole] * 3 + [strip] * 2,
        smem=1,
        limit=18,
        far_out=(0, 1, 4, 5),
        sems=4,
    )
    before, after = exchange(up, down, "gz")
    span = (nx + 2, rows, nz)
    whole = (wide, rows, nz)
    *spans, sums = call(
        basis_main,
        [span] * (ITERS + 1) + [(len(PAIRS) + 1, WIDE, nz)],
        [rhs_wide, inv_wide],
        scratch=[whole] * (6 + ITERS),
        limit=22,
        cost=(wide * rows * nz * 100, 7 * cost_of(whole)),
        far_in=(0, 1),
        far_out=range(ITERS + 1),
        sems=ITERS + 3,
    )
    padded = (groups + 2, rows, nz)
    *strips, dots = call(
        functools.partial(basis_strips, nx),
        [strip] * ITERS + [(devices, WIDE, nz)],
        [strip_rhs, strip_inv, before, after, sums],
        scratch=[padded] * (6 + ITERS) + [strip] * 2,
        far_in=(0, 1),
        far_out=range(ITERS),
        sems=ITERS + 2,
    )
    dots = lax.all_to_all(dots, AXES, 0, 0, tiled=True)

    ranks_y, ranks_z = rank // count_y, rank // count_z
    planes = nz // ranks_y
    table_y, table_x = (planes * ny, count_y * nz), (nx * ranks_y, rank * ranks_y)
    y_high, y_low, x_high, x_low = pl.pallas_call(
        tables,
        out_shape=[jax.ShapeDtypeStruct(one, BF16) for one in (table_y, table_y, table_x, table_x)],
        in_specs=[VMEM] * 2,
        out_specs=[VMEM] * 4,
        scratch_shapes=[pltpu.VMEM((nx, rank * ranks_y), F32)] * 2,
        compiler_params=pltpu.CompilerParams(vmem_limit_bytes=16 * 2**20),
        cost_estimate=pl.CostEstimate(
            flops=4 * nx * ranks_y * rank * ranks_y, bytes_accessed=6 * 2**20, transcendentals=0
        ),
    )(relative(factor_y, "gy").reshape(ny, rank), relative(factor_x, "gx").reshape(nx, rank))
    columns = relative(factor_z, "gz")
    columns = jnp.transpose(columns.reshape(nz, -1))
    high, low = split_table(columns)
    columns = jnp.concatenate(
        [jnp.concatenate([high, high], axis=1), jnp.concatenate([low, low], axis=1)], axis=0
    )
    piece = (4 * nx // 2, ranks_z, nz)
    far = [*strips, *spans, velocity, inv_density]
    pressure, corrected, keep, keep_more, send = call(
        finish,
        [cells, (3,) + cells, piece, piece, (2,) + piece],
        [dots, columns, *far],
        scratch=[span, (nx + 2, ny, nz), strip, pltpu.VMEM((4, 2 * ny, 2 * nz), BF16), cells, (3,) + cells]
        + [one.shape for one in far],
        limit=32,
        far_in=range(2, 2 + len(far)),
        far_out=(0, 1),
        sems=len(far) + 16,
    )

    came = swap(send, "gz", 1)
    send = keep_more + came[1]
    keep = keep + came[0]
    came = swap(send, "gz", 2)

    shape = (4 * nx // planes * ranks_z, nz)
    keep, keep_more, send = call(
        rank_y, [shape] * 2 + [(2,) + shape], [keep, came, y_high, y_low], limit=16
    )
    came = swap(send, "gy", 1)
    send = keep_more + came[1]
    keep = keep + came[0]
    came = swap(send, "gy", 2)

    half = (4 * ranks_z, rank * ranks_y // 2)
    keep, send = call(
        functools.partial(rank_x, ranks_z), [half] * 2, [keep, came, x_high, x_low], limit=16
    )
    mask = 1
    while True:
        came = swap(send, "gx", mask)
        mask *= 2
        if mask >= count_x:
            break
        total = keep + came
        width = total.shape[1] // 2
        keep, send = total[:, :width], total[:, width:]
    core, = call(last_core, [(rank // count_x, 4, ranks_y, ranks_z)], [keep, came], limit=16)
    return pressure, corrected, core


def solution(mesh):
    placed = (
        P(None, "gx", "gy", "gz"),
        P("gx", "gy", "gz"),
        P("gx", None),
        P("gy", None),
        P("gz", None),
    )
    return jax.shard_map(
        per_device,
        mesh=mesh,
        in_specs=placed,
        out_specs=(P("gx", "gy", "gz"), P(None, "gx", "gy", "gz"), P("gx", None, "gy", "gz")),
        check_vma=False,
    )
```

time: 208 us -> 149 us (0.72)
  Pallas kernels: 91.9 us -> 69.8 us
  local copies, waits for them, and re-layouts: 22 us -> 1.79 us
  other arithmetic: 13.6 us -> 0.23 us
  starting transfers between devices: 25.7 us -> 20.1 us
    pallas_call x8 -> x11, Pallas kernels: 91.9 us -> 69.8 us  [the longest x10 68.9 us: call(): pl.pallas_call(body, out_shape=[pltpu.HBM(shape, F32) if n in far_out els...]
    ppermute x5 -> x6, waiting for transfers between devices: 22.1 us -> 39.9 us  [swap(): return lax.ppermute(value, axis, [(i, i ^ mask) for i in range(count)])]
    mul x4 -> x0, local copies, waits for them, and re-layouts: 15.1 us -> none  [the longest x2 14.3 us: per_device(): table.reshape(nx, 1, rank, 1) * eye[None, :, None, :]]
    mul x2 -> x0, other arithmetic: 8.24 us -> none  [the longest x1 7.96 us: per_device(): table.reshape(nx, 1, rank, 1) * eye[None, :, None, :]]
    ppermute x3 -> x2, waiting for transfers between devices: 12.1 us -> 4.14 us  [exchange(): above = lax.ppermute(down, axis, [(i + 1, i) for i in range(ends)])]
    ppermute x3 -> x2, waiting for transfers between devices: 10 us -> 3.26 us  [exchange(): below = lax.ppermute(up, axis, [(i, i + 1) for i in range(ends)])]
    unnamed x34 -> x12, local copies, waits for them, and re-layouts: 6.77 us -> 1.49 us
    ppermute x3 -> x2, starting transfers between devices: 9.63 us -> 5.05 us  [exchange(): below = lax.ppermute(up, axis, [(i, i + 1) for i in range(ends)])]
  transfers between devices with their start and end apart: 12 -> 11, of which waited for: 10 -> 9; matrix products, arithmetic and copies ran while one was open for 13% -> 0% of each run, Pallas kernels for 0% -> 19%
where the time goes in v2:
time: 149 us; the launch traced here: 148 us
  Pallas kernels  69.8 us (47%)
  waiting for transfers between devices  55.5 us (37%)
  starting transfers between devices  20.1 us (13%)
  local copies, waits for them, and re-layouts  1.79 us (1%)
    pallas_call x10, Pallas kernels, call(): pl.pallas_call(body, out_shape=[pltpu.HBM(shape, F32) if n in far_out els...  68.9 us
    ppermute x6, waiting for transfers between devices, swap(): return lax.ppermute(value, axis, [(i, i ^ mask) for i in range(count)])  39.9 us
    all_to_all x1, waiting for transfers between devices, per_device(): dots = lax.all_to_all(dots, AXES, 0, 0, tiled=True)  8.2 us
    all_to_all x1, starting transfers between devices, per_device(): dots = lax.all_to_all(dots, AXES, 0, 0, tiled=True)  7.8 us
    ppermute x2, starting transfers between devices, exchange(): below = lax.ppermute(up, axis, [(i, i + 1) for i in range(ends)])  5.05 us
    ppermute x6, starting transfers between devices, swap(): return lax.ppermute(value, axis, [(i, i ^ mask) for i in range(count)])  4.7 us
    ppermute x2, waiting for transfers between devices, exchange(): above = lax.ppermute(down, axis, [(i + 1, i) for i in range(ends)])  4.14 us
    ppermute x2, waiting for transfers between devices, exchange(): below = lax.ppermute(up, axis, [(i, i + 1) for i in range(ends)])  3.26 us
  transfers between devices with their start and end apart: 11, of which 9 were waited for; matrix products, arithmetic and copies ran while one was open for 0% of the time, Pallas kernels for 19%

profile of v2, /device:TPU:0, one launch (start us, length us, event | category | flops | bytes accessed | tf_op | source)
XLA Modules:
  0.0 148.4 jit_solution(6322001179125392285)
XLA Ops:
  0.6 1.6 %shard_map.77 = f32[712,128]{1,0:T(8,128)S(1)} custom-call(s32[1]{0:T(128)} %bitcast.index, f32[3,32,64,128]{3,2,1,0:T(8,128)} %refs_9_.1, f32[32,64,128]{2,1,0:T(8,128)} %refs_10_.1), custom_call_target="tpu_custom_call" | custom-call | tf_op jit(solution)/shard_map/pallas_call | solution.py:33
  2.2 3.0 %collective-permute-start = (f32[712,128]{1,0:T(8,128)S(1)}, f32[712,128]{1,0:T(8,128)S(1)}, u32[]{:S(2)}, u32[]{:S(2)}) collective-permute-start(f32[712,128]{1,0:T(8,128)S(1)} %shard_map.77), channel_id=1, source_target_pairs={{0,16},{16,0},{1,17},{17,1},{2,18},{18,2},{3,19},{19,3},{4,20},{20... | collective-permute-start | bytes 1093640 | tf_op jit(solution)/shard_map/ppermute | solution.py:923
  5.2 2.8 %shard_map.76.rhs = f32[32,64,128]{2,1,0:T(8,128)S(1)} custom-call(f32[3,32,64,128]{3,2,1,0:T(8,128)S(1)} %copy-done), custom_call_target="tpu_custom_call" | custom-call | flops 2621440 | bytes 4194304 | tf_op jit(solution)/shard_map/pallas_call | solution.py:33
  8.0 5.7 %collective-permute-done.refs_0_ = f32[712,128]{1,0:T(8,128)S(1)} collective-permute-done((f32[712,128]{1,0:T(8,128)S(1)}, f32[712,128]{1,0:T(8,128)S(1)}, u32[]{:S(2)}, u32[]{:S(2)}) %collective-permute-start) | collective-permute-done | bytes 364576 | tf_op jit(solution)/shard_map/ppermute | solution.py:923
  13.7 1.4 shard_map.78
  15.1 3.7 %collective-permute-start.1 = (f32[21,24,128]{2,1,0:T(8,128)S(1)}, f32[21,24,128]{2,1,0:T(8,128)S(1)}, u32[]{:S(2)}, u32[]{:S(2)}) collective-permute-start(f32[21,24,128]{2,1,0:T(8,128)S(1)} %get-tuple-element.36), channel_id=1, source_target_pairs={{0,4},{4,8},{8,12},{1,5},{5,9},{9,13},{2,6},{6,10},{10,14},{3,7},{... | collective-permute-start | bytes 774152 | tf_op jit(solution)/shard_map/ppermute | solution.py:68
  18.9 1.3 collective-permute-start.2
  20.2 3.3 %collective-permute-done.1.refs_1_ = f32[21,24,128]{2,1,0:T(8,128)S(1)} collective-permute-done((f32[21,24,128]{2,1,0:T(8,128)S(1)}, f32[21,24,128]{2,1,0:T(8,128)S(1)}, u32[]{:S(2)}, u32[]{:S(2)}) %collective-permute-start.1) | collective-permute-done | bytes 258080 | tf_op jit(solution)/shard_map/ppermute | solution.py:68
  23.5 4.1 %collective-permute-done.2.refs_2_ = f32[21,24,128]{2,1,0:T(8,128)S(1)} collective-permute-done((f32[21,24,128]{2,1,0:T(8,128)S(1)}, f32[21,24,128]{2,1,0:T(8,128)S(1)}, u32[]{:S(2)}, u32[]{:S(2)}) %collective-permute-start.2) | collective-permute-done | bytes 258080 | tf_op jit(solution)/shard_map/ppermute | solution.py:69
  27.6 10.3 %shard_map.79 = (f32[42,80,128]{2,1,0:T(8,128)}, f32[42,80,128]{2,1,0:T(8,128)}, f32[6,80,128]{2,1,0:T(8,128)}, f32[6,80,128]{2,1,0:T(8,128)S(1)}, f32[11,80,128]{2,1,0:T(8,128)}, /*index=5*/f32[11,80,128]{2,1,0:T(8,128)}) custom-call(s32[1]{0:T(128)} %bitcast.index, f32[3,32,64,128]{3,2,1,0:T(8,128)S(1)} %copy-done, f32[32,64,128]{2,1,0:T(8,128)S(1)} %copy-done.1, ...), custom_call_target="tpu_custom_call" | custom-call | tf_op jit(solution)/shard_map/pallas_call | solution.py:33
  37.9 1.3 collective-permute-start.3
  39.2 1.3 collective-permute-start.4
  40.6 24.0 %shard_map.80 = (f32[34,80,128]{2,1,0:T(8,128)}, f32[34,80,128]{2,1,0:T(8,128)}, f32[34,80,128]{2,1,0:T(8,128)}, f32[34,80,128]{2,1,0:T(8,128)}, f32[34,80,128]{2,1,0:T(8,128)}, /*index=5*/f32[11,8,128]{2,1,0:T(8,128)S(1)}) custom-call(f32[42,80,128]{2,1,0:T(8,128)} %get-tuple-element.42.far_rhs, f32[42,80,128]{2,1,0:T(8,128)} %get-tuple-element.43.far_inv), custom_call_target="tpu_custom_call" | custom-call | flops 43008000 | bytes 12042240 | tf_op jit(solution)/shard_map/pallas_call | solution.py:33
  64.7 12.4 %shard_map.81 = (f32[11,80,128]{2,1,0:T(8,128)}, f32[11,80,128]{2,1,0:T(8,128)}, f32[11,80,128]{2,1,0:T(8,128)}, f32[11,80,128]{2,1,0:T(8,128)}, f32[32,8,128]{2,1,0:T(8,128)}) custom-call(f32[11,80,128]{2,1,0:T(8,128)} %get-tuple-element.38.rhs_far, f32[11,80,128]{2,1,0:T(8,128)} %get-tuple-element.39.inv_far, ...), custom_call_target="tpu_custom_call" | custom-call | tf_op jit(solution)/shard_map/pallas_call | solution.py:33
  77.1 7.8 %all-to-all-start = ((f32[32,8,128]{2,1,0:T(8,128)}), f32[32,8,128]{2,1,0:T(8,128)S(1)}, u32[]{:S(2)}, u32[]{:S(2)}) async-start(f32[32,8,128]{2,1,0:T(8,128)} %get-tuple-element.45), calls=%async_computation | async-start | bytes 262144 | tf_op jit(solution)/shard_map/all_to_all | solution.py:990
  84.9 8.2 %all-to-all-done.dots = f32[32,8,128]{2,1,0:T(8,128)S(1)} async-done(((f32[32,8,128]{2,1,0:T(8,128)}), f32[32,8,128]{2,1,0:T(8,128)S(1)}, u32[]{:S(2)}, u32[]{:S(2)}) %all-to-all-start) | async-done | bytes 131104 | tf_op jit(solution)/shard_map/all_to_all | solution.py:990
  93.1 14.8 %shard_map.82 = (f32[32,64,128]{2,1,0:T(8,128)}, f32[3,32,64,128]{3,2,1,0:T(8,128)}, f32[64,16,128]{2,1,0:T(8,128)S(1)}, f32[64,16,128]{2,1,0:T(8,128)S(1)}, f32[2,64,16,128]{3,2,1,0:T(8,128)S(1)}) custom-call(f32[32,8,128]{2,1,0:T(8,128)S(1)} %all-to-all-done.dots, bf16[128,256]{1,0:T(8,128)(2,1)S(1)} %maximum_maximum_fusion.columns, ...), custom_call_target="tpu_custom_call" | custom-call | tf_op jit(solution)/shard_map/pallas_call | solution.py:33
  107.9 0.3 collective-permute-start.5
  108.3 2.4 %collective-permute-done.5 = f32[2,64,16,128]{3,2,1,0:T(8,128)S(1)} collective-permute-done((f32[2,64,16,128]{3,2,1,0:T(8,128)S(1)}, f32[2,64,16,128]{3,2,1,0:T(8,128)S(1)}, u32[]{:S(2)}, u32[]{:S(2)}) %collective-permute-start.5) | collective-permute-done | bytes 1048608 | tf_op jit(solution)/shard_map/ppermute | solution.py:923
  110.7 0.1 fusion
  110.8 0.6 collective-permute-start.6
  111.9 1.0 shard_map.83
  112.8 12.1 %collective-permute-done.6.came = f32[64,16,128]{2,1,0:T(8,128)S(1)} collective-permute-done((f32[64,16,128]{2,1,0:T(8,128)S(1)}, f32[64,16,128]{2,1,0:T(8,128)S(1)}, u32[]{:S(2)}, u32[]{:S(2)}) %collective-permute-start.6) | collective-permute-done | bytes 524320 | tf_op jit(solution)/shard_map/ppermute | solution.py:923
  124.9 0.6 shard_map.84
  125.6 7.6 %collective-permute-done.7 = f32[2,256,128]{2,1,0:T(8,128)S(1)} collective-permute-done((f32[2,256,128]{2,1,0:T(8,128)S(1)}, f32[2,256,128]{2,1,0:T(8,128)S(1)}, u32[]{:S(2)}, u32[]{:S(2)}) %collective-permute-start.7) | collective-permute-done | bytes 262176 | tf_op jit(solution)/shard_map/ppermute | solution.py:923
  133.3 0.5 collective-permute-start.8
  133.8 7.2 %collective-permute-done.8.came = f32[256,128]{1,0:T(8,128)S(1)} collective-permute-done((f32[256,128]{1,0:T(8,128)S(1)}, f32[256,128]{1,0:T(8,128)S(1)}, u32[]{:S(2)}, u32[]{:S(2)}) %collective-permute-start.8) | collective-permute-done | bytes 131104 | tf_op jit(solution)/shard_map/ppermute | solution.py:923
  141.0 0.7 shard_map.85
  141.6 0.2 collective-permute-start.9
  141.9 4.8 %collective-permute-done.9.came = f32[64,512]{1,0:T(8,128)S(1)} collective-permute-done((f32[64,512]{1,0:T(8,128)S(1)}, f32[64,512]{1,0:T(8,128)S(1)}, u32[]{:S(2)}, u32[]{:S(2)}) %collective-permute-start.9) | collective-permute-done | bytes 131104 | tf_op jit(solution)/shard_map/ppermute | solution.py:923
  146.7 0.3 shard_map.86
  147.0 1.4 copy.11
  (26 shorter events, 0.6 us)
Async XLA Ops:
  0.6 4.6 %copy-start = (f32[3,32,64,128]{3,2,1,0:T(8,128)S(1)}, f32[3,32,64,128]{3,2,1,0:T(8,128)}, u32[]{:S(2)}) copy-start(f32[3,32,64,128]{3,2,1,0:T(8,128)} %refs_9_.1) | copy-start | bytes 9437188
  2.2 11.5 %copy-start.1 = (f32[32,64,128]{2,1,0:T(8,128)S(1)}, f32[32,64,128]{2,1,0:T(8,128)}, u32[]{:S(2)}) copy-start(f32[32,64,128]{2,1,0:T(8,128)} %refs_10_.1) | copy-start | bytes 3145732
  2.2 11.5 %collective-permute-start = (f32[712,128]{1,0:T(8,128)S(1)}, f32[712,128]{1,0:T(8,128)S(1)}, u32[]{:S(2)}, u32[]{:S(2)}) collective-permute-start(f32[712,128]{1,0:T(8,128)S(1)} %shard_map.77), channel_id=1, source_target_pairs={{0,16},{16,0},{1,17},{17,1},{2,18},{18,2},{3,19},{19,3},{4,20},{20... | collective-permute-start | bytes 1093640 | tf_op jit(solution)/shard_map/ppermute | solution.py:923
  15.1 8.3 %collective-permute-start.1 = (f32[21,24,128]{2,1,0:T(8,128)S(1)}, f32[21,24,128]{2,1,0:T(8,128)S(1)}, u32[]{:S(2)}, u32[]{:S(2)}) collective-permute-start(f32[21,24,128]{2,1,0:T(8,128)S(1)} %get-tuple-element.36), channel_id=1, source_target_pairs={{0,4},{4,8},{8,12},{1,5},{5,9},{9,13},{2,6},{6,10},{10,14},{3,7},{... | collective-permute-start | bytes 774152 | tf_op jit(solution)/shard_map/ppermute | solution.py:68
  18.9 21.7 %copy-start.2 = (f32[128,64]{0,1:T(8,128)S(1)}, f32[128,64]{0,1:T(8,128)}, u32[]{:S(2)}) copy-start(f32[128,64]{0,1:T(8,128)} %param.9) | copy-start | bytes 98308
  18.9 8.7 %collective-permute-start.2 = (f32[21,24,128]{2,1,0:T(8,128)S(1)}, f32[21,24,128]{2,1,0:T(8,128)S(1)}, u32[]{:S(2)}, u32[]{:S(2)}) collective-permute-start(f32[21,24,128]{2,1,0:T(8,128)S(1)} %get-tuple-element.37), channel_id=1, source_target_pairs={{4,0},{8,4},{12,8},{5,1},{9,5},{13,9},{6,2},{10,6},{14,10},{7,3},{... | collective-permute-start | bytes 774152 | tf_op jit(solution)/shard_map/ppermute | solution.py:69
  37.9 26.7 %collective-permute-start.3 = (f32[6,80,128]{2,1,0:T(8,128)}, f32[6,80,128]{2,1,0:T(8,128)S(1)}, u32[]{:S(2)}, u32[]{:S(2)}) collective-permute-start(f32[6,80,128]{2,1,0:T(8,128)} %get-tuple-element.40), channel_id=1, source_target_pairs={{0,1},{1,2},{2,3},{4,5},{5,6},{6,7},{8,9},{9,10},{10,11},{12,13},{... | collective-permute-start | bytes 737288 | tf_op jit(solution)/shard_map/ppermute | solution.py:68
  39.2 25.4 %collective-permute-start.4 = (f32[6,80,128]{2,1,0:T(8,128)S(1)}, f32[6,80,128]{2,1,0:T(8,128)S(1)}, u32[]{:S(2)}, u32[]{:S(2)}) collective-permute-start(f32[6,80,128]{2,1,0:T(8,128)S(1)} %get-tuple-element.41), channel_id=1, source_target_pairs={{1,0},{2,1},{3,2},{5,4},{6,5},{7,6},{9,8},{10,9},{11,10},{13,12},{... | collective-permute-start | bytes 737288 | tf_op jit(solution)/shard_map/ppermute | solution.py:69
  77.1 16.0 %all-to-all-start = ((f32[32,8,128]{2,1,0:T(8,128)}), f32[32,8,128]{2,1,0:T(8,128)S(1)}, u32[]{:S(2)}, u32[]{:S(2)}) async-start(f32[32,8,128]{2,1,0:T(8,128)} %get-tuple-element.45), calls=%async_computation | async-start | bytes 262144 | tf_op jit(solution)/shard_map/all_to_all | solution.py:990
  107.9 2.7 %collective-permute-start.5 = (f32[2,64,16,128]{3,2,1,0:T(8,128)S(1)}, f32[2,64,16,128]{3,2,1,0:T(8,128)S(1)}, u32[]{:S(2)}, u32[]{:S(2)}) collective-permute-start(f32[2,64,16,128]{3,2,1,0:T(8,128)S(1)} %get-tuple-element.58), channel_id=1, source_target_pairs={{0,1},{1,0},{2,3},{3,2},{4,5},{5,4},{6,7},{7,6},{8,9},{9,8},{10,11... | collective-permute-start | bytes 3145736 | tf_op jit(solution)/shard_map/ppermute | solution.py:923
  110.7 0.8 copy-start.3
  110.7 0.9 copy-start.4
  110.8 14.2 %collective-permute-start.6 = (f32[64,16,128]{2,1,0:T(8,128)S(1)}, f32[64,16,128]{2,1,0:T(8,128)S(1)}, u32[]{:S(2)}, u32[]{:S(2)}) collective-permute-start(f32[64,16,128]{2,1,0:T(8,128)S(1)} %get-tuple-element.75), channel_id=1, source_target_pairs={{0,2},{1,3},{2,0},{3,1},{4,6},{5,7},{6,4},{7,5},{8,10},{9,11},{10,... | collective-permute-start | bytes 1572872 | tf_op jit(solution)/shard_map/ppermute | solution.py:923
  125.5 7.7 %collective-permute-start.7 = (f32[2,256,128]{2,1,0:T(8,128)S(1)}, f32[2,256,128]{2,1,0:T(8,128)S(1)}, u32[]{:S(2)}, u32[]{:S(2)}) collective-permute-start(f32[2,256,128]{2,1,0:T(8,128)S(1)} %get-tuple-element.63), channel_id=1, source_target_pairs={{0,4},{4,0},{8,12},{12,8},{1,5},{5,1},{9,13},{13,9},{2,6},{6,2},{1... | collective-permute-start | bytes 786440 | tf_op jit(solution)/shard_map/ppermute | solution.py:923
  133.3 7.7 %collective-permute-start.8 = (f32[256,128]{1,0:T(8,128)S(1)}, f32[256,128]{1,0:T(8,128)S(1)}, u32[]{:S(2)}, u32[]{:S(2)}) collective-permute-start(f32[256,128]{1,0:T(8,128)S(1)} %get-tuple-element.77), channel_id=1, source_target_pairs={{0,8},{4,12},{8,0},{12,4},{1,9},{5,13},{9,1},{13,5},{2,10},{6,14},... | collective-permute-start | bytes 393224 | tf_op jit(solution)/shard_map/ppermute | solution.py:923
  141.6 5.0 %collective-permute-start.9 = (f32[64,512]{1,0:T(8,128)S(1)}, f32[64,512]{1,0:T(8,128)S(1)}, u32[]{:S(2)}, u32[]{:S(2)}) collective-permute-start(f32[64,512]{1,0:T(8,128)S(1)} %get-tuple-element.68), channel_id=1, source_target_pairs={{0,16},{16,0},{1,17},{17,1},{2,18},{18,2},{3,19},{19,3},{4,20},{20... | collective-permute-start | bytes 393224 | tf_op jit(solution)/shard_map/ppermute | solution.py:923

commit v3 on v2

--- a/solution.py
+++ b/solution.py
@@ -92,7 +92,7 @@
         rhs[x] = source(velocity, x, nx)
         return carry
 
-    lax.fori_loop(0, nx, plane, 0)
+    lax.fori_loop(0, nx, plane, 0, unroll=4)
 
 
 def pack_x(index, velocity_far, inv_far, *refs):
@@ -239,7 +239,7 @@
             own(begin + 2 * n + parity, (begin + LAYERS) // 2 + n, parity, None)
         return carry
 
-    lax.fori_loop(0, (finish - begin) // 2, planes, 0)
+    lax.fori_loop(0, (finish - begin) // 2, planes, 0, unroll=3)
 
 
 def pack_z(index, velocity, inv, rhs, *refs):
@@ -279,7 +279,7 @@
         ends[x + LAYERS, mine, :] = velocity[2, x]
         return carry
 
-    lax.fori_loop(0, nx, plane, 0)
+    lax.fori_loop(0, nx, plane, 0, unroll=4)
     rhs_wide[LAYERS, mine, :] += below[pl.ds(REACH * ny, ny), :]
     rhs_wide[LAYERS + nx - 1, mine, :] += above[pl.ds(REACH * ny, ny), :]
     for ref in (rhs_wide, inv_wide, ends):
@@ -330,7 +330,7 @@
         finish(x + LAYERS, velocity[1, x, 0:1, :], velocity[1, x, ny - 1 : ny, :])
         return carry
 
-    lax.fori_loop(0, nx, middle, 0)
+    lax.fori_loop(0, nx, middle, 0, unroll=4)
     copies = [
         pltpu.make_async_copy(ref.at[pl.ds(0, wide)], far, sems.at[n])
         for n, (ref, far) in enumerate(((rhs_wide, rhs_far), (inv_wide, inv_far)))
@@ -377,7 +377,7 @@
         down[n] = two
         return carry
 
-    lax.fori_loop(0, halves, both, 0)
+    lax.fori_loop(0, halves, both, 0, unroll=2)
 
     def more(n, carry):
         one, two = pack(n + halves)
@@ -385,7 +385,7 @@
         down[n] += pltpu.roll(two, SPAN // 2, 1)
         return carry
 
-    lax.fori_loop(0, groups - halves, more, 0)
+    lax.fori_loop(0, groups - halves, more, 0, unroll=2)
     for ref, far in ((strip_rhs, strip_rhs_far), (strip_inv, strip_inv_far)):
         copies.append(pltpu.make_async_copy(ref, far, sems.at[len(copies)]))
         copies[-1].start()
@@ -437,7 +437,7 @@
                 self.vs[0][x, here, :] = two
             return carry
 
-        lax.fori_loop(1, self.count - 1, scales, 0)
+        lax.fori_loop(1, self.count - 1, scales, 0, unroll=4)
         zero = jnp.zeros((self.rows, self.nz), F32)
         for ref in (root, self.vs[0]):
             ref[0] = zero
@@ -464,7 +464,7 @@
                 self.az[x, here, :] = z_face
             return carry
 
-        lax.fori_loop(1, self.count - 1, couplings, 0)
+        lax.fori_loop(1, self.count - 1, couplings, 0, unroll=4)
         self.ax[0] = zero
         self.edges(self.ax)
 
@@ -490,7 +490,7 @@
             return carry
 
         start, stop = self.planes(k)
-        lax.fori_loop(start, stop, step, 0)
+        lax.fori_loop(start, stop, step, 0, unroll=4)
         self.edges(self.vs[k + 1])
 
     def products(self, start, stop, mask):
@@ -507,7 +507,7 @@
             return tuple(sums)
 
         zero = jnp.zeros((WIDE, self.nz), F32)
-        return lax.fori_loop(start, stop, measure, (zero,) * (len(PAIRS) + 1))
+        return lax.fori_loop(start, stop, measure, (zero,) * (len(PAIRS) + 1), unroll=2)
 
 
 def basis_main(far_rhs, far_inv, *refs):
@@ -589,8 +589,8 @@
         receive(n + halves, pltpu.roll(before[n], half, 1), pltpu.roll(after[n], half, 1))
         return carry
 
-    lax.fori_loop(0, halves, first, 0)
-    lax.fori_loop(0, groups - halves, second, 0)
+    lax.fori_loop(0, halves, first, 0, unroll=3)
+    lax.fori_loop(0, groups - halves, second, 0, unroll=3)
     stencil = Stencil(inv, root, ax, ay, az, vs, lambda k: (1, groups + 1), edges)
     stencil.prepare(rhs)
     for k in range(ITERS - 1):
@@ -620,14 +620,14 @@
         dots[n] = message
         return carry
 
-    lax.fori_loop(0, dots.shape[0], send, 0)
+    lax.fori_loop(0, dots.shape[0], send, 0, unroll=8)
 
     def result(g, carry):
         for k in range(ITERS):
             vs[k][g] = vs[k][g] * root[g]
         return carry
 
-    lax.fori_loop(1, groups + 1, result, 0)
+    lax.fori_loop(1, groups + 1, result, 0, unroll=4)
     copies = [pltpu.make_async_copy(vs[k].at[pl.ds(1, groups)], outs[k], sems.at[k]) for k in range(ITERS)]
     for copy in copies:
         copy.start()
@@ -728,7 +728,7 @@
 
     for load in loads[:ITERS]:
         load.wait()
-    lax.fori_loop(0, groups, strip, 0)
+    lax.fori_loop(0, groups, strip, 0, unroll=4)
     for load in loads[ITERS : 2 * ITERS + 1]:
         load.wait()
     mine = slice(WIDE, WIDE + ny)
@@ -751,7 +751,7 @@
         gaps[x] = (after - before)[mine]
         return carry
 
-    lax.fori_loop(0, nx + 2, combine, 0)
+    lax.fori_loop(0, nx + 2, combine, 0, unroll=4)
     half = columns.shape[0] // 2
     for load in loads[2 * ITERS + 1 :]:
         load.wait()
@@ -792,7 +792,7 @@
         return carry
 
     for n in range(batch):
-        lax.fori_loop(n * each // 2, (n + 1) * each // 2, pair, 0)
+        lax.fori_loop(n * each // 2, (n + 1) * each // 2, pair, 0, unroll=2)
         part = pl.ds(n * each, each)
         for ref, far in [(pressure.at[part], pressure_far.at[part])] + [
             (corrected.at[d, part], corrected_far.at[d, part]) for d in range(3)
@@ -838,7 +838,7 @@
         x_low[at, :] = jnp.where(here, spread_low[pl.ds(i, 1), :], 0.0).astype(BF16)
         return carry
 
-    lax.fori_loop(0, nx, row, 0)
+    lax.fori_loop(0, nx, row, 0, unroll=4)
 
 
 def split(value):

time: 149 us -> 126 us (0.85)
  Pallas kernels: 69.8 us -> 45.2 us
  waiting for transfers between devices: 55.5 us -> 57.2 us
    pallas_call x10, Pallas kernels: 68.9 us -> 44.3 us  [call(): pl.pallas_call(body, out_shape=[pltpu.HBM(shape, F32) if n in far_out els...]
    ppermute x6, waiting for transfers between devices: 39.9 us -> 41.6 us  [swap(): return lax.ppermute(value, axis, [(i, i ^ mask) for i in range(count)])]
  transfers between devices with their start and end apart: 11 -> 11, of which waited for: 9 -> 9; matrix products, arithmetic and copies ran while one was open for 0% -> 0% of each run, Pallas kernels for 19% -> 11%
where the time goes in v3:
time: 126 us; the launch traced here: 125 us
  waiting for transfers between devices  57.2 us (45%)
  Pallas kernels  45.2 us (36%)
  starting transfers between devices  20.2 us (16%)
  local copies, waits for them, and re-layouts  1.79 us (1%)
    pallas_call x10, Pallas kernels, call(): pl.pallas_call(body, out_shape=[pltpu.HBM(shape, F32) if n in far_out els...  44.3 us
    ppermute x6, waiting for transfers between devices, swap(): return lax.ppermute(value, axis, [(i, i ^ mask) for i in range(count)])  41.6 us
    all_to_all x1, waiting for transfers between devices, per_device(): dots = lax.all_to_all(dots, AXES, 0, 0, tiled=True)  8.2 us
    all_to_all x1, starting transfers between devices, per_device(): dots = lax.all_to_all(dots, AXES, 0, 0, tiled=True)  7.8 us
    ppermute x2, starting transfers between devices, exchange(): below = lax.ppermute(up, axis, [(i, i + 1) for i in range(ends)])  5.05 us
    ppermute x6, starting transfers between devices, swap(): return lax.ppermute(value, axis, [(i, i ^ mask) for i in range(count)])  4.73 us
    ppermute x2, waiting for transfers between devices, exchange(): above = lax.ppermute(down, axis, [(i + 1, i) for i in range(ends)])  4.14 us
    ppermute x2, waiting for transfers between devices, exchange(): below = lax.ppermute(up, axis, [(i, i + 1) for i in range(ends)])  3.26 us
  transfers between devices with their start and end apart: 11, of which 9 were waited for; matrix products, arithmetic and copies ran while one was open for 0% of the time, Pallas kernels for 11%

profile of v3, /device:TPU:0, one launch (start us, length us, event | category | flops | bytes accessed | tf_op | source)
XLA Modules:
  0.0 125.4 jit_solution(3514861782222556324)
XLA Ops:
  0.6 1.6 %shard_map.77 = f32[712,128]{1,0:T(8,128)S(1)} custom-call(s32[1]{0:T(128)} %bitcast.index, f32[3,32,64,128]{3,2,1,0:T(8,128)} %refs_9_.1, f32[32,64,128]{2,1,0:T(8,128)} %refs_10_.1), custom_call_target="tpu_custom_call" | custom-call | tf_op jit(solution)/shard_map/pallas_call | solution.py:33
  2.2 3.0 %collective-permute-start = (f32[712,128]{1,0:T(8,128)S(1)}, f32[712,128]{1,0:T(8,128)S(1)}, u32[]{:S(2)}, u32[]{:S(2)}) collective-permute-start(f32[712,128]{1,0:T(8,128)S(1)} %shard_map.77), channel_id=1, source_target_pairs={{0,16},{16,0},{1,17},{17,1},{2,18},{18,2},{3,19},{19,3},{4,20},{20... | collective-permute-start | bytes 1093640 | tf_op jit(solution)/shard_map/ppermute | solution.py:923
  5.2 1.1 shard_map.76.rhs
  6.3 7.4 %collective-permute-done.refs_0_ = f32[712,128]{1,0:T(8,128)S(1)} collective-permute-done((f32[712,128]{1,0:T(8,128)S(1)}, f32[712,128]{1,0:T(8,128)S(1)}, u32[]{:S(2)}, u32[]{:S(2)}) %collective-permute-start) | collective-permute-done | bytes 364576 | tf_op jit(solution)/shard_map/ppermute | solution.py:923
  13.7 0.7 shard_map.78
  14.5 3.7 %collective-permute-start.1 = (f32[21,24,128]{2,1,0:T(8,128)S(1)}, f32[21,24,128]{2,1,0:T(8,128)S(1)}, u32[]{:S(2)}, u32[]{:S(2)}) collective-permute-start(f32[21,24,128]{2,1,0:T(8,128)S(1)} %get-tuple-element.36), channel_id=1, source_target_pairs={{0,4},{4,8},{8,12},{1,5},{5,9},{9,13},{2,6},{6,10},{10,14},{3,7},{... | collective-permute-start | bytes 774152 | tf_op jit(solution)/shard_map/ppermute | solution.py:68
  18.2 1.3 %collective-permute-start.2 = (f32[21,24,128]{2,1,0:T(8,128)S(1)}, f32[21,24,128]{2,1,0:T(8,128)S(1)}, u32[]{:S(2)}, u32[]{:S(2)}) collective-permute-start(f32[21,24,128]{2,1,0:T(8,128)S(1)} %get-tuple-element.37), channel_id=1, source_target_pairs={{4,0},{8,4},{12,8},{5,1},{9,5},{13,9},{6,2},{10,6},{14,10},{7,3},{... | collective-permute-start | bytes 774152 | tf_op jit(solution)/shard_map/ppermute | solution.py:69
  19.5 3.3 %collective-permute-done.1.refs_1_ = f32[21,24,128]{2,1,0:T(8,128)S(1)} collective-permute-done((f32[21,24,128]{2,1,0:T(8,128)S(1)}, f32[21,24,128]{2,1,0:T(8,128)S(1)}, u32[]{:S(2)}, u32[]{:S(2)}) %collective-permute-start.1) | collective-permute-done | bytes 258080 | tf_op jit(solution)/shard_map/ppermute | solution.py:68
  22.8 4.1 %collective-permute-done.2.refs_2_ = f32[21,24,128]{2,1,0:T(8,128)S(1)} collective-permute-done((f32[21,24,128]{2,1,0:T(8,128)S(1)}, f32[21,24,128]{2,1,0:T(8,128)S(1)}, u32[]{:S(2)}, u32[]{:S(2)}) %collective-permute-start.2) | collective-permute-done | bytes 258080 | tf_op jit(solution)/shard_map/ppermute | solution.py:69
  26.9 7.3 %shard_map.79 = (f32[42,80,128]{2,1,0:T(8,128)}, f32[42,80,128]{2,1,0:T(8,128)}, f32[6,80,128]{2,1,0:T(8,128)}, f32[6,80,128]{2,1,0:T(8,128)S(1)}, f32[11,80,128]{2,1,0:T(8,128)}, /*index=5*/f32[11,80,128]{2,1,0:T(8,128)}) custom-call(s32[1]{0:T(128)} %bitcast.index, f32[3,32,64,128]{3,2,1,0:T(8,128)S(1)} %copy-done, f32[32,64,128]{2,1,0:T(8,128)S(1)} %copy-done.1, ...), custom_call_target="tpu_custom_call" | custom-call | tf_op jit(solution)/shard_map/pallas_call | solution.py:33
  34.2 1.3 %collective-permute-start.3 = (f32[6,80,128]{2,1,0:T(8,128)}, f32[6,80,128]{2,1,0:T(8,128)S(1)}, u32[]{:S(2)}, u32[]{:S(2)}) collective-permute-start(f32[6,80,128]{2,1,0:T(8,128)} %get-tuple-element.40), channel_id=1, source_target_pairs={{0,1},{1,2},{2,3},{4,5},{5,6},{6,7},{8,9},{9,10},{10,11},{12,13},{... | collective-permute-start | bytes 737288 | tf_op jit(solution)/shard_map/ppermute | solution.py:68
  35.5 1.3 %collective-permute-start.4 = (f32[6,80,128]{2,1,0:T(8,128)S(1)}, f32[6,80,128]{2,1,0:T(8,128)S(1)}, u32[]{:S(2)}, u32[]{:S(2)}) collective-permute-start(f32[6,80,128]{2,1,0:T(8,128)S(1)} %get-tuple-element.41), channel_id=1, source_target_pairs={{1,0},{2,1},{3,2},{5,4},{6,5},{7,6},{9,8},{10,9},{11,10},{13,12},{... | collective-permute-start | bytes 737288 | tf_op jit(solution)/shard_map/ppermute | solution.py:69
  36.9 12.1 %shard_map.80 = (f32[34,80,128]{2,1,0:T(8,128)}, f32[34,80,128]{2,1,0:T(8,128)}, f32[34,80,128]{2,1,0:T(8,128)}, f32[34,80,128]{2,1,0:T(8,128)}, f32[34,80,128]{2,1,0:T(8,128)}, /*index=5*/f32[11,8,128]{2,1,0:T(8,128)S(1)}) custom-call(f32[42,80,128]{2,1,0:T(8,128)} %get-tuple-element.42.far_rhs, f32[42,80,128]{2,1,0:T(8,128)} %get-tuple-element.43.far_inv), custom_call_target="tpu_custom_call" | custom-call | flops 43008000 | bytes 12042240 | tf_op jit(solution)/shard_map/pallas_call | solution.py:33
  49.0 9.1 %shard_map.81 = (f32[11,80,128]{2,1,0:T(8,128)}, f32[11,80,128]{2,1,0:T(8,128)}, f32[11,80,128]{2,1,0:T(8,128)}, f32[11,80,128]{2,1,0:T(8,128)}, f32[32,8,128]{2,1,0:T(8,128)}) custom-call(f32[11,80,128]{2,1,0:T(8,128)} %get-tuple-element.38.rhs_far, f32[11,80,128]{2,1,0:T(8,128)} %get-tuple-element.39.inv_far, ...), custom_call_target="tpu_custom_call" | custom-call | tf_op jit(solution)/shard_map/pallas_call | solution.py:33
  58.2 7.8 %all-to-all-start = ((f32[32,8,128]{2,1,0:T(8,128)}), f32[32,8,128]{2,1,0:T(8,128)S(1)}, u32[]{:S(2)}, u32[]{:S(2)}) async-start(f32[32,8,128]{2,1,0:T(8,128)} %get-tuple-element.45), calls=%async_computation | async-start | bytes 262144 | tf_op jit(solution)/shard_map/all_to_all | solution.py:990
  66.0 8.2 %all-to-all-done.dots = f32[32,8,128]{2,1,0:T(8,128)S(1)} async-done(((f32[32,8,128]{2,1,0:T(8,128)}), f32[32,8,128]{2,1,0:T(8,128)S(1)}, u32[]{:S(2)}, u32[]{:S(2)}) %all-to-all-start) | async-done | bytes 131104 | tf_op jit(solution)/shard_map/all_to_all | solution.py:990
  74.2 10.8 %shard_map.82 = (f32[32,64,128]{2,1,0:T(8,128)}, f32[3,32,64,128]{3,2,1,0:T(8,128)}, f32[64,16,128]{2,1,0:T(8,128)S(1)}, f32[64,16,128]{2,1,0:T(8,128)S(1)}, f32[2,64,16,128]{3,2,1,0:T(8,128)S(1)}) custom-call(f32[32,8,128]{2,1,0:T(8,128)S(1)} %all-to-all-done.dots, bf16[128,256]{1,0:T(8,128)(2,1)S(1)} %maximum_maximum_fusion.columns, ...), custom_call_target="tpu_custom_call" | custom-call | tf_op jit(solution)/shard_map/pallas_call | solution.py:33
  85.0 0.3 collective-permute-start.5
  85.3 2.4 %collective-permute-done.5 = f32[2,64,16,128]{3,2,1,0:T(8,128)S(1)} collective-permute-done((f32[2,64,16,128]{3,2,1,0:T(8,128)S(1)}, f32[2,64,16,128]{3,2,1,0:T(8,128)S(1)}, u32[]{:S(2)}, u32[]{:S(2)}) %collective-permute-start.5) | collective-permute-done | bytes 1048608 | tf_op jit(solution)/shard_map/ppermute | solution.py:923
  87.7 0.1 fusion
  87.9 0.6 collective-permute-start.6
  89.0 0.9 shard_map.83
  89.8 12.2 %collective-permute-done.6.came = f32[64,16,128]{2,1,0:T(8,128)S(1)} collective-permute-done((f32[64,16,128]{2,1,0:T(8,128)S(1)}, f32[64,16,128]{2,1,0:T(8,128)S(1)}, u32[]{:S(2)}, u32[]{:S(2)}) %collective-permute-start.6) | collective-permute-done | bytes 524320 | tf_op jit(solution)/shard_map/ppermute | solution.py:923
  102.0 0.6 shard_map.84
  102.7 7.6 %collective-permute-done.7 = f32[2,256,128]{2,1,0:T(8,128)S(1)} collective-permute-done((f32[2,256,128]{2,1,0:T(8,128)S(1)}, f32[2,256,128]{2,1,0:T(8,128)S(1)}, u32[]{:S(2)}, u32[]{:S(2)}) %collective-permute-start.7) | collective-permute-done | bytes 262176 | tf_op jit(solution)/shard_map/ppermute | solution.py:923
  110.4 0.5 collective-permute-start.8
  110.9 7.2 %collective-permute-done.8.came = f32[256,128]{1,0:T(8,128)S(1)} collective-permute-done((f32[256,128]{1,0:T(8,128)S(1)}, f32[256,128]{1,0:T(8,128)S(1)}, u32[]{:S(2)}, u32[]{:S(2)}) %collective-permute-start.8) | collective-permute-done | bytes 131104 | tf_op jit(solution)/shard_map/ppermute | solution.py:923
  118.0 0.7 shard_map.85
  118.7 0.2 collective-permute-start.9
  118.9 4.8 %collective-permute-done.9.came = f32[64,512]{1,0:T(8,128)S(1)} collective-permute-done((f32[64,512]{1,0:T(8,128)S(1)}, f32[64,512]{1,0:T(8,128)S(1)}, u32[]{:S(2)}, u32[]{:S(2)}) %collective-permute-start.9) | collective-permute-done | bytes 131104 | tf_op jit(solution)/shard_map/ppermute | solution.py:923
  123.7 0.3 shard_map.86
  124.1 1.4 %copy.11 = f32[32,4,16,16]{0,3,2,1:T(8,128)} copy(f32[32,4,16,16]{3,2,1,0:T(8,128)S(1)} %shard_map.86) | data formatting | bytes 262144
  (26 shorter events, 0.6 us)
Async XLA Ops:
  0.6 4.6 %copy-start = (f32[3,32,64,128]{3,2,1,0:T(8,128)S(1)}, f32[3,32,64,128]{3,2,1,0:T(8,128)}, u32[]{:S(2)}) copy-start(f32[3,32,64,128]{3,2,1,0:T(8,128)} %refs_9_.1) | copy-start | bytes 9437188
  2.2 11.5 %copy-start.1 = (f32[32,64,128]{2,1,0:T(8,128)S(1)}, f32[32,64,128]{2,1,0:T(8,128)}, u32[]{:S(2)}) copy-start(f32[32,64,128]{2,1,0:T(8,128)} %refs_10_.1) | copy-start | bytes 3145732
  2.2 11.5 %collective-permute-start = (f32[712,128]{1,0:T(8,128)S(1)}, f32[712,128]{1,0:T(8,128)S(1)}, u32[]{:S(2)}, u32[]{:S(2)}) collective-permute-start(f32[712,128]{1,0:T(8,128)S(1)} %shard_map.77), channel_id=1, source_target_pairs={{0,16},{16,0},{1,17},{17,1},{2,18},{18,2},{3,19},{19,3},{4,20},{20... | collective-permute-start | bytes 1093640 | tf_op jit(solution)/shard_map/ppermute | solution.py:923
  14.5 8.3 %collective-permute-start.1 = (f32[21,24,128]{2,1,0:T(8,128)S(1)}, f32[21,24,128]{2,1,0:T(8,128)S(1)}, u32[]{:S(2)}, u32[]{:S(2)}) collective-permute-start(f32[21,24,128]{2,1,0:T(8,128)S(1)} %get-tuple-element.36), channel_id=1, source_target_pairs={{0,4},{4,8},{8,12},{1,5},{5,9},{9,13},{2,6},{6,10},{10,14},{3,7},{... | collective-permute-start | bytes 774152 | tf_op jit(solution)/shard_map/ppermute | solution.py:68
  18.2 18.7 %copy-start.2 = (f32[128,64]{0,1:T(8,128)S(1)}, f32[128,64]{0,1:T(8,128)}, u32[]{:S(2)}) copy-start(f32[128,64]{0,1:T(8,128)} %param.9) | copy-start | bytes 98308
  18.2 8.7 %collective-permute-start.2 = (f32[21,24,128]{2,1,0:T(8,128)S(1)}, f32[21,24,128]{2,1,0:T(8,128)S(1)}, u32[]{:S(2)}, u32[]{:S(2)}) collective-permute-start(f32[21,24,128]{2,1,0:T(8,128)S(1)} %get-tuple-element.37), channel_id=1, source_target_pairs={{4,0},{8,4},{12,8},{5,1},{9,5},{13,9},{6,2},{10,6},{14,10},{7,3},{... | collective-permute-start | bytes 774152 | tf_op jit(solution)/shard_map/ppermute | solution.py:69
  34.2 14.8 %collective-permute-start.3 = (f32[6,80,128]{2,1,0:T(8,128)}, f32[6,80,128]{2,1,0:T(8,128)S(1)}, u32[]{:S(2)}, u32[]{:S(2)}) collective-permute-start(f32[6,80,128]{2,1,0:T(8,128)} %get-tuple-element.40), channel_id=1, source_target_pairs={{0,1},{1,2},{2,3},{4,5},{5,6},{6,7},{8,9},{9,10},{10,11},{12,13},{... | collective-permute-start | bytes 737288 | tf_op jit(solution)/shard_map/ppermute | solution.py:68
  35.5 13.5 %collective-permute-start.4 = (f32[6,80,128]{2,1,0:T(8,128)S(1)}, f32[6,80,128]{2,1,0:T(8,128)S(1)}, u32[]{:S(2)}, u32[]{:S(2)}) collective-permute-start(f32[6,80,128]{2,1,0:T(8,128)S(1)} %get-tuple-element.41), channel_id=1, source_target_pairs={{1,0},{2,1},{3,2},{5,4},{6,5},{7,6},{9,8},{10,9},{11,10},{13,12},{... | collective-permute-start | bytes 737288 | tf_op jit(solution)/shard_map/ppermute | solution.py:69
  58.2 16.0 %all-to-all-start = ((f32[32,8,128]{2,1,0:T(8,128)}), f32[32,8,128]{2,1,0:T(8,128)S(1)}, u32[]{:S(2)}, u32[]{:S(2)}) async-start(f32[32,8,128]{2,1,0:T(8,128)} %get-tuple-element.45), calls=%async_computation | async-start | bytes 262144 | tf_op jit(solution)/shard_map/all_to_all | solution.py:990
  85.0 2.7 %collective-permute-start.5 = (f32[2,64,16,128]{3,2,1,0:T(8,128)S(1)}, f32[2,64,16,128]{3,2,1,0:T(8,128)S(1)}, u32[]{:S(2)}, u32[]{:S(2)}) collective-permute-start(f32[2,64,16,128]{3,2,1,0:T(8,128)S(1)} %get-tuple-element.58), channel_id=1, source_target_pairs={{0,1},{1,0},{2,3},{3,2},{4,5},{5,4},{6,7},{7,6},{8,9},{9,8},{10,11... | collective-permute-start | bytes 3145736 | tf_op jit(solution)/shard_map/ppermute | solution.py:923
  87.7 0.8 copy-start.3
  87.7 0.9 copy-start.4
  87.9 14.1 %collective-permute-start.6 = (f32[64,16,128]{2,1,0:T(8,128)S(1)}, f32[64,16,128]{2,1,0:T(8,128)S(1)}, u32[]{:S(2)}, u32[]{:S(2)}) collective-permute-start(f32[64,16,128]{2,1,0:T(8,128)S(1)} %get-tuple-element.75), channel_id=1, source_target_pairs={{0,2},{1,3},{2,0},{3,1},{4,6},{5,7},{6,4},{7,5},{8,10},{9,11},{10,... | collective-permute-start | bytes 1572872 | tf_op jit(solution)/shard_map/ppermute | solution.py:923
  102.6 7.7 %collective-permute-start.7 = (f32[2,256,128]{2,1,0:T(8,128)S(1)}, f32[2,256,128]{2,1,0:T(8,128)S(1)}, u32[]{:S(2)}, u32[]{:S(2)}) collective-permute-start(f32[2,256,128]{2,1,0:T(8,128)S(1)} %get-tuple-element.63), channel_id=1, source_target_pairs={{0,4},{4,0},{8,12},{12,8},{1,5},{5,1},{9,13},{13,9},{2,6},{6,2},{1... | collective-permute-start | bytes 786440 | tf_op jit(solution)/shard_map/ppermute | solution.py:923
  110.4 7.7 %collective-permute-start.8 = (f32[256,128]{1,0:T(8,128)S(1)}, f32[256,128]{1,0:T(8,128)S(1)}, u32[]{:S(2)}, u32[]{:S(2)}) collective-permute-start(f32[256,128]{1,0:T(8,128)S(1)} %get-tuple-element.77), channel_id=1, source_target_pairs={{0,8},{4,12},{8,0},{12,4},{1,9},{5,13},{9,1},{13,5},{2,10},{6,14},... | collective-permute-start | bytes 393224 | tf_op jit(solution)/shard_map/ppermute | solution.py:923
  118.7 5.0 %collective-permute-start.9 = (f32[64,512]{1,0:T(8,128)S(1)}, f32[64,512]{1,0:T(8,128)S(1)}, u32[]{:S(2)}, u32[]{:S(2)}) collective-permute-start(f32[64,512]{1,0:T(8,128)S(1)} %get-tuple-element.68), channel_id=1, source_target_pairs={{0,16},{16,0},{1,17},{17,1},{2,18},{18,2},{3,19},{19,3},{4,20},{20... | collective-permute-start | bytes 393224 | tf_op jit(solution)/shard_map/ppermute | solution.py:923

commit v4 on v3

--- a/solution.py
+++ b/solution.py
@@ -28,12 +28,14 @@
 BF16 = jnp.bfloat16
 
 
-def call(body, outs, operands, scratch=(), smem=0, limit=12, cost=None, far_in=(), far_out=(), sems=0):
+def call(body, outs, operands, scratch=(), smem=0, limit=12, cost=None, far_in=(), far_out=(), pinned=(), sems=0):
     scratch = [pltpu.VMEM(shape, F32) if isinstance(shape, tuple) else shape for shape in scratch]
     return pl.pallas_call(
         body,
         out_shape=[
-            pltpu.HBM(shape, F32) if n in far_out else jax.ShapeDtypeStruct(shape, F32)
+            pltpu.HBM(shape, F32)
+            if n in far_out or n in pinned
+            else jax.ShapeDtypeStruct(shape, F32)
             for n, shape in enumerate(outs)
         ],
         in_specs=[SMEM if n < smem else HBM if n in far_in else VMEM for n in range(len(operands))],
@@ -44,7 +46,9 @@
         and pl.CostEstimate(flops=cost[0], bytes_accessed=cost[1], transcendentals=0),
     )(
         *(
-            pltpu.with_memory_space_constraint(one, pltpu.HBM) if n in far_in else one
+            pltpu.with_memory_space_constraint(one, pltpu.HBM)
+            if n in far_in
+            else one
             for n, one in enumerate(operands)
         )
     )
@@ -404,9 +408,9 @@
 
 
 class Stencil:
-    def __init__(self, inv, root, ax, ay, az, vs, planes, edges=None):
+    def __init__(self, inv, root, ax, ay, az, vs, planes, edges=None, unroll=4):
         self.inv, self.root, self.ax, self.ay, self.az, self.vs = inv, root, ax, ay, az, vs
-        self.planes, self.edges = planes, edges or (lambda ref: None)
+        self.planes, self.edges, self.unroll = planes, edges or (lambda ref: None), unroll
         self.count, self.rows, self.nz = inv.shape
         self.tiles = self.rows // WIDE
 
@@ -419,7 +423,7 @@
     def left(self, value):
         return pltpu.roll(value, 1, 1)
 
-    def prepare(self, rhs):
+    def prepare(self, rhs, parts=None):
         inv, root = self.inv, self.root
         self.edges(inv)
 
@@ -437,7 +441,8 @@
                 self.vs[0][x, here, :] = two
             return carry
 
-        lax.fori_loop(1, self.count - 1, scales, 0, unroll=4)
+        for start, stop in parts or [(1, self.count - 1)]:
+            lax.fori_loop(start, stop, scales, 0, unroll=self.unroll)
         zero = jnp.zeros((self.rows, self.nz), F32)
         for ref in (root, self.vs[0]):
             ref[0] = zero
@@ -464,7 +469,7 @@
                 self.az[x, here, :] = z_face
             return carry
 
-        lax.fori_loop(1, self.count - 1, couplings, 0, unroll=4)
+        lax.fori_loop(1, self.count - 1, couplings, 0, unroll=self.unroll)
         self.ax[0] = zero
         self.edges(self.ax)
 
@@ -490,7 +495,7 @@
             return carry
 
         start, stop = self.planes(k)
-        lax.fori_loop(start, stop, step, 0, unroll=4)
+        lax.fori_loop(start, stop, step, 0, unroll=self.unroll)
         self.edges(self.vs[k + 1])
 
     def products(self, start, stop, mask):
@@ -510,28 +515,36 @@
         return lax.fori_loop(start, stop, measure, (zero,) * (len(PAIRS) + 1), unroll=2)
 
 
-def basis_main(far_rhs, far_inv, *refs):
+def basis_main(rhs_far, inv_far, *refs):
     outs, sums = refs[: ITERS + 1], refs[ITERS + 1]
     rhs, inv, root, ax, ay, az = refs[ITERS + 2 : ITERS + 8]
     vs, sems = refs[ITERS + 8 : -1], refs[-1]
     wide, rows, nz = ax.shape
     nx = wide - 2 * LAYERS
-    loads = [
-        pltpu.make_async_copy(far, ref, sems.at[n]) for n, (far, ref) in enumerate(((far_rhs, rhs), (far_inv, inv)))
-    ]
-    for load in loads:
-        load.start()
-    for load in loads:
-        load.wait()
+    batch = 4
+    bounds = [n * wide // batch for n in range(batch + 1)]
+    loads = []
+    for n in range(batch):
+        part = pl.ds(bounds[n], bounds[n + 1] - bounds[n])
+        for far, ref in ((inv_far, inv), (rhs_far, rhs)):
+            loads.append(pltpu.make_async_copy(far.at[part], ref.at[part], sems.at[ITERS + 1 + len(loads)]))
+            loads[-1].start()
+
+    def ready():
+        for n in range(batch):
+            for load in loads[2 * n : 2 * n + 2]:
+                load.wait()
+            yield max(bounds[n] - 1, 1), bounds[n + 1] - 1
+
     stencil = Stencil(inv, root, ax, ay, az, vs, lambda k: (2 + k, wide - 2 - k))
     copies = []
 
     def send(n, ref):
-        copy = pltpu.make_async_copy(ref.at[pl.ds(LAYERS - 1, nx + 2)], outs[n], sems.at[2 + n])
+        copy = pltpu.make_async_copy(ref.at[pl.ds(LAYERS - 1, nx + 2)], outs[n], sems.at[n])
         copy.start()
         copies.append(copy)
 
-    stencil.prepare(rhs)
+    stencil.prepare(rhs, ready())
     send(ITERS, root)
     send(0, vs[0])
     for k in range(ITERS - 1):
@@ -548,7 +561,8 @@
 def basis_strips(nx, rhs_far, inv_far, before, after, sums, *refs):
     outs, dots = refs[:ITERS], refs[ITERS]
     rhs, inv, root, ax, ay, az = refs[ITERS + 1 : ITERS + 7]
-    vs, strip_rhs, strip_inv, sems = refs[ITERS + 7 : -3], *refs[-3:]
+    vs, outs_near = refs[ITERS + 7 : 2 * ITERS + 7], refs[2 * ITERS + 7 : 3 * ITERS + 7]
+    strip_rhs, strip_inv, sems = refs[-3:]
     groups, rows, nz = strip_inv.shape
     loads = [
         pltpu.make_async_copy(far, ref, sems.at[ITERS + n])
@@ -591,10 +605,25 @@
 
     lax.fori_loop(0, halves, first, 0, unroll=3)
     lax.fori_loop(0, groups - halves, second, 0, unroll=3)
-    stencil = Stencil(inv, root, ax, ay, az, vs, lambda k: (1, groups + 1), edges)
+    stencil = Stencil(inv, root, ax, ay, az, vs, lambda k: (1, groups + 1), edges, groups)
     stencil.prepare(rhs)
+    copies = []
+
+    def result(k):
+        ref = outs_near[k]
+
+        def plane(g, carry):
+            ref[g] = vs[k][g] * root[g]
+            return carry
+
+        lax.fori_loop(1, groups + 1, plane, 0, unroll=groups)
+        copies.append(pltpu.make_async_copy(ref.at[pl.ds(1, groups)], outs[k], sems.at[k]))
+        copies[-1].start()
+
+    result(0)
     for k in range(ITERS - 1):
         stencil.extend(k)
+        result(k + 1)
     lane = lanes((WIDE, nz))
     part = lane // SPAN
     spot = lane % SPAN
@@ -622,15 +651,6 @@
 
     lax.fori_loop(0, dots.shape[0], send, 0, unroll=8)
 
-    def result(g, carry):
-        for k in range(ITERS):
-            vs[k][g] = vs[k][g] * root[g]
-        return carry
-
-    lax.fori_loop(1, groups + 1, result, 0, unroll=4)
-    copies = [pltpu.make_async_copy(vs[k].at[pl.ds(1, groups)], outs[k], sems.at[k]) for k in range(ITERS)]
-    for copy in copies:
-        copy.start()
     for copy in copies:
         copy.wait()
 
@@ -706,12 +726,33 @@
     inputs = 2 * ITERS + 3
     pressure_far, corrected_far, keep, keep_more, send, p, gaps, mixed, cut, pressure, corrected = refs[inputs : inputs + 11]
     held, sems = refs[inputs + 11 : -1], refs[-1]
-    loads = [pltpu.make_async_copy(far, ref, sems.at[n]) for n, (far, ref) in enumerate(zip(refs, held))]
-    for load in loads:
-        load.start()
     strips, spans, roots = held[:ITERS], held[ITERS : 2 * ITERS], held[2 * ITERS]
     velocity, inv = held[2 * ITERS + 1 :]
     nx, ny, nz = inv.shape
+    batch = 4
+    each = nx // batch
+    used = 0
+
+    def start(far, ref):
+        nonlocal used
+        copy = pltpu.make_async_copy(far, ref, sems.at[used])
+        used += 1
+        copy.start()
+        return copy
+
+    strip_loads = [start(far, ref) for far, ref in zip(refs[:ITERS], strips)]
+    span_loads, other_loads, bounds = [], [], []
+    for n in range(batch):
+        low, high = (n * each + 2 if n else 0), (n + 1) * each + 2
+        bounds.append((low, high))
+        part = pl.ds(low, high - low)
+        pairs = zip(refs[ITERS : 2 * ITERS + 1], held[ITERS : 2 * ITERS + 1])
+        span_loads.append([start(far.at[part], ref.at[part]) for far, ref in pairs])
+        part = pl.ds(n * each, each)
+        other_loads.append(
+            [start(refs[2 * ITERS + 1].at[d, part], velocity.at[d, part]) for d in range(3)]
+            + [start(refs[2 * ITERS + 2].at[part], inv.at[part])]
+        )
     shape = (ny, nz)
     groups = mixed.shape[0]
     total = dots[0]
@@ -726,11 +767,9 @@
         mixed[g] = value
         return carry
 
-    for load in loads[:ITERS]:
+    for load in strip_loads:
         load.wait()
     lax.fori_loop(0, groups, strip, 0, unroll=4)
-    for load in loads[ITERS : 2 * ITERS + 1]:
-        load.wait()
     mine = slice(WIDE, WIDE + ny)
     lane = lanes(spans[0].shape[1:])
 
@@ -751,13 +790,7 @@
         gaps[x] = (after - before)[mine]
         return carry
 
-    lax.fori_loop(0, nx + 2, combine, 0, unroll=4)
     half = columns.shape[0] // 2
-    for load in loads[2 * ITERS + 1 :]:
-        load.wait()
-    batch = 4
-    each = nx // batch
-    stores = []
 
     def pair(n, carry):
         for which in range(2):
@@ -791,20 +824,23 @@
             send[1, block] = out[3 * quarter :]
         return carry
 
+    stores = []
     for n in range(batch):
+        for load in span_loads[n]:
+            load.wait()
+        lax.fori_loop(*bounds[n], combine, 0, unroll=4)
+        for load in other_loads[n]:
+            load.wait()
         lax.fori_loop(n * each // 2, (n + 1) * each // 2, pair, 0, unroll=2)
         part = pl.ds(n * each, each)
-        for ref, far in [(pressure.at[part], pressure_far.at[part])] + [
-            (corrected.at[d, part], corrected_far.at[d, part]) for d in range(3)
-        ]:
-            store = pltpu.make_async_copy(ref, far, sems.at[len(loads) + len(stores)])
-            store.start()
-            stores.append(store)
+        stores.append(start(pressure.at[part], pressure_far.at[part]))
+        for d in range(3):
+            stores.append(start(corrected.at[d, part], corrected_far.at[d, part]))
     for store in stores:
         store.wait()
 
 
-def tables(factor_y, factor_x, y_high, y_low, x_high, x_low, spread_high, spread_low):
+def tables(count_x, factor_y, factor_x, y_high, y_low, x_high, x_low, spread_high, spread_low):
     ny, rank = factor_y.shape
     nx = factor_x.shape[0]
     planes = y_high.shape[0] // ny
@@ -826,11 +862,14 @@
             y_low[n * ny : (n + 1) * ny, h * nz : (h + 1) * nz] = low
     width = x_high.shape[1]
     shape = (rank, width)
-    copy = jnp.where(lanes(shape) // ranks == sublanes(shape), 1.0, 0.0).astype(BF16)
+    own = rank // count_x
+    lane = lanes(shape)
+    copy = lane // (ranks * own) * own + lane % own == sublanes(shape)
+    copy = jnp.where(copy, 1.0, 0.0).astype(BF16)
     for ref, value in zip((spread_high, spread_low), split(factor_x[...])):
         ref[...] = jnp.dot(value, copy, preferred_element_type=F32)
     shape = (ranks, width)
-    here = lanes(shape) % ranks == sublanes(shape)
+    here = lanes(shape) // own % ranks == sublanes(shape)
 
     def row(i, carry):
         at = pl.ds(pl.multiple_of(i * ranks, ranks), ranks)
@@ -857,27 +896,41 @@
     return dot(ah, bh) + (dot(al, bh) + dot(ah, bl))
 
 
-def rank_y(kept, came, wide_high, wide_low, keep, keep_more, send):
-    blocks, ranks, nz = kept.shape
-    group = wide_high.shape[0] // nz
-    parts = []
-    for n in range(blocks // group):
-        parts.append(
-            jnp.concatenate(
-                [kept[n * group + q] + came[n * group + q] for q in range(group)], axis=1
-            )
-        )
-    x = jnp.concatenate(parts, axis=0)
-    out = three(split(x), (wide_high[...], wide_low[...]))
-    quarter = out.shape[1] // 4
-    keep[...] = out[:, 0:quarter]
-    keep_more[...] = out[:, quarter : 2 * quarter]
-    send[0] = out[:, 2 * quarter : 3 * quarter]
-    send[1] = out[:, 3 * quarter :]
-
-
-def rank_x(ranks, kept, came, wide_high, wide_low, *outs):
-    u = kept[...] + came[...]
+def rank_y(x, table):
+    blocks, ranks, nz = x.shape
+    group = table[0].shape[0] // nz
+    parts = [
+        jnp.concatenate([x[n * group + q] for q in range(group)], axis=1) for n in range(blocks // group)
+    ]
+    out = three(split(jnp.concatenate(parts, axis=0)), table)
+    return [out[:, n * nz : (n + 1) * nz] for n in range(out.shape[1] // nz)]
+
+
+def tail_one(kept, more, came, high, low, p_send, p_keep, q_send, q_keep, q_more):
+    half = kept.shape[0] // 2
+    p_send[...] = more[0:half] + came[1, 0:half]
+    p_keep[...] = kept[0:half] + came[0, 0:half]
+    x = jnp.concatenate([kept[half:] + came[0, half:], more[half:] + came[1, half:]], axis=0)
+    q_keep[...], q_more[...], q_send[0], q_send[1] = rank_y(x, (high[...], low[...]))
+
+
+def tail_two(p_kept, p_came, q_kept, q_more, q_came, high, low, p_send, p_keep, p_more, q_send, q_keep):
+    q_send[...] = q_more[...] + q_came[1]
+    q_keep[...] = q_kept[...] + q_came[0]
+    parts = rank_y(p_kept[...] + p_came[...], (high[...], low[...]))
+    p_keep[...], p_more[...], p_send[0], p_send[1] = parts
+
+
+def tail_three(p_kept, p_more, p_came, q_kept, q_came, p_send, p_keep, q_send, q_keep):
+    half = q_keep.shape[0]
+    p_send[...] = p_more[...] + p_came[1]
+    p_keep[...] = p_kept[...] + p_came[0]
+    q_send[...] = q_kept[half:] + q_came[half:]
+    q_keep[...] = q_kept[0:half] + q_came[0:half]
+
+
+def rank_x(ranks, p_kept, p_came, q_kept, q_came, wide_high, wide_low, *outs):
+    u = jnp.concatenate([p_kept[...] + p_came[...], q_kept[...] + q_came[...]], axis=0)
     rows, nz = u.shape
     group = wide_high.shape[0] // nz
     parts = []
@@ -895,10 +948,11 @@
 
 
 def last_core(kept, came, core):
-    ranks_x, fields, ranks_y, ranks_z = core.shape
-    z = jnp.transpose(kept[...] + came[...])
+    fields, ranks_y, ranks_z, ranks_x = core.shape
+    z = kept[...] + came[...]
     for f in range(fields):
-        core[:, f] = z[:, f * ranks_z : (f + 1) * ranks_z].reshape(ranks_x, ranks_y, ranks_z)
+        for b in range(ranks_y):
+            core[f, b] = z[f * ranks_z : (f + 1) * ranks_z, b * ranks_x : (b + 1) * ranks_x]
 
 
 def relative(factor, axis):
@@ -975,14 +1029,14 @@
         cost=(wide * rows * nz * 100, 7 * cost_of(whole)),
         far_in=(0, 1),
         far_out=range(ITERS + 1),
-        sems=ITERS + 3,
+        sems=ITERS + 9,
     )
     padded = (groups + 2, rows, nz)
     *strips, dots = call(
         functools.partial(basis_strips, nx),
         [strip] * ITERS + [(devices, WIDE, nz)],
         [strip_rhs, strip_inv, before, after, sums],
-        scratch=[padded] * (6 + ITERS) + [strip] * 2,
+        scratch=[padded] * (6 + 2 * ITERS) + [strip] * 2,
         far_in=(0, 1),
         far_out=range(ITERS),
         sems=ITERS + 2,
@@ -993,7 +1047,7 @@
     planes = nz // ranks_y
     table_y, table_x = (planes * ny, count_y * nz), (nx * ranks_y, rank * ranks_y)
     y_high, y_low, x_high, x_low = pl.pallas_call(
-        tables,
+        functools.partial(tables, count_x),
         out_shape=[jax.ShapeDtypeStruct(one, BF16) for one in (table_y, table_y, table_x, table_x)],
         in_specs=[VMEM] * 2,
         out_specs=[VMEM] * 4,
@@ -1020,26 +1074,35 @@
         limit=32,
         far_in=range(2, 2 + len(far)),
         far_out=(0, 1),
-        sems=len(far) + 16,
+        sems=ITERS + 4 * (ITERS + 5) + 16,
     )
 
     came = swap(send, "gz", 1)
-    send = keep_more + came[1]
-    keep = keep + came[0]
-    came = swap(send, "gz", 2)
-
-    shape = (4 * nx // planes * ranks_z, nz)
-    keep, keep_more, send = call(
-        rank_y, [shape] * 2 + [(2,) + shape], [keep, came, y_high, y_low], limit=16
-    )
-    came = swap(send, "gy", 1)
-    send = keep_more + came[1]
-    keep = keep + came[0]
-    came = swap(send, "gy", 2)
-
+    table = [y_high, y_low]
+    part = (piece[0] // 2, ranks_z, nz)
+    half = (2 * nx // planes * ranks_z, nz)
+    full = (2 * half[0], nz)
+    p_send, p_keep, q_send, q_keep, q_more = call(
+        tail_one, [part, part, (2,) + full, full, full], [keep, keep_more, came, *table], limit=16
+    )
+    p_came, q_came = swap(p_send, "gz", 2), swap(q_send, "gy", 1)
+    p_send, p_keep, p_more, q_send, q_keep = call(
+        tail_two,
+        [(2,) + half, half, half, full, full],
+        [p_keep, p_came, q_keep, q_more, q_came, *table],
+        limit=16,
+    )
+    p_came, q_came = swap(p_send, "gy", 1), swap(q_send, "gy", 2)
+    p_send, p_keep, q_send, q_keep = call(
+        tail_three, [half] * 4, [p_keep, p_more, p_came, q_keep, q_came]
+    )
+    p_came, q_came = swap(p_send, "gy", 2), swap(q_send, "gz", 2)
     half = (4 * ranks_z, rank * ranks_y // 2)
     keep, send = call(
-        functools.partial(rank_x, ranks_z), [half] * 2, [keep, came, x_high, x_low], limit=16
+        functools.partial(rank_x, ranks_z),
+        [half] * 2,
+        [p_keep, p_came, q_keep, q_came, x_high, x_low],
+        limit=16,
     )
     mask = 1
     while True:
@@ -1050,8 +1113,8 @@
         total = keep + came
         width = total.shape[1] // 2
         keep, send = total[:, :width], total[:, width:]
-    core, = call(last_core, [(rank // count_x, 4, ranks_y, ranks_z)], [keep, came], limit=16)
-    return pressure, corrected, core
+    core, = call(last_core, [(4, ranks_y, ranks_z, rank // count_x)], [keep, came], limit=16, pinned=(0,))
+    return pressure, corrected, jnp.transpose(core, (3, 0, 1, 2))
 
 
 def solution(mesh):

time: 126 us -> 114 us (0.905)
  waiting for transfers between devices: 57.2 us -> 46.3 us
  starting transfers between devices: 20.2 us -> 24.6 us
  Pallas kernels: 45.2 us -> 41 us
  local copies, waits for them, and re-layouts: 1.79 us -> 0.4 us
    ppermute x6 -> x9, waiting for transfers between devices: 41.6 us -> 30.7 us  [swap(): return lax.ppermute(value, axis, [(i, i ^ mask) for i in range(count)])]
    ppermute x6 -> x9, starting transfers between devices: 4.73 us -> 9.22 us  [swap(): return lax.ppermute(value, axis, [(i, i ^ mask) for i in range(count)])]
    pallas_call x11 -> x13, Pallas kernels: 45.2 us -> 41 us  [the longest x12 40.2 us: call(): pl.pallas_call(body, out_shape=[pltpu.HBM(shape, F32) if n in far_out or...]
    unnamed x12 -> x11, local copies, waits for them, and re-layouts: 1.49 us -> 0.1 us
  transfers between devices with their start and end apart: 11 -> 14, of which waited for: 9 -> 11; matrix products, arithmetic and copies ran while one was open for 0% -> 0% of each run, Pallas kernels for 11% -> 12%
where the time goes in v4:
time: 114 us; the launch traced here: 113 us
  waiting for transfers between devices  46.3 us (41%)
  Pallas kernels  41 us (36%)
  starting transfers between devices  24.6 us (22%)
    pallas_call x12, Pallas kernels, call(): pl.pallas_call(body, out_shape=[pltpu.HBM(shape, F32) if n in far_out or...  40.2 us
    ppermute x9, waiting for transfers between devices, swap(): return lax.ppermute(value, axis, [(i, i ^ mask) for i in range(count)])  30.7 us
    ppermute x9, starting transfers between devices, swap(): return lax.ppermute(value, axis, [(i, i ^ mask) for i in range(count)])  9.22 us
    all_to_all x1, waiting for transfers between devices, per_device(): dots = lax.all_to_all(dots, AXES, 0, 0, tiled=True)  8.2 us
    all_to_all x1, starting transfers between devices, per_device(): dots = lax.all_to_all(dots, AXES, 0, 0, tiled=True)  7.8 us
    ppermute x2, starting transfers between devices, exchange(): below = lax.ppermute(up, axis, [(i, i + 1) for i in range(ends)])  5.05 us
    ppermute x2, waiting for transfers between devices, exchange(): above = lax.ppermute(down, axis, [(i + 1, i) for i in range(ends)])  4.14 us
    ppermute x2, waiting for transfers between devices, exchange(): below = lax.ppermute(up, axis, [(i, i + 1) for i in range(ends)])  3.26 us
  transfers between devices with their start and end apart: 14, of which 11 were waited for; matrix products, arithmetic and copies ran while one was open for 0% of the time, Pallas kernels for 12%

profile of v4, /device:TPU:0, one launch (start us, length us, event | category | flops | bytes accessed | tf_op | source)
XLA Modules:
  0.0 113.3 jit_solution(16977561163592319025)
XLA Ops:
  0.6 1.6 %shard_map.77 = f32[712,128]{1,0:T(8,128)S(1)} custom-call(s32[1]{0:T(128)} %bitcast.index, f32[3,32,64,128]{3,2,1,0:T(8,128)} %refs_9_.1, f32[32,64,128]{2,1,0:T(8,128)} %refs_10_.1), custom_call_target="tpu_custom_call" | custom-call | tf_op jit(solution)/shard_map/pallas_call | solution.py:33
  2.2 3.0 %collective-permute-start = (f32[712,128]{1,0:T(8,128)S(1)}, f32[712,128]{1,0:T(8,128)S(1)}, u32[]{:S(2)}, u32[]{:S(2)}) collective-permute-start(f32[712,128]{1,0:T(8,128)S(1)} %shard_map.77), channel_id=1, source_target_pairs={{0,16},{16,0},{1,17},{17,1},{2,18},{18,2},{3,19},{19,3},{4,20},{20... | collective-permute-start | bytes 1093640 | tf_op jit(solution)/shard_map/ppermute | solution.py:977
  5.2 1.1 shard_map.76.rhs
  6.3 7.4 %collective-permute-done.refs_0_ = f32[712,128]{1,0:T(8,128)S(1)} collective-permute-done((f32[712,128]{1,0:T(8,128)S(1)}, f32[712,128]{1,0:T(8,128)S(1)}, u32[]{:S(2)}, u32[]{:S(2)}) %collective-permute-start) | collective-permute-done | bytes 364576 | tf_op jit(solution)/shard_map/ppermute | solution.py:977
  13.7 0.7 shard_map.78
  14.5 3.7 %collective-permute-start.1 = (f32[21,24,128]{2,1,0:T(8,128)S(1)}, f32[21,24,128]{2,1,0:T(8,128)S(1)}, u32[]{:S(2)}, u32[]{:S(2)}) collective-permute-start(f32[21,24,128]{2,1,0:T(8,128)S(1)} %get-tuple-element.47), channel_id=1, source_target_pairs={{0,4},{4,8},{8,12},{1,5},{5,9},{9,13},{2,6},{6,10},{10,14},{3,7},{... | collective-permute-start | bytes 774152 | tf_op jit(solution)/shard_map/ppermute | solution.py:72
  18.2 1.3 %collective-permute-start.2 = (f32[21,24,128]{2,1,0:T(8,128)S(1)}, f32[21,24,128]{2,1,0:T(8,128)S(1)}, u32[]{:S(2)}, u32[]{:S(2)}) collective-permute-start(f32[21,24,128]{2,1,0:T(8,128)S(1)} %get-tuple-element.48), channel_id=1, source_target_pairs={{4,0},{8,4},{12,8},{5,1},{9,5},{13,9},{6,2},{10,6},{14,10},{7,3},{... | collective-permute-start | bytes 774152 | tf_op jit(solution)/shard_map/ppermute | solution.py:73
  19.5 3.3 %collective-permute-done.1.refs_1_ = f32[21,24,128]{2,1,0:T(8,128)S(1)} collective-permute-done((f32[21,24,128]{2,1,0:T(8,128)S(1)}, f32[21,24,128]{2,1,0:T(8,128)S(1)}, u32[]{:S(2)}, u32[]{:S(2)}) %collective-permute-start.1) | collective-permute-done | bytes 258080 | tf_op jit(solution)/shard_map/ppermute | solution.py:72
  22.8 4.1 %collective-permute-done.2.refs_2_ = f32[21,24,128]{2,1,0:T(8,128)S(1)} collective-permute-done((f32[21,24,128]{2,1,0:T(8,128)S(1)}, f32[21,24,128]{2,1,0:T(8,128)S(1)}, u32[]{:S(2)}, u32[]{:S(2)}) %collective-permute-start.2) | collective-permute-done | bytes 258080 | tf_op jit(solution)/shard_map/ppermute | solution.py:73
  26.9 7.3 %shard_map.79 = (f32[42,80,128]{2,1,0:T(8,128)}, f32[42,80,128]{2,1,0:T(8,128)}, f32[6,80,128]{2,1,0:T(8,128)}, f32[6,80,128]{2,1,0:T(8,128)S(1)}, f32[11,80,128]{2,1,0:T(8,128)}, /*index=5*/f32[11,80,128]{2,1,0:T(8,128)}) custom-call(s32[1]{0:T(128)} %bitcast.index, f32[3,32,64,128]{3,2,1,0:T(8,128)S(1)} %copy-done, f32[32,64,128]{2,1,0:T(8,128)S(1)} %copy-done.1, ...), custom_call_target="tpu_custom_call" | custom-call | tf_op jit(solution)/shard_map/pallas_call | solution.py:33
  34.2 1.3 %collective-permute-start.3 = (f32[6,80,128]{2,1,0:T(8,128)}, f32[6,80,128]{2,1,0:T(8,128)S(1)}, u32[]{:S(2)}, u32[]{:S(2)}) collective-permute-start(f32[6,80,128]{2,1,0:T(8,128)} %get-tuple-element.51), channel_id=1, source_target_pairs={{0,1},{1,2},{2,3},{4,5},{5,6},{6,7},{8,9},{9,10},{10,11},{12,13},{... | collective-permute-start | bytes 737288 | tf_op jit(solution)/shard_map/ppermute | solution.py:72
  35.6 1.3 %collective-permute-start.4 = (f32[6,80,128]{2,1,0:T(8,128)S(1)}, f32[6,80,128]{2,1,0:T(8,128)S(1)}, u32[]{:S(2)}, u32[]{:S(2)}) collective-permute-start(f32[6,80,128]{2,1,0:T(8,128)S(1)} %get-tuple-element.52), channel_id=1, source_target_pairs={{1,0},{2,1},{3,2},{5,4},{6,5},{7,6},{9,8},{10,9},{11,10},{13,12},{... | collective-permute-start | bytes 737288 | tf_op jit(solution)/shard_map/ppermute | solution.py:73
  36.9 11.8 %shard_map.80 = (f32[34,80,128]{2,1,0:T(8,128)}, f32[34,80,128]{2,1,0:T(8,128)}, f32[34,80,128]{2,1,0:T(8,128)}, f32[34,80,128]{2,1,0:T(8,128)}, f32[34,80,128]{2,1,0:T(8,128)}, /*index=5*/f32[11,8,128]{2,1,0:T(8,128)S(1)}) custom-call(f32[42,80,128]{2,1,0:T(8,128)} %get-tuple-element.53.rhs_far, f32[42,80,128]{2,1,0:T(8,128)} %get-tuple-element.54.inv_far), custom_call_target="tpu_custom_call" | custom-call | flops 43008000 | bytes 12042240 | tf_op jit(solution)/shard_map/pallas_call | solution.py:33
  48.8 5.5 %shard_map.81 = (f32[11,80,128]{2,1,0:T(8,128)}, f32[11,80,128]{2,1,0:T(8,128)}, f32[11,80,128]{2,1,0:T(8,128)}, f32[11,80,128]{2,1,0:T(8,128)}, f32[32,8,128]{2,1,0:T(8,128)}) custom-call(f32[11,80,128]{2,1,0:T(8,128)} %get-tuple-element.49.rhs_far, f32[11,80,128]{2,1,0:T(8,128)} %get-tuple-element.50.inv_far, ...), custom_call_target="tpu_custom_call" | custom-call | tf_op jit(solution)/shard_map/pallas_call | solution.py:33
  54.2 7.8 %all-to-all-start = ((f32[32,8,128]{2,1,0:T(8,128)}), f32[32,8,128]{2,1,0:T(8,128)S(1)}, u32[]{:S(2)}, u32[]{:S(2)}) async-start(f32[32,8,128]{2,1,0:T(8,128)} %get-tuple-element.56), calls=%async_computation | async-start | bytes 262144 | tf_op jit(solution)/shard_map/all_to_all | solution.py:1044
  62.1 8.2 %all-to-all-done.dots = f32[32,8,128]{2,1,0:T(8,128)S(1)} async-done(((f32[32,8,128]{2,1,0:T(8,128)}), f32[32,8,128]{2,1,0:T(8,128)S(1)}, u32[]{:S(2)}, u32[]{:S(2)}) %all-to-all-start) | async-done | bytes 131104 | tf_op jit(solution)/shard_map/all_to_all | solution.py:1044
  70.3 9.6 %shard_map.82 = (f32[32,64,128]{2,1,0:T(8,128)}, f32[3,32,64,128]{3,2,1,0:T(8,128)}, f32[64,16,128]{2,1,0:T(8,128)S(1)}, f32[64,16,128]{2,1,0:T(8,128)S(1)}, f32[2,64,16,128]{3,2,1,0:T(8,128)S(1)}) custom-call(f32[32,8,128]{2,1,0:T(8,128)S(1)} %all-to-all-done.dots, bf16[128,256]{1,0:T(8,128)(2,1)S(1)} %maximum_maximum_fusion.columns, ...), custom_call_target="tpu_custom_call" | custom-call | tf_op jit(solution)/shard_map/pallas_call | solution.py:33
  80.7 0.8 shard_map.83
  81.5 1.1 %collective-permute-done.5.came = f32[2,64,16,128]{3,2,1,0:T(8,128)S(1)} collective-permute-done((f32[2,64,16,128]{3,2,1,0:T(8,128)S(1)}, f32[2,64,16,128]{3,2,1,0:T(8,128)S(1)}, u32[]{:S(2)}, u32[]{:S(2)}) %collective-permute-start.5) | collective-permute-done | bytes 1048608 | tf_op jit(solution)/shard_map/ppermute | solution.py:977
  82.6 0.6 shard_map.84
  83.8 1.0 collective-permute-start.7
  84.8 7.0 %collective-permute-done.6.p_came = f32[32,16,128]{2,1,0:T(8,128)S(1)} collective-permute-done((f32[32,16,128]{2,1,0:T(8,128)S(1)}, f32[32,16,128]{2,1,0:T(8,128)S(1)}, u32[]{:S(2)}, u32[]{:S(2)}) %collective-permute-start.6) | collective-permute-done | bytes 262176 | tf_op jit(solution)/shard_map/ppermute | solution.py:977
  92.3 1.0 collective-permute-start.8
  93.3 1.2 %collective-permute-start.9 = (f32[256,128]{1,0:T(8,128)S(1)}, f32[256,128]{1,0:T(8,128)S(1)}, u32[]{:S(2)}, u32[]{:S(2)}) collective-permute-start(f32[256,128]{1,0:T(8,128)S(1)} %get-tuple-element.82), channel_id=1, source_target_pairs={{0,8},{4,12},{8,0},{12,4},{1,9},{5,13},{9,1},{13,5},{2,10},{6,14},... | collective-permute-start | bytes 393224 | tf_op jit(solution)/shard_map/ppermute | solution.py:977
  94.5 4.3 %collective-permute-done.8.p_came = f32[2,128,128]{2,1,0:T(8,128)S(1)} collective-permute-done((f32[2,128,128]{2,1,0:T(8,128)S(1)}, f32[2,128,128]{2,1,0:T(8,128)S(1)}, u32[]{:S(2)}, u32[]{:S(2)}) %collective-permute-start.8) | collective-permute-done | bytes 131104 | tf_op jit(solution)/shard_map/ppermute | solution.py:977
  98.7 2.6 %collective-permute-done.9.q_came = f32[256,128]{1,0:T(8,128)S(1)} collective-permute-done((f32[256,128]{1,0:T(8,128)S(1)}, f32[256,128]{1,0:T(8,128)S(1)}, u32[]{:S(2)}, u32[]{:S(2)}) %collective-permute-start.9) | collective-permute-done | bytes 131104 | tf_op jit(solution)/shard_map/ppermute | solution.py:977
  101.6 1.2 %collective-permute-start.11 = (f32[128,128]{1,0:T(8,128)S(1)}, f32[128,128]{1,0:T(8,128)S(1)}, u32[]{:S(2)}, u32[]{:S(2)}) collective-permute-start(f32[128,128]{1,0:T(8,128)S(1)} %get-tuple-element.86), channel_id=1, source_target_pairs={{0,2},{1,3},{2,0},{3,1},{4,6},{5,7},{6,4},{7,5},{8,10},{9,11},{10,... | collective-permute-start | bytes 196616 | tf_op jit(solution)/shard_map/ppermute | solution.py:977
  102.8 3.9 %collective-permute-done.10.p_came = f32[128,128]{1,0:T(8,128)S(1)} collective-permute-done((f32[128,128]{1,0:T(8,128)S(1)}, f32[128,128]{1,0:T(8,128)S(1)}, u32[]{:S(2)}, u32[]{:S(2)}) %collective-permute-start.10) | collective-permute-done | bytes 65568 | tf_op jit(solution)/shard_map/ppermute | solution.py:977
  106.6 0.7 shard_map.87
  107.3 0.8 collective-permute-start.12
  108.1 4.2 %collective-permute-done.12.came = f32[64,512]{1,0:T(8,128)S(1)} collective-permute-done((f32[64,512]{1,0:T(8,128)S(1)}, f32[64,512]{1,0:T(8,128)S(1)}, u32[]{:S(2)}, u32[]{:S(2)}) %collective-permute-start.12) | collective-permute-done | bytes 131104 | tf_op jit(solution)/shard_map/ppermute | solution.py:977
  112.3 1.0 shard_map.88
  (31 shorter events, 2.1 us)
Async XLA Ops:
  0.6 4.6 %copy-start = (f32[3,32,64,128]{3,2,1,0:T(8,128)S(1)}, f32[3,32,64,128]{3,2,1,0:T(8,128)}, u32[]{:S(2)}) copy-start(f32[3,32,64,128]{3,2,1,0:T(8,128)} %refs_9_.1) | copy-start | bytes 9437188
  2.2 11.5 %copy-start.1 = (f32[32,64,128]{2,1,0:T(8,128)S(1)}, f32[32,64,128]{2,1,0:T(8,128)}, u32[]{:S(2)}) copy-start(f32[32,64,128]{2,1,0:T(8,128)} %refs_10_.1) | copy-start | bytes 3145732
  2.2 11.5 %collective-permute-start = (f32[712,128]{1,0:T(8,128)S(1)}, f32[712,128]{1,0:T(8,128)S(1)}, u32[]{:S(2)}, u32[]{:S(2)}) collective-permute-start(f32[712,128]{1,0:T(8,128)S(1)} %shard_map.77), channel_id=1, source_target_pairs={{0,16},{16,0},{1,17},{17,1},{2,18},{18,2},{3,19},{19,3},{4,20},{20... | collective-permute-start | bytes 1093640 | tf_op jit(solution)/shard_map/ppermute | solution.py:977
  14.5 8.3 %collective-permute-start.1 = (f32[21,24,128]{2,1,0:T(8,128)S(1)}, f32[21,24,128]{2,1,0:T(8,128)S(1)}, u32[]{:S(2)}, u32[]{:S(2)}) collective-permute-start(f32[21,24,128]{2,1,0:T(8,128)S(1)} %get-tuple-element.47), channel_id=1, source_target_pairs={{0,4},{4,8},{8,12},{1,5},{5,9},{9,13},{2,6},{6,10},{10,14},{3,7},{... | collective-permute-start | bytes 774152 | tf_op jit(solution)/shard_map/ppermute | solution.py:72
  18.2 18.7 %copy-start.2 = (f32[128,64]{0,1:T(8,128)S(1)}, f32[128,64]{0,1:T(8,128)}, u32[]{:S(2)}) copy-start(f32[128,64]{0,1:T(8,128)} %param.9) | copy-start | bytes 98308
  18.2 8.7 %collective-permute-start.2 = (f32[21,24,128]{2,1,0:T(8,128)S(1)}, f32[21,24,128]{2,1,0:T(8,128)S(1)}, u32[]{:S(2)}, u32[]{:S(2)}) collective-permute-start(f32[21,24,128]{2,1,0:T(8,128)S(1)} %get-tuple-element.48), channel_id=1, source_target_pairs={{4,0},{8,4},{12,8},{5,1},{9,5},{13,9},{6,2},{10,6},{14,10},{7,3},{... | collective-permute-start | bytes 774152 | tf_op jit(solution)/shard_map/ppermute | solution.py:73
  34.2 14.5 %collective-permute-start.3 = (f32[6,80,128]{2,1,0:T(8,128)}, f32[6,80,128]{2,1,0:T(8,128)S(1)}, u32[]{:S(2)}, u32[]{:S(2)}) collective-permute-start(f32[6,80,128]{2,1,0:T(8,128)} %get-tuple-element.51), channel_id=1, source_target_pairs={{0,1},{1,2},{2,3},{4,5},{5,6},{6,7},{8,9},{9,10},{10,11},{12,13},{... | collective-permute-start | bytes 737288 | tf_op jit(solution)/shard_map/ppermute | solution.py:72
  35.6 13.2 %collective-permute-start.4 = (f32[6,80,128]{2,1,0:T(8,128)S(1)}, f32[6,80,128]{2,1,0:T(8,128)S(1)}, u32[]{:S(2)}, u32[]{:S(2)}) collective-permute-start(f32[6,80,128]{2,1,0:T(8,128)S(1)} %get-tuple-element.52), channel_id=1, source_target_pairs={{1,0},{2,1},{3,2},{5,4},{6,5},{7,6},{9,8},{10,9},{11,10},{13,12},{... | collective-permute-start | bytes 737288 | tf_op jit(solution)/shard_map/ppermute | solution.py:73
  54.2 16.0 %all-to-all-start = ((f32[32,8,128]{2,1,0:T(8,128)}), f32[32,8,128]{2,1,0:T(8,128)S(1)}, u32[]{:S(2)}, u32[]{:S(2)}) async-start(f32[32,8,128]{2,1,0:T(8,128)} %get-tuple-element.56), calls=%async_computation | async-start | bytes 262144 | tf_op jit(solution)/shard_map/all_to_all | solution.py:1044
  70.3 9.9 %copy-start.3 = (f32[64,64]{1,0:T(8,128)S(1)}, f32[64,64]{1,0:T(8,128)}, u32[]{:S(2)}) copy-start(f32[64,64]{1,0:T(8,128)} %param.8) | copy-start | bytes 49156
  70.3 10.1 %copy-start.4 = (f32[32,64]{1,0:T(8,128)S(1)}, f32[32,64]{1,0:T(8,128)}, u32[]{:S(2)}) copy-start(f32[32,64]{1,0:T(8,128)} %param.7) | copy-start | bytes 24580
  79.9 2.7 %collective-permute-start.5 = (f32[2,64,16,128]{3,2,1,0:T(8,128)S(1)}, f32[2,64,16,128]{3,2,1,0:T(8,128)S(1)}, u32[]{:S(2)}, u32[]{:S(2)}) collective-permute-start(f32[2,64,16,128]{3,2,1,0:T(8,128)S(1)} %get-tuple-element.70), channel_id=1, source_target_pairs={{0,1},{1,0},{2,3},{3,2},{4,5},{5,4},{6,7},{7,6},{8,9},{9,8},{10,11... | collective-permute-start | bytes 3145736 | tf_op jit(solution)/shard_map/ppermute | solution.py:977
  83.2 8.5 %collective-permute-start.6 = (f32[32,16,128]{2,1,0:T(8,128)S(1)}, f32[32,16,128]{2,1,0:T(8,128)S(1)}, u32[]{:S(2)}, u32[]{:S(2)}) collective-permute-start(f32[32,16,128]{2,1,0:T(8,128)S(1)} %get-tuple-element.74), channel_id=1, source_target_pairs={{0,2},{1,3},{2,0},{3,1},{4,6},{5,7},{6,4},{7,5},{8,10},{9,11},{10,... | collective-permute-start | bytes 786440 | tf_op jit(solution)/shard_map/ppermute | solution.py:977
  83.8 8.1 %collective-permute-start.7 = (f32[2,256,128]{2,1,0:T(8,128)S(1)}, f32[2,256,128]{2,1,0:T(8,128)S(1)}, u32[]{:S(2)}, u32[]{:S(2)}) collective-permute-start(f32[2,256,128]{2,1,0:T(8,128)S(1)} %get-tuple-element.77), channel_id=1, source_target_pairs={{0,4},{4,0},{8,12},{12,8},{1,5},{5,1},{9,13},{13,9},{2,6},{6,2},{1... | collective-permute-start | bytes 786440 | tf_op jit(solution)/shard_map/ppermute | solution.py:977
  92.3 6.5 %collective-permute-start.8 = (f32[2,128,128]{2,1,0:T(8,128)S(1)}, f32[2,128,128]{2,1,0:T(8,128)S(1)}, u32[]{:S(2)}, u32[]{:S(2)}) collective-permute-start(f32[2,128,128]{2,1,0:T(8,128)S(1)} %get-tuple-element.80), channel_id=1, source_target_pairs={{0,4},{4,0},{8,12},{12,8},{1,5},{5,1},{9,13},{13,9},{2,6},{6,2},{1... | collective-permute-start | bytes 393224 | tf_op jit(solution)/shard_map/ppermute | solution.py:977
  93.3 8.1 %collective-permute-start.9 = (f32[256,128]{1,0:T(8,128)S(1)}, f32[256,128]{1,0:T(8,128)S(1)}, u32[]{:S(2)}, u32[]{:S(2)}) collective-permute-start(f32[256,128]{1,0:T(8,128)S(1)} %get-tuple-element.82), channel_id=1, source_target_pairs={{0,8},{4,12},{8,0},{12,4},{1,9},{5,13},{9,1},{13,5},{2,10},{6,14},... | collective-permute-start | bytes 393224 | tf_op jit(solution)/shard_map/ppermute | solution.py:977
  101.4 5.2 %collective-permute-start.10 = (f32[128,128]{1,0:T(8,128)S(1)}, f32[128,128]{1,0:T(8,128)S(1)}, u32[]{:S(2)}, u32[]{:S(2)}) collective-permute-start(f32[128,128]{1,0:T(8,128)S(1)} %get-tuple-element.84), channel_id=1, source_target_pairs={{0,8},{4,12},{8,0},{12,4},{1,9},{5,13},{9,1},{13,5},{2,10},{6,14},... | collective-permute-start | bytes 196616 | tf_op jit(solution)/shard_map/ppermute | solution.py:977
  101.6 5.0 %collective-permute-start.11 = (f32[128,128]{1,0:T(8,128)S(1)}, f32[128,128]{1,0:T(8,128)S(1)}, u32[]{:S(2)}, u32[]{:S(2)}) collective-permute-start(f32[128,128]{1,0:T(8,128)S(1)} %get-tuple-element.86), channel_id=1, source_target_pairs={{0,2},{1,3},{2,0},{3,1},{4,6},{5,7},{6,4},{7,5},{8,10},{9,11},{10,... | collective-permute-start | bytes 196616 | tf_op jit(solution)/shard_map/ppermute | solution.py:977
  107.3 5.0 %collective-permute-start.12 = (f32[64,512]{1,0:T(8,128)S(1)}, f32[64,512]{1,0:T(8,128)S(1)}, u32[]{:S(2)}, u32[]{:S(2)}) collective-permute-start(f32[64,512]{1,0:T(8,128)S(1)} %get-tuple-element.90), channel_id=1, source_target_pairs={{0,16},{16,0},{1,17},{17,1},{2,18},{18,2},{3,19},{19,3},{4,20},{20... | collective-permute-start | bytes 393224 | tf_op jit(solution)/shard_map/ppermute | solution.py:977

commit v5 on v4

--- a/solution.py
+++ b/solution.py
@@ -89,14 +89,13 @@
     return -0.5 * total
 
 
-def sources(velocity, rhs):
-    nx = rhs.shape[0]
-
-    def plane(x, carry):
-        rhs[x] = source(velocity, x, nx)
-        return carry
-
-    lax.fori_loop(0, nx, plane, 0, unroll=4)
+def ring(one, two, axis, closed=True):
+    count = lax.axis_size(axis)
+    near = [(i, i ^ 1) for i in range(count)]
+    far = [(i, (i + 1 if i % 2 else i - 1) % count) for i in range(count)]
+    if not closed:
+        far = [(i, j) for i, j in far if abs(i - j) == 1]
+    return lax.ppermute(one, axis, near), lax.ppermute(two, axis, far)
 
 
 def pack_x(index, velocity_far, inv_far, *refs):
@@ -160,6 +159,20 @@
         return self.ref[where] * self.factor
 
 
+class Picked:
+    def __init__(self, first, one, two, there):
+        self.first, self.one, self.two, self.factor = first, one, two, jnp.where(there, 1.0, 0.0)
+
+    def __getitem__(self, where):
+        return jnp.where(self.first, self.one[where], self.two[where]) * self.factor
+
+
+def sides(index, axis, messages):
+    here, count = index[2 * axis], index[2 * axis + 1]
+    same, (one, two) = here % 2 == 0, messages
+    return Picked(same, two, one, here > 0), Picked(same, one, two, here < count - 1)
+
+
 def sides_x(index, messages):
     if len(messages) == 2:
         return messages
@@ -167,31 +180,80 @@
     return Scaled(messages[0], 1.0 - first), Scaled(messages[0], first)
 
 
-def pack_y(index, velocity, inv, rhs, *refs):
+EARLY = (LAYERS + 1) // 2
+EACH = REACH + 1 + LAYERS + 1
+
+
+def put(up, down, pair, parity, rows_rhs, ghost, rows_inv, first, last, same=None):
+    offset = parity * EACH
+    row = (1, up.shape[2])
+
+    def store(start, count, lower, upper):
+        if same is not None:
+            lower, upper = jnp.where(same, lower, upper), jnp.where(same, upper, lower)
+        up[pair, pl.ds(offset + start, count), :] = upper
+        down[pair, pl.ds(offset + start, count), :] = lower
+
+    store(0, REACH, *rows_rhs)
+    store(REACH, 1, -0.5 * ghost[0], 0.5 * ghost[1])
+    store(REACH + 1, LAYERS, *rows_inv)
+    both = []
+    for part in range(2):
+        ends = jnp.zeros(row, F32)
+        for k in range(REACH):
+            ends = jnp.where(lanes(row) == 2 * k, first[part][k : k + 1], ends)
+            ends = jnp.where(lanes(row) == 2 * k + 1, last[part][k : k + 1], ends)
+        both.append(ends)
+    store(EACH - 1, 1, *both)
+
+
+def put_own(up, down, velocity, inv, rhs, x, pair, parity, extra, same=None):
+    ny, nz = inv.shape[1:]
+    low, high = rhs[x, 0:REACH, :], rhs[x, ny - REACH : ny, :]
+    if extra is not None:
+        low = low + extra[pl.ds(REACH * ny, REACH), :]
+        high = high + extra[pl.ds((REACH + 1) * ny - REACH, REACH), :]
+    ghost = (velocity[1, x, 0:1, :], velocity[1, x, ny - 1 : ny, :])
+    rows_inv = (inv[x, 0:LAYERS, :], inv[x, ny - LAYERS : ny, :])
+    head, tail = velocity[2, x, 0:REACH, :], velocity[2, x, ny - REACH : ny, :]
+    first = (head[:, 0:1], tail[:, 0:1])
+    last = (head[:, nz - 1 : nz], tail[:, nz - 1 : nz])
+    put(up, down, pair, parity, (low, high), ghost, rows_inv, first, last, same)
+
+
+def pack_y_own(index, velocity, inv, rhs, up, down):
+    nx = rhs.shape[0]
+    same = index[2] % 2 == 0
+
+    def plane(x, carry):
+        rhs[x] = source(velocity, x, nx)
+        return carry
+
+    lax.fori_loop(0, nx, plane, 0, unroll=4)
+
+    def planes(n, carry):
+        for parity in range(2):
+            put_own(up, down, velocity, inv, rhs, 1 + 2 * n + parity, n, parity, None, same)
+        return carry
+
+    lax.fori_loop(0, up.shape[0], planes, 0, unroll=3)
+
+
+def pack_y_halo(index, velocity, inv, rhs, *refs):
     (below, above), (up, down) = sides_x(index, refs[:-2]), refs[-2:]
+    same = index[2] % 2 == 0
     nx, ny, nz = inv.shape
-    each = REACH + 1 + LAYERS + 1
-
-    def put(pair, parity, rows_rhs, ghost, rows_inv, first, last):
-        offset = parity * each
-        for message, part in ((up, 1), (down, 0)):
-            message[pair, pl.ds(offset, REACH), :] = rows_rhs[part]
-            message[pair, pl.ds(offset + REACH, 1), :] = (0.5 if part else -0.5) * ghost[part]
-            message[pair, pl.ds(offset + REACH + 1, LAYERS), :] = rows_inv[part]
-            ends = jnp.zeros((1, nz), F32)
-            for k in range(REACH):
-                ends = jnp.where(lanes((1, nz)) == 2 * k, first[part][k : k + 1], ends)
-                ends = jnp.where(lanes((1, nz)) == 2 * k + 1, last[part][k : k + 1], ends)
-            message[pair, pl.ds(offset + each - 1, 1), :] = ends
+    skip = (nx + 2 * LAYERS) // 2 - 2 * EARLY
 
     def halo(x, message, k_rhs, k_inv, extra):
+        pair = x // 2 if x // 2 < EARLY else x // 2 - skip
         base = (REACH + 1 + k_inv) * ny
         rows_inv = (message[pl.ds(base, LAYERS), :], message[pl.ds(base + ny - LAYERS, LAYERS), :])
         zero_row = jnp.zeros((1, nz), F32)
         zero = jnp.zeros((REACH, nz), F32)
         if k_rhs is None:
             column = jnp.zeros((REACH, 1), F32)
-            put(x // 2, x % 2, (zero, zero), (zero_row, zero_row), rows_inv, (column, column), (column, column))
+            put(up, down, pair, x % 2, (zero, zero), (zero_row, zero_row), rows_inv, (column, column), (column, column), same)
             return
         low, high = message[pl.ds(k_rhs * ny, REACH), :], message[pl.ds((k_rhs + 1) * ny - REACH, REACH), :]
         if extra is not None:
@@ -204,7 +266,7 @@
         head, tail = message[pl.ds(ends, REACH), :], message[pl.ds(ends + ny - REACH, REACH), :]
         first = (head[:, 2 * k_rhs : 2 * k_rhs + 1], tail[:, 2 * k_rhs : 2 * k_rhs + 1])
         last = (head[:, 2 * k_rhs + 1 : 2 * k_rhs + 2], tail[:, 2 * k_rhs + 1 : 2 * k_rhs + 2])
-        put(x // 2, x % 2, (low, high), ghost, rows_inv, first, last)
+        put(up, down, pair, x % 2, (low, high), ghost, rows_inv, first, last, same)
 
     for k in range(LAYERS):
         halo(k, below, k - 1 if k else None, k, (-0.5, 0) if k == LAYERS - 1 else None)
@@ -215,45 +277,19 @@
             k,
             (0.5, nx - 1) if k == 0 else None,
         )
-
-    def own(x, pair, parity, extra):
-        low, high = rhs[x, 0:REACH, :], rhs[x, ny - REACH : ny, :]
-        if extra is not None:
-            low = low + extra[pl.ds(REACH * ny, REACH), :]
-            high = high + extra[pl.ds((REACH + 1) * ny - REACH, REACH), :]
-        ghost = (velocity[1, x, 0:1, :], velocity[1, x, ny - 1 : ny, :])
-        rows_inv = (inv[x, 0:LAYERS, :], inv[x, ny - LAYERS : ny, :])
-        head, tail = velocity[2, x, 0:REACH, :], velocity[2, x, ny - REACH : ny, :]
-        first = (head[:, 0:1], tail[:, 0:1])
-        last = (head[:, nz - 1 : nz], tail[:, nz - 1 : nz])
-        put(pair, parity, (low, high), ghost, rows_inv, first, last)
-
-    def at(x, extra):
-        own(x, (x + LAYERS) // 2, (x + LAYERS) % 2, extra)
-
-    at(0, below)
-    at(nx - 1, above)
-    begin = 1 + (1 + LAYERS) % 2
-    finish = begin + (nx - 1 - begin) // 2 * 2
-    for x in (*range(1, begin), *range(finish, nx - 1)):
-        at(x, None)
-
-    def planes(n, carry):
-        for parity in range(2):
-            own(begin + 2 * n + parity, (begin + LAYERS) // 2 + n, parity, None)
-        return carry
-
-    lax.fori_loop(0, (finish - begin) // 2, planes, 0, unroll=3)
+    put_own(up, down, velocity, inv, rhs, 0, EARLY - 1, 1, below, same)
+    put_own(up, down, velocity, inv, rhs, nx - 1, EARLY, 0, above, same)
 
 
 def pack_z(index, velocity, inv, rhs, *refs):
-    (below, above), before, after = sides_x(index, refs[:-14]), refs[-14], refs[-13]
+    (below, above), received = sides_x(index, refs[:-16]), refs[-16:-12]
+    received = [*sides(index, 1, received[:2]), *sides(index, 1, received[2:])]
+    same = index[4] % 2 == 0
     rhs_far, inv_far, up, down, strip_rhs_far, strip_inv_far = refs[-12:-6]
     rhs_wide, inv_wide, ends, strip_rhs, strip_inv, sems = refs[-6:]
     nx, ny, nz = inv.shape
     wide = nx + 2 * LAYERS
     rows = ny + 2 * WIDE
-    each = REACH + 1 + LAYERS + 1
     mine = pl.ds(WIDE, ny)
     edge = (WIDE, nz)
     groups = strip_rhs.shape[0]
@@ -291,9 +327,14 @@
             ref[x] = jnp.zeros((rows, nz), F32)
 
     def finish(x, ghost_low, ghost_high):
-        low, high = before[x // 2], after[x // 2]
-        low = jnp.where(x % 2 == 0, low, pltpu.roll(low, ROWS - each, 0))[0:SLOT]
-        high = jnp.where(x % 2 == 0, high, pltpu.roll(high, ROWS - each, 0))[0:SLOT]
+        pair = x // 2
+        if not isinstance(x, int):
+            low, high = (ref[pair - EARLY] for ref in received[:2])
+        else:
+            pair = pair if pair < EARLY else pair - (wide // 2 - 2 * EARLY)
+            low, high = (ref[pair] for ref in received[2:])
+        low = jnp.where(x % 2 == 0, low, pltpu.roll(low, ROWS - EACH, 0))[0:SLOT]
+        high = jnp.where(x % 2 == 0, high, pltpu.roll(high, ROWS - EACH, 0))[0:SLOT]
         part = pltpu.roll(low, WIDE - REACH, 0)[0:WIDE]
         part = jnp.where(sublanes(edge) >= WIDE - REACH, part, 0.0)
         part = part - jnp.where(sublanes(edge) == WIDE - 1, 0.5 * ghost_low, 0.0)
@@ -312,7 +353,7 @@
             sublanes(edge) == WIDE - 1, high[REACH : REACH + 1], 0.0
         )
         for message, start, place in ((low, WIDE - REACH, 0), (high, 0, WIDE + ny)):
-            line = message[each - 1 : each]
+            line = message[EACH - 1 : EACH]
             one = jnp.zeros(edge, F32)
             two = jnp.zeros(edge, F32)
             for k in range(REACH):
@@ -334,7 +375,9 @@
         finish(x + LAYERS, velocity[1, x, 0:1, :], velocity[1, x, ny - 1 : ny, :])
         return carry
 
-    lax.fori_loop(0, nx, middle, 0, unroll=4)
+    lax.fori_loop(1, nx - 1, middle, 0, unroll=10)
+    for x in (0, nx - 1):
+        finish(x + LAYERS, velocity[1, x, 0:1, :], velocity[1, x, ny - 1 : ny, :])
     copies = [
         pltpu.make_async_copy(ref.at[pl.ds(0, wide)], far, sems.at[n])
         for n, (ref, far) in enumerate(((rhs_wide, rhs_far), (inv_wide, inv_far)))
@@ -377,16 +420,16 @@
 
     def both(n, carry):
         one, two = pack(n)
-        up[n] = one
-        down[n] = two
+        up[n] = jnp.where(same, one, two)
+        down[n] = jnp.where(same, two, one)
         return carry
 
     lax.fori_loop(0, halves, both, 0, unroll=2)
 
     def more(n, carry):
         one, two = pack(n + halves)
-        up[n] += pltpu.roll(one, SPAN // 2, 1)
-        down[n] += pltpu.roll(two, SPAN // 2, 1)
+        up[n] += pltpu.roll(jnp.where(same, one, two), SPAN // 2, 1)
+        down[n] += pltpu.roll(jnp.where(same, two, one), SPAN // 2, 1)
         return carry
 
     lax.fori_loop(0, groups - halves, more, 0, unroll=2)
@@ -408,7 +451,7 @@
 
 
 class Stencil:
-    def __init__(self, inv, root, ax, ay, az, vs, planes, edges=None, unroll=4):
+    def __init__(self, inv, root, ax, ay, az, vs, planes, edges=None, unroll=6):
         self.inv, self.root, self.ax, self.ay, self.az, self.vs = inv, root, ax, ay, az, vs
         self.planes, self.edges, self.unroll = planes, edges or (lambda ref: None), unroll
         self.count, self.rows, self.nz = inv.shape
@@ -512,7 +555,7 @@
             return tuple(sums)
 
         zero = jnp.zeros((WIDE, self.nz), F32)
-        return lax.fori_loop(start, stop, measure, (zero,) * (len(PAIRS) + 1), unroll=2)
+        return lax.fori_loop(start, stop, measure, (zero,) * (len(PAIRS) + 1), unroll=4)
 
 
 def basis_main(rhs_far, inv_far, *refs):
@@ -558,7 +601,8 @@
         copy.wait()
 
 
-def basis_strips(nx, rhs_far, inv_far, before, after, sums, *refs):
+def basis_strips(nx, index, rhs_far, inv_far, one, two, sums, *refs):
+    before, after = sides(index, 2, (one, two))
     outs, dots = refs[:ITERS], refs[ITERS]
     rhs, inv, root, ax, ay, az = refs[ITERS + 1 : ITERS + 7]
     vs, outs_near = refs[ITERS + 7 : 2 * ITERS + 7], refs[2 * ITERS + 7 : 3 * ITERS + 7]
@@ -572,7 +616,7 @@
         load.start()
     for load in loads:
         load.wait()
-    halves = before.shape[0]
+    halves = one.shape[0]
     whole = (rows, nz)
     place = lanes(whole) % SPAN
 
@@ -831,7 +875,7 @@
         lax.fori_loop(*bounds[n], combine, 0, unroll=4)
         for load in other_loads[n]:
             load.wait()
-        lax.fori_loop(n * each // 2, (n + 1) * each // 2, pair, 0, unroll=2)
+        lax.fori_loop(n * each // 2, (n + 1) * each // 2, pair, 0, unroll=4)
         part = pl.ds(n * each, each)
         stores.append(start(pressure.at[part], pressure_far.at[part]))
         for d in range(3):
@@ -984,24 +1028,34 @@
     devices = count_x * count_y * count_z
     cells = (nx, ny, nz)
     rank = factor_x.shape[1]
-    index = lax.axis_index("gx").reshape(1)
+    index_x = lax.axis_index("gx").reshape(1)
+    index = jnp.stack([jnp.int32(f(axis)) for axis in AXES for f in (lax.axis_index, lax.axis_size)])
 
     shape = (((REACH + 1 + LAYERS + 1) * ny + 2 * REACH), nz)
     number = 1 if count_x == 2 else 2
     sent = call(
         pack_x,
         [shape] * number,
-        [index, velocity, inv_density],
+        [index_x, velocity, inv_density],
         scratch=[(number, 3, LAYERS, ny, nz), (number, LAYERS, ny, nz)],
         smem=1,
         far_in=(1, 2),
         sems=4 * number,
     )
     near = [swap(sent[0], "gx", 1)] if count_x == 2 else list(exchange(*sent, "gx"))
-    rhs, = call(sources, [cells], [velocity], cost=(nx * ny * nz * 10, 4 * cost_of(cells)))
-    shape = (wide // 2, ROWS, nz)
-    up, down = call(pack_y, [shape, shape], [index, velocity, inv_density, rhs, *near], smem=1)
-    before, after = exchange(up, down, "gy")
+    pairs = wide // 2 - 2 * EARLY
+    shape = (pairs, ROWS, nz)
+    rhs, up, down = call(
+        pack_y_own,
+        [cells, shape, shape],
+        [index, velocity, inv_density],
+        smem=1,
+        cost=(nx * ny * nz * 10, 6 * cost_of(cells)),
+    )
+    received = list(ring(up, down, "gy", closed=False))
+    shape = (2 * EARLY, ROWS, nz)
+    up, down = call(pack_y_halo, [shape, shape], [index, velocity, inv_density, rhs, *near], smem=1)
+    received += ring(up, down, "gy")
     parts = nz // SPAN
     groups = -(-wide // parts)
     message = (-(-groups // 2), rows, nz)
@@ -1010,14 +1064,14 @@
     rhs_wide, inv_wide, up, down, strip_rhs, strip_inv = call(
         pack_z,
         [(wide, rows, nz)] * 2 + [message, message, strip, strip],
-        [index, velocity, inv_density, rhs, *near, before, after],
+        [index, velocity, inv_density, rhs, *near, *received],
         scratch=[whole] * 3 + [strip] * 2,
         smem=1,
         limit=18,
         far_out=(0, 1, 4, 5),
         sems=4,
     )
-    before, after = exchange(up, down, "gz")
+    came = ring(up, down, "gz")
     span = (nx + 2, rows, nz)
     whole = (wide, rows, nz)
     *spans, sums = call(
@@ -1035,9 +1089,10 @@
     *strips, dots = call(
         functools.partial(basis_strips, nx),
         [strip] * ITERS + [(devices, WIDE, nz)],
-        [strip_rhs, strip_inv, before, after, sums],
+        [index, strip_rhs, strip_inv, *came, sums],
         scratch=[padded] * (6 + 2 * ITERS) + [strip] * 2,
-        far_in=(0, 1),
+        smem=1,
+        far_in=(1, 2),
         far_out=range(ITERS),
         sems=ITERS + 2,
     )

time: 114 us -> 104 us (0.912)
  waiting for transfers between devices: 46.3 us -> 38.1 us
  starting transfers between devices: 24.6 us -> 21.4 us
  local copies, waits for them, and re-layouts: 0.4 us -> 1.7 us
    ppermute x9, waiting for transfers between devices: 30.7 us -> 26.4 us  [swap(): return lax.ppermute(value, axis, [(i, i ^ mask) for i in range(count)])]
    all_to_all x1, starting transfers between devices: 7.8 us -> 3.96 us  [per_device(): dots = lax.all_to_all(dots, AXES, 0, 0, tiled=True)]
    ppermute x4 -> x6, waiting for transfers between devices: 7.41 us -> 3.68 us  [ring(): return (lax.ppermute(one, axis, near), lax.ppermute(two, axis, far))]
    unnamed x11 -> x13, local copies, waits for them, and re-layouts: 0.1 us -> 1.32 us
    ppermute x4 -> x6, starting transfers between devices: 7.63 us -> 8.37 us  [ring(): return (lax.ppermute(one, axis, near), lax.ppermute(two, axis, far))]
  transfers between devices with their start and end apart: 14 -> 16, of which waited for: 11 -> 10; matrix products, arithmetic and copies ran while one was open for 0% -> 1% of each run, Pallas kernels for 12% -> 14%
where the time goes in v5:
time: 104 us
  Pallas kernels  42 us (40%)
  waiting for transfers between devices  38.1 us (37%)
  starting transfers between devices  21.4 us (21%)
  local copies, waits for them, and re-layouts  1.7 us (2%)
    pallas_call x12, Pallas kernels, call(): pl.pallas_call(body, out_shape=[pltpu.HBM(shape, F32) if n in far_out or...  41.2 us
    ppermute x9, waiting for transfers between devices, swap(): return lax.ppermute(value, axis, [(i, i ^ mask) for i in range(count)])  26.4 us
    ppermute x9, starting transfers between devices, swap(): return lax.ppermute(value, axis, [(i, i ^ mask) for i in range(count)])  9.05 us
    ppermute x6, starting transfers between devices, ring(): return (lax.ppermute(one, axis, near), lax.ppermute(two, axis, far))  8.37 us
    all_to_all x1, waiting for transfers between devices, per_device(): dots = lax.all_to_all(dots, AXES, 0, 0, tiled=True)  8.02 us
    all_to_all x1, starting transfers between devices, per_device(): dots = lax.all_to_all(dots, AXES, 0, 0, tiled=True)  3.96 us
    ppermute x6, waiting for transfers between devices, ring(): return (lax.ppermute(one, axis, near), lax.ppermute(two, axis, far))  3.68 us
  transfers between devices with their start and end apart: 16, of which 10 were waited for; matrix products, arithmetic and copies ran while one was open for 1% of the time, Pallas kernels for 14%

profile of v5, /device:TPU:0, one launch (start us, length us, event | category | flops | bytes accessed | tf_op | source)
XLA Modules:
  0.0 104.0 jit_solution(16237833009957126269)
XLA Ops:
  0.6 2.3 %shard_map.77 = f32[712,128]{1,0:T(8,128)} custom-call(s32[1]{0:T(128)} %bitcast.index, f32[3,32,64,128]{3,2,1,0:T(8,128)} %refs_9_.1, f32[32,64,128]{2,1,0:T(8,128)} %refs_10_.1), custom_call_target="tpu_custom_call" | custom-call | tf_op jit(solution)/shard_map/pallas_call | solution.py:33
  2.9 3.0 %collective-permute-start = (f32[712,128]{1,0:T(8,128)}, f32[712,128]{1,0:T(8,128)S(1)}, u32[]{:S(2)}, u32[]{:S(2)}) collective-permute-start(f32[712,128]{1,0:T(8,128)} %shard_map.77), channel_id=1, source_target_pairs={{0,16},{16,0},{1,17},{17,1},{2,18},{18,2},{3,19},{19,3},{4,20},{20... | collective-permute-start | bytes 1093640 | tf_op jit(solution)/shard_map/ppermute | solution.py:1021
  6.0 1.2 %copy-done.1 = f32[32,64,128]{2,1,0:T(8,128)S(1)} copy-done((f32[32,64,128]{2,1,0:T(8,128)S(1)}, f32[32,64,128]{2,1,0:T(8,128)}, u32[]{:S(2)}) %copy-start.1) | copy-done | bytes 1048600
  7.3 2.2 %shard_map.76 = (f32[32,64,128]{2,1,0:T(8,128)S(1)}, f32[15,24,128]{2,1,0:T(8,128)S(1)}, f32[15,24,128]{2,1,0:T(8,128)S(1)}) custom-call(s32[6]{0:T(128)S(1)} %stack.34.index, f32[3,32,64,128]{3,2,1,0:T(8,128)S(1)} %copy-done, f32[32,64,128]{2,1,0:T(8,128)S(1)} %copy-done.1), custom_call_target="tpu_custom_call" | custom-call | flops 2621440 | bytes 6291456 | tf_op jit(solution)/shard_map/pallas_call | solution.py:33
  9.5 1.6 %collective-permute-start.1 = (f32[15,24,128]{2,1,0:T(8,128)S(1)}, f32[15,24,128]{2,1,0:T(8,128)S(1)}, u32[]{:S(2)}, u32[]{:S(2)}) collective-permute-start(f32[15,24,128]{2,1,0:T(8,128)S(1)} %get-tuple-element.51), channel_id=1, source_target_pairs={{0,4},{4,0},{8,12},{12,8},{1,5},{5,1},{9,13},{13,9},{2,6},{6,2},{1... | collective-permute-start | bytes 552968 | tf_op jit(solution)/shard_map/ppermute | solution.py:98
  11.1 0.7 collective-permute-start.2
  11.8 2.9 %collective-permute-done.refs_0_ = f32[712,128]{1,0:T(8,128)S(1)} collective-permute-done((f32[712,128]{1,0:T(8,128)}, f32[712,128]{1,0:T(8,128)S(1)}, u32[]{:S(2)}, u32[]{:S(2)}) %collective-permute-start) | collective-permute-done | bytes 364576 | tf_op jit(solution)/shard_map/ppermute | solution.py:1021
  14.7 0.7 shard_map.78
  15.4 1.9 %collective-permute-start.3 = (f32[6,24,128]{2,1,0:T(8,128)S(1)}, f32[6,24,128]{2,1,0:T(8,128)S(1)}, u32[]{:S(2)}, u32[]{:S(2)}) collective-permute-start(f32[6,24,128]{2,1,0:T(8,128)S(1)} %get-tuple-element.53), channel_id=1, source_target_pairs={{0,4},{4,0},{8,12},{12,8},{1,5},{5,1},{9,13},{13,9},{2,6},{6,2},{1... | collective-permute-start | bytes 221192 | tf_op jit(solution)/shard_map/ppermute | solution.py:98
  17.3 2.5 %collective-permute-start.4 = (f32[6,24,128]{2,1,0:T(8,128)S(1)}, f32[6,24,128]{2,1,0:T(8,128)S(1)}, u32[]{:S(2)}, u32[]{:S(2)}) collective-permute-start(f32[6,24,128]{2,1,0:T(8,128)S(1)} %get-tuple-element.54), channel_id=1, source_target_pairs={{0,12},{4,8},{8,4},{12,0},{1,13},{5,9},{9,5},{13,1},{2,14},{6,10},... | collective-permute-start | bytes 221192 | tf_op jit(solution)/shard_map/ppermute | solution.py:98
  19.8 3.6 %collective-permute-done.4.refs_4_ = f32[6,24,128]{2,1,0:T(8,128)S(1)} collective-permute-done((f32[6,24,128]{2,1,0:T(8,128)S(1)}, f32[6,24,128]{2,1,0:T(8,128)S(1)}, u32[]{:S(2)}, u32[]{:S(2)}) %collective-permute-start.4) | collective-permute-done | bytes 73760 | tf_op jit(solution)/shard_map/ppermute | solution.py:98
  23.4 7.5 %shard_map.79 = (f32[42,80,128]{2,1,0:T(8,128)}, f32[42,80,128]{2,1,0:T(8,128)}, f32[6,80,128]{2,1,0:T(8,128)}, f32[6,80,128]{2,1,0:T(8,128)}, f32[11,80,128]{2,1,0:T(8,128)}, /*index=5*/f32[11,80,128]{2,1,0:T(8,128)}) custom-call(s32[6]{0:T(128)S(1)} %stack.34.index, f32[3,32,64,128]{3,2,1,0:T(8,128)S(1)} %copy-done, f32[32,64,128]{2,1,0:T(8,128)S(1)} %copy-done.2, ...), custom_call_target="tpu_custom_call" | custom-call | tf_op jit(solution)/shard_map/pallas_call | solution.py:33
  31.0 1.6 %collective-permute-start.6 = (f32[6,80,128]{2,1,0:T(8,128)}, f32[6,80,128]{2,1,0:T(8,128)S(1)}, u32[]{:S(2)}, u32[]{:S(2)}) collective-permute-start(f32[6,80,128]{2,1,0:T(8,128)} %get-tuple-element.58), channel_id=1, source_target_pairs={{0,3},{1,2},{2,1},{3,0},{4,7},{5,6},{6,5},{7,4},{8,11},{9,10},{10,... | collective-permute-start | bytes 737288 | tf_op jit(solution)/shard_map/ppermute | solution.py:98
  32.7 11.4 %shard_map.80 = (f32[34,80,128]{2,1,0:T(8,128)}, f32[34,80,128]{2,1,0:T(8,128)}, f32[34,80,128]{2,1,0:T(8,128)}, f32[34,80,128]{2,1,0:T(8,128)}, f32[34,80,128]{2,1,0:T(8,128)}, /*index=5*/f32[11,8,128]{2,1,0:T(8,128)S(1)}) custom-call(f32[42,80,128]{2,1,0:T(8,128)} %get-tuple-element.59.rhs_far, f32[42,80,128]{2,1,0:T(8,128)} %get-tuple-element.60.inv_far), custom_call_target="tpu_custom_call" | custom-call | flops 43008000 | bytes 12042240 | tf_op jit(solution)/shard_map/pallas_call | solution.py:33
  44.1 6.1 %shard_map.81 = (f32[11,80,128]{2,1,0:T(8,128)}, f32[11,80,128]{2,1,0:T(8,128)}, f32[11,80,128]{2,1,0:T(8,128)}, f32[11,80,128]{2,1,0:T(8,128)}, f32[32,8,128]{2,1,0:T(8,128)}) custom-call(s32[6]{0:T(128)S(1)} %stack.34.index, f32[11,80,128]{2,1,0:T(8,128)} %get-tuple-element.55.rhs_far, f32[11,80,128]{2,1,0:T(8,128)} %get-tuple-element.56.inv_far, ...), custom_call_target="tpu_custom_call" | custom-call | tf_op jit(solution)/shard_map/pallas_call | solution.py:33
  50.2 4.0 %all-to-all-start = ((f32[32,8,128]{2,1,0:T(8,128)}), f32[32,8,128]{2,1,0:T(8,128)S(1)}, u32[]{:S(2)}, u32[]{:S(2)}) async-start(f32[32,8,128]{2,1,0:T(8,128)} %get-tuple-element.62), calls=%async_computation | async-start | bytes 262144 | tf_op jit(solution)/shard_map/all_to_all | solution.py:1099
  54.1 8.0 %all-to-all-done.dots = f32[32,8,128]{2,1,0:T(8,128)S(1)} async-done(((f32[32,8,128]{2,1,0:T(8,128)}), f32[32,8,128]{2,1,0:T(8,128)S(1)}, u32[]{:S(2)}, u32[]{:S(2)}) %all-to-all-start) | async-done | bytes 131104 | tf_op jit(solution)/shard_map/all_to_all | solution.py:1099
  62.2 8.4 %shard_map.82 = (f32[32,64,128]{2,1,0:T(8,128)}, f32[3,32,64,128]{3,2,1,0:T(8,128)}, f32[64,16,128]{2,1,0:T(8,128)S(1)}, f32[64,16,128]{2,1,0:T(8,128)S(1)}, f32[2,64,16,128]{3,2,1,0:T(8,128)S(1)}) custom-call(f32[32,8,128]{2,1,0:T(8,128)S(1)} %all-to-all-done.dots, bf16[128,256]{1,0:T(8,128)(2,1)S(1)} %maximum_maximum_fusion.columns, ...), custom_call_target="tpu_custom_call" | custom-call | tf_op jit(solution)/shard_map/pallas_call | solution.py:33
  71.3 0.8 shard_map.83
  72.1 1.1 %collective-permute-done.7.came = f32[2,64,16,128]{3,2,1,0:T(8,128)S(1)} collective-permute-done((f32[2,64,16,128]{3,2,1,0:T(8,128)S(1)}, f32[2,64,16,128]{3,2,1,0:T(8,128)S(1)}, u32[]{:S(2)}, u32[]{:S(2)}) %collective-permute-start.7) | collective-permute-done | bytes 1048608 | tf_op jit(solution)/shard_map/ppermute | solution.py:1021
  74.5 0.9 collective-permute-start.9
  75.4 7.0 %collective-permute-done.8.p_came = f32[32,16,128]{2,1,0:T(8,128)S(1)} collective-permute-done((f32[32,16,128]{2,1,0:T(8,128)S(1)}, f32[32,16,128]{2,1,0:T(8,128)S(1)}, u32[]{:S(2)}, u32[]{:S(2)}) %collective-permute-start.8) | collective-permute-done | bytes 262176 | tf_op jit(solution)/shard_map/ppermute | solution.py:1021
  83.0 1.0 collective-permute-start.10
  84.0 1.2 %collective-permute-start.11 = (f32[256,128]{1,0:T(8,128)S(1)}, f32[256,128]{1,0:T(8,128)S(1)}, u32[]{:S(2)}, u32[]{:S(2)}) collective-permute-start(f32[256,128]{1,0:T(8,128)S(1)} %get-tuple-element.88), channel_id=1, source_target_pairs={{0,8},{4,12},{8,0},{12,4},{1,9},{5,13},{9,1},{13,5},{2,10},{6,14},... | collective-permute-start | bytes 393224 | tf_op jit(solution)/shard_map/ppermute | solution.py:1021
  85.1 4.3 %collective-permute-done.10.p_came = f32[2,128,128]{2,1,0:T(8,128)S(1)} collective-permute-done((f32[2,128,128]{2,1,0:T(8,128)S(1)}, f32[2,128,128]{2,1,0:T(8,128)S(1)}, u32[]{:S(2)}, u32[]{:S(2)}) %collective-permute-start.10) | collective-permute-done | bytes 131104 | tf_op jit(solution)/shard_map/ppermute | solution.py:1021
  89.4 2.7 %collective-permute-done.11.q_came = f32[256,128]{1,0:T(8,128)S(1)} collective-permute-done((f32[256,128]{1,0:T(8,128)S(1)}, f32[256,128]{1,0:T(8,128)S(1)}, u32[]{:S(2)}, u32[]{:S(2)}) %collective-permute-start.11) | collective-permute-done | bytes 131104 | tf_op jit(solution)/shard_map/ppermute | solution.py:1021
  92.3 1.2 %collective-permute-start.13 = (f32[128,128]{1,0:T(8,128)S(1)}, f32[128,128]{1,0:T(8,128)S(1)}, u32[]{:S(2)}, u32[]{:S(2)}) collective-permute-start(f32[128,128]{1,0:T(8,128)S(1)} %get-tuple-element.92), channel_id=1, source_target_pairs={{0,2},{1,3},{2,0},{3,1},{4,6},{5,7},{6,4},{7,5},{8,10},{9,11},{10,... | collective-permute-start | bytes 196616 | tf_op jit(solution)/shard_map/ppermute | solution.py:1021
  93.5 3.9 %collective-permute-done.12.p_came = f32[128,128]{1,0:T(8,128)S(1)} collective-permute-done((f32[128,128]{1,0:T(8,128)S(1)}, f32[128,128]{1,0:T(8,128)S(1)}, u32[]{:S(2)}, u32[]{:S(2)}) %collective-permute-start.12) | collective-permute-done | bytes 65568 | tf_op jit(solution)/shard_map/ppermute | solution.py:1021
  97.4 0.7 shard_map.87
  98.0 0.7 collective-permute-start.14
  98.7 4.4 %collective-permute-done.14.came = f32[64,512]{1,0:T(8,128)S(1)} collective-permute-done((f32[64,512]{1,0:T(8,128)S(1)}, f32[64,512]{1,0:T(8,128)S(1)}, u32[]{:S(2)}, u32[]{:S(2)}) %collective-permute-start.14) | collective-permute-done | bytes 131104 | tf_op jit(solution)/shard_map/ppermute | solution.py:1021
  103.1 1.0 shard_map.88
  (38 shorter events, 2.9 us)
Async XLA Ops:
  0.6 5.4 %copy-start = (f32[3,32,64,128]{3,2,1,0:T(8,128)S(1)}, f32[3,32,64,128]{3,2,1,0:T(8,128)}, u32[]{:S(2)}) copy-start(f32[3,32,64,128]{3,2,1,0:T(8,128)} %refs_9_.1) | copy-start | bytes 9437188
  2.9 11.7 %collective-permute-start = (f32[712,128]{1,0:T(8,128)}, f32[712,128]{1,0:T(8,128)S(1)}, u32[]{:S(2)}, u32[]{:S(2)}) collective-permute-start(f32[712,128]{1,0:T(8,128)} %shard_map.77), channel_id=1, source_target_pairs={{0,16},{16,0},{1,17},{17,1},{2,18},{18,2},{3,19},{19,3},{4,20},{20... | collective-permute-start | bytes 1093640 | tf_op jit(solution)/shard_map/ppermute | solution.py:1021
  6.0 1.2 %copy-start.1 = (f32[32,64,128]{2,1,0:T(8,128)S(1)}, f32[32,64,128]{2,1,0:T(8,128)}, u32[]{:S(2)}) copy-start(f32[32,64,128]{2,1,0:T(8,128)} %refs_10_.1) | copy-start | bytes 3145732
  9.5 10.2 %collective-permute-start.1 = (f32[15,24,128]{2,1,0:T(8,128)S(1)}, f32[15,24,128]{2,1,0:T(8,128)S(1)}, u32[]{:S(2)}, u32[]{:S(2)}) collective-permute-start(f32[15,24,128]{2,1,0:T(8,128)S(1)} %get-tuple-element.51), channel_id=1, source_target_pairs={{0,4},{4,0},{8,12},{12,8},{1,5},{5,1},{9,13},{13,9},{2,6},{6,2},{1... | collective-permute-start | bytes 552968 | tf_op jit(solution)/shard_map/ppermute | solution.py:98
  11.1 8.6 %collective-permute-start.2 = (f32[15,24,128]{2,1,0:T(8,128)S(1)}, f32[15,24,128]{2,1,0:T(8,128)S(1)}, u32[]{:S(2)}, u32[]{:S(2)}) collective-permute-start(f32[15,24,128]{2,1,0:T(8,128)S(1)} %get-tuple-element.52), channel_id=1, source_target_pairs={{4,8},{8,4},{5,9},{9,5},{6,10},{10,6},{7,11},{11,7},{20,24},{24,20... | collective-permute-start | bytes 552968 | tf_op jit(solution)/shard_map/ppermute | solution.py:98
  14.7 8.7 %copy-start.2 = (f32[32,64,128]{2,1,0:T(8,128)S(1)}, f32[32,64,128]{2,1,0:T(8,128)}, u32[]{:S(2)}) copy-start(f32[32,64,128]{2,1,0:T(8,128)} %refs_10_.1) | copy-start | bytes 3145732
  15.4 4.4 %collective-permute-start.3 = (f32[6,24,128]{2,1,0:T(8,128)S(1)}, f32[6,24,128]{2,1,0:T(8,128)S(1)}, u32[]{:S(2)}, u32[]{:S(2)}) collective-permute-start(f32[6,24,128]{2,1,0:T(8,128)S(1)} %get-tuple-element.53), channel_id=1, source_target_pairs={{0,4},{4,0},{8,12},{12,8},{1,5},{5,1},{9,13},{13,9},{2,6},{6,2},{1... | collective-permute-start | bytes 221192 | tf_op jit(solution)/shard_map/ppermute | solution.py:98
  17.2 15.4 %copy-start.3 = (f32[128,64]{0,1:T(8,128)S(1)}, f32[128,64]{0,1:T(8,128)}, u32[]{:S(2)}) copy-start(f32[128,64]{0,1:T(8,128)} %param.9) | copy-start | bytes 98308
  17.3 6.2 %collective-permute-start.4 = (f32[6,24,128]{2,1,0:T(8,128)S(1)}, f32[6,24,128]{2,1,0:T(8,128)S(1)}, u32[]{:S(2)}, u32[]{:S(2)}) collective-permute-start(f32[6,24,128]{2,1,0:T(8,128)S(1)} %get-tuple-element.54), channel_id=1, source_target_pairs={{0,12},{4,8},{8,4},{12,0},{1,13},{5,9},{9,5},{13,1},{2,14},{6,10},... | collective-permute-start | bytes 221192 | tf_op jit(solution)/shard_map/ppermute | solution.py:98
  30.9 13.1 %collective-permute-start.5 = (f32[6,80,128]{2,1,0:T(8,128)}, f32[6,80,128]{2,1,0:T(8,128)S(1)}, u32[]{:S(2)}, u32[]{:S(2)}) collective-permute-start(f32[6,80,128]{2,1,0:T(8,128)} %get-tuple-element.57), channel_id=1, source_target_pairs={{0,1},{1,0},{2,3},{3,2},{4,5},{5,4},{6,7},{7,6},{8,9},{9,8},{10,11... | collective-permute-start | bytes 737288 | tf_op jit(solution)/shard_map/ppermute | solution.py:98
  31.0 13.0 %collective-permute-start.6 = (f32[6,80,128]{2,1,0:T(8,128)}, f32[6,80,128]{2,1,0:T(8,128)S(1)}, u32[]{:S(2)}, u32[]{:S(2)}) collective-permute-start(f32[6,80,128]{2,1,0:T(8,128)} %get-tuple-element.58), channel_id=1, source_target_pairs={{0,3},{1,2},{2,1},{3,0},{4,7},{5,6},{6,5},{7,4},{8,11},{9,10},{10,... | collective-permute-start | bytes 737288 | tf_op jit(solution)/shard_map/ppermute | solution.py:98
  50.2 12.0 %all-to-all-start = ((f32[32,8,128]{2,1,0:T(8,128)}), f32[32,8,128]{2,1,0:T(8,128)S(1)}, u32[]{:S(2)}, u32[]{:S(2)}) async-start(f32[32,8,128]{2,1,0:T(8,128)} %get-tuple-element.62), calls=%async_computation | async-start | bytes 262144 | tf_op jit(solution)/shard_map/all_to_all | solution.py:1099
  62.2 8.7 %copy-start.4 = (f32[64,64]{1,0:T(8,128)S(1)}, f32[64,64]{1,0:T(8,128)}, u32[]{:S(2)}) copy-start(f32[64,64]{1,0:T(8,128)} %param.8) | copy-start | bytes 49156
  62.2 8.9 %copy-start.5 = (f32[32,64]{1,0:T(8,128)S(1)}, f32[32,64]{1,0:T(8,128)}, u32[]{:S(2)}) copy-start(f32[32,64]{1,0:T(8,128)} %param.7) | copy-start | bytes 24580
  70.5 2.7 %collective-permute-start.7 = (f32[2,64,16,128]{3,2,1,0:T(8,128)S(1)}, f32[2,64,16,128]{3,2,1,0:T(8,128)S(1)}, u32[]{:S(2)}, u32[]{:S(2)}) collective-permute-start(f32[2,64,16,128]{3,2,1,0:T(8,128)S(1)} %get-tuple-element.76), channel_id=1, source_target_pairs={{0,1},{1,0},{2,3},{3,2},{4,5},{5,4},{6,7},{7,6},{8,9},{9,8},{10,11... | collective-permute-start | bytes 3145736 | tf_op jit(solution)/shard_map/ppermute | solution.py:1021
  73.9 8.5 %collective-permute-start.8 = (f32[32,16,128]{2,1,0:T(8,128)S(1)}, f32[32,16,128]{2,1,0:T(8,128)S(1)}, u32[]{:S(2)}, u32[]{:S(2)}) collective-permute-start(f32[32,16,128]{2,1,0:T(8,128)S(1)} %get-tuple-element.80), channel_id=1, source_target_pairs={{0,2},{1,3},{2,0},{3,1},{4,6},{5,7},{6,4},{7,5},{8,10},{9,11},{10,... | collective-permute-start | bytes 786440 | tf_op jit(solution)/shard_map/ppermute | solution.py:1021
  74.5 8.1 %collective-permute-start.9 = (f32[2,256,128]{2,1,0:T(8,128)S(1)}, f32[2,256,128]{2,1,0:T(8,128)S(1)}, u32[]{:S(2)}, u32[]{:S(2)}) collective-permute-start(f32[2,256,128]{2,1,0:T(8,128)S(1)} %get-tuple-element.83), channel_id=1, source_target_pairs={{0,4},{4,0},{8,12},{12,8},{1,5},{5,1},{9,13},{13,9},{2,6},{6,2},{1... | collective-permute-start | bytes 786440 | tf_op jit(solution)/shard_map/ppermute | solution.py:1021
  83.0 6.5 %collective-permute-start.10 = (f32[2,128,128]{2,1,0:T(8,128)S(1)}, f32[2,128,128]{2,1,0:T(8,128)S(1)}, u32[]{:S(2)}, u32[]{:S(2)}) collective-permute-start(f32[2,128,128]{2,1,0:T(8,128)S(1)} %get-tuple-element.86), channel_id=1, source_target_pairs={{0,4},{4,0},{8,12},{12,8},{1,5},{5,1},{9,13},{13,9},{2,6},{6,2},{1... | collective-permute-start | bytes 393224 | tf_op jit(solution)/shard_map/ppermute | solution.py:1021
  84.0 8.1 %collective-permute-start.11 = (f32[256,128]{1,0:T(8,128)S(1)}, f32[256,128]{1,0:T(8,128)S(1)}, u32[]{:S(2)}, u32[]{:S(2)}) collective-permute-start(f32[256,128]{1,0:T(8,128)S(1)} %get-tuple-element.88), channel_id=1, source_target_pairs={{0,8},{4,12},{8,0},{12,4},{1,9},{5,13},{9,1},{13,5},{2,10},{6,14},... | collective-permute-start | bytes 393224 | tf_op jit(solution)/shard_map/ppermute | solution.py:1021
  92.1 5.2 %collective-permute-start.12 = (f32[128,128]{1,0:T(8,128)S(1)}, f32[128,128]{1,0:T(8,128)S(1)}, u32[]{:S(2)}, u32[]{:S(2)}) collective-permute-start(f32[128,128]{1,0:T(8,128)S(1)} %get-tuple-element.90), channel_id=1, source_target_pairs={{0,8},{4,12},{8,0},{12,4},{1,9},{5,13},{9,1},{13,5},{2,10},{6,14},... | collective-permute-start | bytes 196616 | tf_op jit(solution)/shard_map/ppermute | solution.py:1021
  92.3 5.1 %collective-permute-start.13 = (f32[128,128]{1,0:T(8,128)S(1)}, f32[128,128]{1,0:T(8,128)S(1)}, u32[]{:S(2)}, u32[]{:S(2)}) collective-permute-start(f32[128,128]{1,0:T(8,128)S(1)} %get-tuple-element.92), channel_id=1, source_target_pairs={{0,2},{1,3},{2,0},{3,1},{4,6},{5,7},{6,4},{7,5},{8,10},{9,11},{10,... | collective-permute-start | bytes 196616 | tf_op jit(solution)/shard_map/ppermute | solution.py:1021
  98.0 5.0 %collective-permute-start.14 = (f32[64,512]{1,0:T(8,128)S(1)}, f32[64,512]{1,0:T(8,128)S(1)}, u32[]{:S(2)}, u32[]{:S(2)}) collective-permute-start(f32[64,512]{1,0:T(8,128)S(1)} %get-tuple-element.96), channel_id=1, source_target_pairs={{0,16},{16,0},{1,17},{17,1},{2,18},{18,2},{3,19},{19,3},{4,20},{20... | collective-permute-start | bytes 393224 | tf_op jit(solution)/shard_map/ppermute | solution.py:1021

commit v6 on v5

--- a/solution.py
+++ b/solution.py
@@ -89,12 +89,17 @@
     return -0.5 * total
 
 
-def ring(one, two, axis, closed=True):
+def ring(one, two, axis, closed=True, beside=None):
     count = lax.axis_size(axis)
     near = [(i, i ^ 1) for i in range(count)]
     far = [(i, (i + 1 if i % 2 else i - 1) % count) for i in range(count)]
     if not closed:
         far = [(i, j) for i, j in far if abs(i - j) == 1]
+    if beside:
+        near, far = (
+            [(x * count + i, (1 - x) * count + j) for x in range(2) for i, j in pairs] for pairs in (near, far)
+        )
+        axis = (beside, axis)
     return lax.ppermute(one, axis, near), lax.ppermute(two, axis, far)
 
 
@@ -221,8 +226,14 @@
     put(up, down, pair, parity, (low, high), ghost, rows_inv, first, last, same)
 
 
-def pack_y_own(index, velocity, inv, rhs, up, down):
-    nx = rhs.shape[0]
+def put_rows(up, down, pair, start, lower, upper, same):
+    up[pair, pl.ds(start, REACH), :] = jnp.where(same, upper, lower)
+    down[pair, pl.ds(start, REACH), :] = jnp.where(same, lower, upper)
+
+
+def pack_y_own(index, velocity, inv, sent, rhs, up, down, *across):
+    del sent
+    nx, ny, nz = rhs.shape
     same = index[2] % 2 == 0
 
     def plane(x, carry):
@@ -233,10 +244,23 @@
 
     def planes(n, carry):
         for parity in range(2):
-            put_own(up, down, velocity, inv, rhs, 1 + 2 * n + parity, n, parity, None, same)
+            put_own(up, down, velocity, inv, rhs, 2 * n + parity, n, parity, None, same)
         return carry
 
-    lax.fori_loop(0, up.shape[0], planes, 0, unroll=3)
+    def edge_rows(x):
+        return velocity[0, x, 0:REACH, :], velocity[0, x, ny - REACH : ny, :]
+
+    if across:
+        first = index[0] == 0
+        for k in range(LAYERS):
+            x = jnp.where(first, nx - LAYERS + k, k)
+            put_own(*across, velocity, inv, rhs, x, 0, k, None, same)
+        rows = edge_rows(jnp.where(first, nx - 1, 0))
+        sign = jnp.where(first, 0.5, -0.5)
+        put_rows(*across, 0, LAYERS * EACH, sign * rows[0], sign * rows[1], same)
+    lax.fori_loop(0, nx // 2, planes, 0, unroll=4)
+    put_rows(up, down, nx // 2, 0, *edge_rows(0), same)
+    put_rows(up, down, nx // 2, REACH, *edge_rows(nx - 1), same)
 
 
 def pack_y_halo(index, velocity, inv, rhs, *refs):
@@ -281,7 +305,7 @@
     put_own(up, down, velocity, inv, rhs, nx - 1, EARLY, 0, above, same)
 
 
-def pack_z(index, velocity, inv, rhs, *refs):
+def pack_z(across, index, velocity, inv, rhs, *refs):
     (below, above), received = sides_x(index, refs[:-16]), refs[-16:-12]
     received = [*sides(index, 1, received[:2]), *sides(index, 1, received[2:])]
     same = index[4] % 2 == 0
@@ -326,15 +350,46 @@
         for x in range(wide, ref.shape[0]):
             ref[x] = jnp.zeros((rows, nz), F32)
 
+    first = index[0] == 0
+    own, far = received[:2], received[2:]
+
+    def from_pair(refs, pair, parity):
+        values = [ref[pair] for ref in refs]
+        if isinstance(parity, int):
+            return [(pltpu.roll(value, ROWS - EACH, 0) if parity else value)[0:SLOT] for value in values]
+        return [jnp.where(parity == 0, value, pltpu.roll(value, ROWS - EACH, 0))[0:SLOT] for value in values]
+
+    def extra(refs, pair, start, factor):
+        values = [ref[pair] for ref in refs]
+        size = values[0].shape[0]
+        values = [pltpu.roll(value, (size - start) % size, 0)[0:SLOT] for value in values]
+        return [jnp.where(sublanes((SLOT, nz)) < REACH, factor * value, 0.0) for value in values]
+
+    def rows_of(x):
+        if not isinstance(x, int):
+            return from_pair(own, (x - LAYERS) // 2, (x - LAYERS) % 2)
+        inside = LAYERS <= x < LAYERS + nx
+        upper = x >= LAYERS + nx - 1
+        if not across:
+            return from_pair(far, x // 2 - (wide // 2 - 2 * EARLY if upper else 0), x % 2)
+        there = jnp.where(first, 1.0, 0.0) if upper else jnp.where(first, 0.0, 1.0)
+        if inside:
+            values = from_pair(own, (x - LAYERS) // 2, (x - LAYERS) % 2)
+            rows_at = (0, pl.ds(LAYERS * EACH // SLOT * SLOT, SLOT), slice(None))
+            more = extra(far, rows_at, LAYERS * EACH % SLOT, there)
+        else:
+            k = x - LAYERS - nx if upper else x
+            values = [there * ref[0, pl.ds(k * EACH, SLOT), :] for ref in far]
+            if x == LAYERS - 1:
+                more = extra(own, nx // 2, 0, -0.5)
+            elif x == LAYERS + nx:
+                more = extra(own, nx // 2, REACH, 0.5)
+            else:
+                return values
+        return [one + two for one, two in zip(values, more)]
+
     def finish(x, ghost_low, ghost_high):
-        pair = x // 2
-        if not isinstance(x, int):
-            low, high = (ref[pair - EARLY] for ref in received[:2])
-        else:
-            pair = pair if pair < EARLY else pair - (wide // 2 - 2 * EARLY)
-            low, high = (ref[pair] for ref in received[2:])
-        low = jnp.where(x % 2 == 0, low, pltpu.roll(low, ROWS - EACH, 0))[0:SLOT]
-        high = jnp.where(x % 2 == 0, high, pltpu.roll(high, ROWS - EACH, 0))[0:SLOT]
+        low, high = rows_of(x)
         part = pltpu.roll(low, WIDE - REACH, 0)[0:WIDE]
         part = jnp.where(sublanes(edge) >= WIDE - REACH, part, 0.0)
         part = part - jnp.where(sublanes(edge) == WIDE - 1, 0.5 * ghost_low, 0.0)
@@ -1043,26 +1098,31 @@
         sems=4 * number,
     )
     near = [swap(sent[0], "gx", 1)] if count_x == 2 else list(exchange(*sent, "gx"))
-    pairs = wide // 2 - 2 * EARLY
-    shape = (pairs, ROWS, nz)
-    rhs, up, down = call(
+    across = count_x == 2
+    shape = (nx // 2 + 1, ROWS, nz)
+    corner = (1, -(-(LAYERS * EACH + REACH) // SLOT) * SLOT, nz)
+    rhs, up, down, *corners = call(
         pack_y_own,
-        [cells, shape, shape],
-        [index, velocity, inv_density],
+        [cells, shape, shape] + ([corner, corner] if across else []),
+        [index, velocity, inv_density, sent[0]],
         smem=1,
         cost=(nx * ny * nz * 10, 6 * cost_of(cells)),
+        far_in=(3,),
     )
     received = list(ring(up, down, "gy", closed=False))
-    shape = (2 * EARLY, ROWS, nz)
-    up, down = call(pack_y_halo, [shape, shape], [index, velocity, inv_density, rhs, *near], smem=1)
-    received += ring(up, down, "gy")
+    if across:
+        received += ring(*corners, "gy", beside="gx", closed=False)
+    else:
+        shape = (2 * EARLY, ROWS, nz)
+        up, down = call(pack_y_halo, [shape, shape], [index, velocity, inv_density, rhs, *near], smem=1)
+        received += ring(up, down, "gy")
     parts = nz // SPAN
     groups = -(-wide // parts)
     message = (-(-groups // 2), rows, nz)
     whole = (groups * parts, rows, nz)
     strip = (groups, rows, nz)
     rhs_wide, inv_wide, up, down, strip_rhs, strip_inv = call(
-        pack_z,
+        functools.partial(pack_z, across),
         [(wide, rows, nz)] * 2 + [message, message, strip, strip],
         [index, velocity, inv_density, rhs, *near, *received],
         scratch=[whole] * 3 + [strip] * 2,

time: 104 us -> 101 us (0.971)
  waiting for transfers between devices: 38.1 us -> 32.6 us
  starting transfers between devices: 21.4 us -> 24.2 us
    ppermute x9, waiting for transfers between devices: 26.4 us -> 23.4 us  [swap(): return lax.ppermute(value, axis, [(i, i ^ mask) for i in range(count)])]
    ppermute x6, waiting for transfers between devices: 3.68 us -> 1.25 us  [ring(): return (lax.ppermute(one, axis, near), lax.ppermute(two, axis, far))]
    all_to_all x1, starting transfers between devices: 3.96 us -> 5.93 us  [per_device(): dots = lax.all_to_all(dots, AXES, 0, 0, tiled=True)]
    pallas_call x12 -> x11, Pallas kernels: 41.2 us -> 40.2 us  [call(): pl.pallas_call(body, out_shape=[pltpu.HBM(shape, F32) if n in far_out or...]
  transfers between devices with their start and end apart: 16 -> 16, of which waited for: 10 -> 9; matrix products, arithmetic and copies ran while one was open for 1% -> 1% of each run, Pallas kernels for 14% -> 14%
where the time goes in v6:
time: 101 us
  Pallas kernels  41 us (41%)
  waiting for transfers between devices  32.6 us (32%)
  starting transfers between devices  24.2 us (24%)
  local copies, waits for them, and re-layouts  1.7 us (2%)
    pallas_call x11, Pallas kernels, call(): pl.pallas_call(body, out_shape=[pltpu.HBM(shape, F32) if n in far_out or...  40.2 us
    ppermute x9, waiting for transfers between devices, swap(): return lax.ppermute(value, axis, [(i, i ^ mask) for i in range(count)])  23.4 us
    ppermute x9, starting transfers between devices, swap(): return lax.ppermute(value, axis, [(i, i ^ mask) for i in range(count)])  9.15 us
    ppermute x6, starting transfers between devices, ring(): return (lax.ppermute(one, axis, near), lax.ppermute(two, axis, far))  9.12 us
    all_to_all x1, waiting for transfers between devices, per_device(): dots = lax.all_to_all(dots, AXES, 0, 0, tiled=True)  8.02 us
    all_to_all x1, starting transfers between devices, per_device(): dots = lax.all_to_all(dots, AXES, 0, 0, tiled=True)  5.93 us
  transfers between devices with their start and end apart: 16, of which 9 were waited for; matrix products, arithmetic and copies ran while one was open for 1% of the time, Pallas kernels for 14%

profile of v6, /device:TPU:0, one launch (start us, length us, event | category | flops | bytes accessed | tf_op | source)
XLA Modules:
  0.0 100.5 jit_solution(12810999379431766352)
XLA Ops:
  0.6 1.6 %shard_map.76.sent = f32[712,128]{1,0:T(8,128)S(1)} custom-call(s32[1]{0:T(128)} %bitcast.index, f32[3,32,64,128]{3,2,1,0:T(8,128)} %refs_9_.1, f32[32,64,128]{2,1,0:T(8,128)} %refs_10_.1), custom_call_target="tpu_custom_call" | custom-call | tf_op jit(solution)/shard_map/pallas_call | solution.py:33
  2.2 3.0 %collective-permute-start = (f32[712,128]{1,0:T(8,128)S(1)}, f32[712,128]{1,0:T(8,128)}, u32[]{:S(2)}, u32[]{:S(2)}) collective-permute-start(f32[712,128]{1,0:T(8,128)S(1)} %shard_map.76.sent), channel_id=1, source_target_pairs={{0,16},{16,0},{1,17},{17,1},{2,18},{18,2},{3,19},{19,3},{4,20},{20... | collective-permute-start | bytes 1093640 | tf_op jit(solution)/shard_map/ppermute | solution.py:1076
  5.3 1.2 %copy-done.1 = f32[32,64,128]{2,1,0:T(8,128)S(1)} copy-done((f32[32,64,128]{2,1,0:T(8,128)S(1)}, f32[32,64,128]{2,1,0:T(8,128)}, u32[]{:S(2)}) %copy-start.1) | copy-done | bytes 1048600
  6.6 2.3 %shard_map.77 = (f32[32,64,128]{2,1,0:T(8,128)S(1)}, f32[17,24,128]{2,1,0:T(8,128)S(1)}, f32[17,24,128]{2,1,0:T(8,128)S(1)}, f32[1,64,128]{2,1,0:T(8,128)S(1)}, f32[1,64,128]{2,1,0:T(8,128)S(1)}) custom-call(s32[6]{0:T(128)S(1)} %stack.34.index, f32[3,32,64,128]{3,2,1,0:T(8,128)S(1)} %copy-done, f32[32,64,128]{2,1,0:T(8,128)S(1)} %copy-done.1, ...), custom_call_target="tpu_custom_call" | custom-call | flops 2621440 | bytes 6291456 | tf_op jit(solution)/shard_map/pallas_call | solution.py:33
  8.8 1.6 %collective-permute-start.1 = (f32[17,24,128]{2,1,0:T(8,128)S(1)}, f32[17,24,128]{2,1,0:T(8,128)S(1)}, u32[]{:S(2)}, u32[]{:S(2)}) collective-permute-start(f32[17,24,128]{2,1,0:T(8,128)S(1)} %get-tuple-element.51), channel_id=1, source_target_pairs={{0,4},{4,0},{8,12},{12,8},{1,5},{5,1},{9,13},{13,9},{2,6},{6,2},{1... | collective-permute-start | bytes 626696 | tf_op jit(solution)/shard_map/ppermute | solution.py:103
  10.5 0.7 collective-permute-start.2
  11.1 4.5 %collective-permute-start.3 = (f32[1,64,128]{2,1,0:T(8,128)S(1)}, f32[1,64,128]{2,1,0:T(8,128)S(1)}, u32[]{:S(2)}, u32[]{:S(2)}) collective-permute-start(f32[1,64,128]{2,1,0:T(8,128)S(1)} %get-tuple-element.53), channel_id=1, source_target_pairs={{0,20},{4,16},{8,28},{12,24},{16,4},{20,0},{24,12},{28,8},{1,21},{... | collective-permute-start | bytes 98312 | tf_op jit(solution)/shard_map/ppermute | solution.py:103
  15.6 0.7 collective-permute-start.4
  16.3 1.2 %collective-permute-done.3.refs_3_ = f32[1,64,128]{2,1,0:T(8,128)S(1)} collective-permute-done((f32[1,64,128]{2,1,0:T(8,128)S(1)}, f32[1,64,128]{2,1,0:T(8,128)S(1)}, u32[]{:S(2)}, u32[]{:S(2)}) %collective-permute-start.3) | collective-permute-done | bytes 32800 | tf_op jit(solution)/shard_map/ppermute | solution.py:103
  17.5 7.9 %shard_map.78 = (f32[42,80,128]{2,1,0:T(8,128)}, f32[42,80,128]{2,1,0:T(8,128)}, f32[6,80,128]{2,1,0:T(8,128)}, f32[6,80,128]{2,1,0:T(8,128)S(1)}, f32[11,80,128]{2,1,0:T(8,128)}, /*index=5*/f32[11,80,128]{2,1,0:T(8,128)}) custom-call(s32[6]{0:T(128)S(1)} %stack.34.index, f32[3,32,64,128]{3,2,1,0:T(8,128)S(1)} %copy-done, f32[32,64,128]{2,1,0:T(8,128)S(1)} %copy-done.2, ...), custom_call_target="tpu_custom_call" | custom-call | tf_op jit(solution)/shard_map/pallas_call | solution.py:33
  25.6 1.6 %collective-permute-start.6 = (f32[6,80,128]{2,1,0:T(8,128)S(1)}, f32[6,80,128]{2,1,0:T(8,128)S(1)}, u32[]{:S(2)}, u32[]{:S(2)}) collective-permute-start(f32[6,80,128]{2,1,0:T(8,128)S(1)} %get-tuple-element.58), channel_id=1, source_target_pairs={{0,3},{1,2},{2,1},{3,0},{4,7},{5,6},{6,5},{7,4},{8,11},{9,10},{10,... | collective-permute-start | bytes 737288 | tf_op jit(solution)/shard_map/ppermute | solution.py:103
  27.2 11.4 %shard_map.79 = (f32[34,80,128]{2,1,0:T(8,128)}, f32[34,80,128]{2,1,0:T(8,128)}, f32[34,80,128]{2,1,0:T(8,128)}, f32[34,80,128]{2,1,0:T(8,128)}, f32[34,80,128]{2,1,0:T(8,128)}, /*index=5*/f32[11,8,128]{2,1,0:T(8,128)S(1)}) custom-call(f32[42,80,128]{2,1,0:T(8,128)} %get-tuple-element.59.rhs_far, f32[42,80,128]{2,1,0:T(8,128)} %get-tuple-element.60.inv_far), custom_call_target="tpu_custom_call" | custom-call | flops 43008000 | bytes 12042240 | tf_op jit(solution)/shard_map/pallas_call | solution.py:33
  38.6 6.1 %shard_map.80 = (f32[11,80,128]{2,1,0:T(8,128)}, f32[11,80,128]{2,1,0:T(8,128)}, f32[11,80,128]{2,1,0:T(8,128)}, f32[11,80,128]{2,1,0:T(8,128)}, f32[32,8,128]{2,1,0:T(8,128)}) custom-call(s32[6]{0:T(128)S(1)} %stack.34.index, f32[11,80,128]{2,1,0:T(8,128)} %get-tuple-element.55.rhs_far, f32[11,80,128]{2,1,0:T(8,128)} %get-tuple-element.56.inv_far, ...), custom_call_target="tpu_custom_call" | custom-call | tf_op jit(solution)/shard_map/pallas_call | solution.py:33
  44.7 5.9 %all-to-all-start = ((f32[32,8,128]{2,1,0:T(8,128)}), f32[32,8,128]{2,1,0:T(8,128)S(1)}, u32[]{:S(2)}, u32[]{:S(2)}) async-start(f32[32,8,128]{2,1,0:T(8,128)} %get-tuple-element.62), calls=%async_computation | async-start | bytes 262144 | tf_op jit(solution)/shard_map/all_to_all | solution.py:1159
  50.7 8.0 %all-to-all-done.dots = f32[32,8,128]{2,1,0:T(8,128)S(1)} async-done(((f32[32,8,128]{2,1,0:T(8,128)}), f32[32,8,128]{2,1,0:T(8,128)S(1)}, u32[]{:S(2)}, u32[]{:S(2)}) %all-to-all-start) | async-done | bytes 131104 | tf_op jit(solution)/shard_map/all_to_all | solution.py:1159
  58.7 8.4 %shard_map.81 = (f32[32,64,128]{2,1,0:T(8,128)}, f32[3,32,64,128]{3,2,1,0:T(8,128)}, f32[64,16,128]{2,1,0:T(8,128)S(1)}, f32[64,16,128]{2,1,0:T(8,128)S(1)}, f32[2,64,16,128]{3,2,1,0:T(8,128)S(1)}) custom-call(f32[32,8,128]{2,1,0:T(8,128)S(1)} %all-to-all-done.dots, bf16[128,256]{1,0:T(8,128)(2,1)S(1)} %maximum_maximum_fusion.columns, ...), custom_call_target="tpu_custom_call" | custom-call | tf_op jit(solution)/shard_map/pallas_call | solution.py:33
  67.8 0.8 shard_map.82
  68.6 1.1 %collective-permute-done.7.came = f32[2,64,16,128]{3,2,1,0:T(8,128)S(1)} collective-permute-done((f32[2,64,16,128]{3,2,1,0:T(8,128)S(1)}, f32[2,64,16,128]{3,2,1,0:T(8,128)S(1)}, u32[]{:S(2)}, u32[]{:S(2)}) %collective-permute-start.7) | collective-permute-done | bytes 1048608 | tf_op jit(solution)/shard_map/ppermute | solution.py:1076
  69.8 0.6 shard_map.83
  70.4 0.6 collective-permute-start.8
  71.0 0.9 collective-permute-start.9
  72.0 7.0 %collective-permute-done.8.p_came = f32[32,16,128]{2,1,0:T(8,128)S(1)} collective-permute-done((f32[32,16,128]{2,1,0:T(8,128)S(1)}, f32[32,16,128]{2,1,0:T(8,128)S(1)}, u32[]{:S(2)}, u32[]{:S(2)}) %collective-permute-start.8) | collective-permute-done | bytes 262176 | tf_op jit(solution)/shard_map/ppermute | solution.py:1076
  79.5 1.0 %collective-permute-start.10 = (f32[2,128,128]{2,1,0:T(8,128)S(1)}, f32[2,128,128]{2,1,0:T(8,128)S(1)}, u32[]{:S(2)}, u32[]{:S(2)}) collective-permute-start(f32[2,128,128]{2,1,0:T(8,128)S(1)} %get-tuple-element.86), channel_id=1, source_target_pairs={{0,4},{4,0},{8,12},{12,8},{1,5},{5,1},{9,13},{13,9},{2,6},{6,2},{1... | collective-permute-start | bytes 393224 | tf_op jit(solution)/shard_map/ppermute | solution.py:1076
  80.5 1.2 %collective-permute-start.11 = (f32[256,128]{1,0:T(8,128)S(1)}, f32[256,128]{1,0:T(8,128)S(1)}, u32[]{:S(2)}, u32[]{:S(2)}) collective-permute-start(f32[256,128]{1,0:T(8,128)S(1)} %get-tuple-element.88), channel_id=1, source_target_pairs={{0,8},{4,12},{8,0},{12,4},{1,9},{5,13},{9,1},{13,5},{2,10},{6,14},... | collective-permute-start | bytes 393224 | tf_op jit(solution)/shard_map/ppermute | solution.py:1076
  81.7 4.3 %collective-permute-done.10.p_came = f32[2,128,128]{2,1,0:T(8,128)S(1)} collective-permute-done((f32[2,128,128]{2,1,0:T(8,128)S(1)}, f32[2,128,128]{2,1,0:T(8,128)S(1)}, u32[]{:S(2)}, u32[]{:S(2)}) %collective-permute-start.10) | collective-permute-done | bytes 131104 | tf_op jit(solution)/shard_map/ppermute | solution.py:1076
  85.9 2.7 %collective-permute-done.11.q_came = f32[256,128]{1,0:T(8,128)S(1)} collective-permute-done((f32[256,128]{1,0:T(8,128)S(1)}, f32[256,128]{1,0:T(8,128)S(1)}, u32[]{:S(2)}, u32[]{:S(2)}) %collective-permute-start.11) | collective-permute-done | bytes 131104 | tf_op jit(solution)/shard_map/ppermute | solution.py:1076
  88.8 1.2 %collective-permute-start.13 = (f32[128,128]{1,0:T(8,128)S(1)}, f32[128,128]{1,0:T(8,128)S(1)}, u32[]{:S(2)}, u32[]{:S(2)}) collective-permute-start(f32[128,128]{1,0:T(8,128)S(1)} %get-tuple-element.92), channel_id=1, source_target_pairs={{0,2},{1,3},{2,0},{3,1},{4,6},{5,7},{6,4},{7,5},{8,10},{9,11},{10,... | collective-permute-start | bytes 196616 | tf_op jit(solution)/shard_map/ppermute | solution.py:1076
  90.0 3.9 %collective-permute-done.12.p_came = f32[128,128]{1,0:T(8,128)S(1)} collective-permute-done((f32[128,128]{1,0:T(8,128)S(1)}, f32[128,128]{1,0:T(8,128)S(1)}, u32[]{:S(2)}, u32[]{:S(2)}) %collective-permute-start.12) | collective-permute-done | bytes 65568 | tf_op jit(solution)/shard_map/ppermute | solution.py:1076
  93.9 0.7 shard_map.86
  94.5 0.8 collective-permute-start.14
  95.3 4.3 %collective-permute-done.14.came = f32[64,512]{1,0:T(8,128)S(1)} collective-permute-done((f32[64,512]{1,0:T(8,128)S(1)}, f32[64,512]{1,0:T(8,128)S(1)}, u32[]{:S(2)}, u32[]{:S(2)}) %collective-permute-start.14) | collective-permute-done | bytes 131104 | tf_op jit(solution)/shard_map/ppermute | solution.py:1076
  99.6 1.0 shard_map.87
  (39 shorter events, 1.7 us)
Async XLA Ops:
  0.6 4.7 %copy-start = (f32[3,32,64,128]{3,2,1,0:T(8,128)S(1)}, f32[3,32,64,128]{3,2,1,0:T(8,128)}, u32[]{:S(2)}) copy-start(f32[3,32,64,128]{3,2,1,0:T(8,128)} %refs_9_.1) | copy-start | bytes 9437188
  2.2 3.1 %copy-start.3 = (f32[712,128]{1,0:T(8,128)}, f32[712,128]{1,0:T(8,128)S(1)}, u32[]{:S(2)}) copy-start(f32[712,128]{1,0:T(8,128)S(1)} %shard_map.76.sent) | copy-start | bytes 1093636
  2.2 15.3 %collective-permute-start = (f32[712,128]{1,0:T(8,128)S(1)}, f32[712,128]{1,0:T(8,128)}, u32[]{:S(2)}, u32[]{:S(2)}) collective-permute-start(f32[712,128]{1,0:T(8,128)S(1)} %shard_map.76.sent), channel_id=1, source_target_pairs={{0,16},{16,0},{1,17},{17,1},{2,18},{18,2},{3,19},{19,3},{4,20},{20... | collective-permute-start | bytes 1093640 | tf_op jit(solution)/shard_map/ppermute | solution.py:1076
  5.3 1.2 %copy-start.1 = (f32[32,64,128]{2,1,0:T(8,128)S(1)}, f32[32,64,128]{2,1,0:T(8,128)}, u32[]{:S(2)}) copy-start(f32[32,64,128]{2,1,0:T(8,128)} %refs_10_.1) | copy-start | bytes 3145732
  6.6 11.0 %copy-start.2 = (f32[32,64,128]{2,1,0:T(8,128)S(1)}, f32[32,64,128]{2,1,0:T(8,128)}, u32[]{:S(2)}) copy-start(f32[32,64,128]{2,1,0:T(8,128)} %refs_10_.1) | copy-start | bytes 3145732
  8.8 8.7 %collective-permute-start.1 = (f32[17,24,128]{2,1,0:T(8,128)S(1)}, f32[17,24,128]{2,1,0:T(8,128)S(1)}, u32[]{:S(2)}, u32[]{:S(2)}) collective-permute-start(f32[17,24,128]{2,1,0:T(8,128)S(1)} %get-tuple-element.51), channel_id=1, source_target_pairs={{0,4},{4,0},{8,12},{12,8},{1,5},{5,1},{9,13},{13,9},{2,6},{6,2},{1... | collective-permute-start | bytes 626696 | tf_op jit(solution)/shard_map/ppermute | solution.py:103
  10.5 7.0 %collective-permute-start.2 = (f32[17,24,128]{2,1,0:T(8,128)S(1)}, f32[17,24,128]{2,1,0:T(8,128)S(1)}, u32[]{:S(2)}, u32[]{:S(2)}) collective-permute-start(f32[17,24,128]{2,1,0:T(8,128)S(1)} %get-tuple-element.52), channel_id=1, source_target_pairs={{4,8},{8,4},{5,9},{9,5},{6,10},{10,6},{7,11},{11,7},{20,24},{24,20... | collective-permute-start | bytes 626696 | tf_op jit(solution)/shard_map/ppermute | solution.py:103
  11.1 6.4 %collective-permute-start.3 = (f32[1,64,128]{2,1,0:T(8,128)S(1)}, f32[1,64,128]{2,1,0:T(8,128)S(1)}, u32[]{:S(2)}, u32[]{:S(2)}) collective-permute-start(f32[1,64,128]{2,1,0:T(8,128)S(1)} %get-tuple-element.53), channel_id=1, source_target_pairs={{0,20},{4,16},{8,28},{12,24},{16,4},{20,0},{24,12},{28,8},{1,21},{... | collective-permute-start | bytes 98312 | tf_op jit(solution)/shard_map/ppermute | solution.py:103
  15.6 1.9 %collective-permute-start.4 = (f32[1,64,128]{2,1,0:T(8,128)S(1)}, f32[1,64,128]{2,1,0:T(8,128)S(1)}, u32[]{:S(2)}, u32[]{:S(2)}) collective-permute-start(f32[1,64,128]{2,1,0:T(8,128)S(1)} %get-tuple-element.54), channel_id=1, source_target_pairs={{4,24},{8,20},{20,8},{24,4},{5,25},{9,21},{21,9},{25,5},{6,26},{10... | collective-permute-start | bytes 98312 | tf_op jit(solution)/shard_map/ppermute | solution.py:103
  17.5 9.7 %copy-start.4 = (f32[128,64]{0,1:T(8,128)S(1)}, f32[128,64]{0,1:T(8,128)}, u32[]{:S(2)}) copy-start(f32[128,64]{0,1:T(8,128)} %param.9) | copy-start | bytes 98308
  25.5 13.1 %collective-permute-start.5 = (f32[6,80,128]{2,1,0:T(8,128)}, f32[6,80,128]{2,1,0:T(8,128)S(1)}, u32[]{:S(2)}, u32[]{:S(2)}) collective-permute-start(f32[6,80,128]{2,1,0:T(8,128)} %get-tuple-element.57), channel_id=1, source_target_pairs={{0,1},{1,0},{2,3},{3,2},{4,5},{5,4},{6,7},{7,6},{8,9},{9,8},{10,11... | collective-permute-start | bytes 737288 | tf_op jit(solution)/shard_map/ppermute | solution.py:103
  25.6 13.0 %collective-permute-start.6 = (f32[6,80,128]{2,1,0:T(8,128)S(1)}, f32[6,80,128]{2,1,0:T(8,128)S(1)}, u32[]{:S(2)}, u32[]{:S(2)}) collective-permute-start(f32[6,80,128]{2,1,0:T(8,128)S(1)} %get-tuple-element.58), channel_id=1, source_target_pairs={{0,3},{1,2},{2,1},{3,0},{4,7},{5,6},{6,5},{7,4},{8,11},{9,10},{10,... | collective-permute-start | bytes 737288 | tf_op jit(solution)/shard_map/ppermute | solution.py:103
  44.7 14.0 %all-to-all-start = ((f32[32,8,128]{2,1,0:T(8,128)}), f32[32,8,128]{2,1,0:T(8,128)S(1)}, u32[]{:S(2)}, u32[]{:S(2)}) async-start(f32[32,8,128]{2,1,0:T(8,128)} %get-tuple-element.62), calls=%async_computation | async-start | bytes 262144 | tf_op jit(solution)/shard_map/all_to_all | solution.py:1159
  58.7 8.7 %copy-start.5 = (f32[64,64]{1,0:T(8,128)S(1)}, f32[64,64]{1,0:T(8,128)}, u32[]{:S(2)}) copy-start(f32[64,64]{1,0:T(8,128)} %param.8) | copy-start | bytes 49156
  58.7 8.9 %copy-start.6 = (f32[32,64]{1,0:T(8,128)S(1)}, f32[32,64]{1,0:T(8,128)}, u32[]{:S(2)}) copy-start(f32[32,64]{1,0:T(8,128)} %param.7) | copy-start | bytes 24580
  67.1 2.7 %collective-permute-start.7 = (f32[2,64,16,128]{3,2,1,0:T(8,128)S(1)}, f32[2,64,16,128]{3,2,1,0:T(8,128)S(1)}, u32[]{:S(2)}, u32[]{:S(2)}) collective-permute-start(f32[2,64,16,128]{3,2,1,0:T(8,128)S(1)} %get-tuple-element.76), channel_id=1, source_target_pairs={{0,1},{1,0},{2,3},{3,2},{4,5},{5,4},{6,7},{7,6},{8,9},{9,8},{10,11... | collective-permute-start | bytes 3145736 | tf_op jit(solution)/shard_map/ppermute | solution.py:1076
  70.4 8.5 %collective-permute-start.8 = (f32[32,16,128]{2,1,0:T(8,128)S(1)}, f32[32,16,128]{2,1,0:T(8,128)S(1)}, u32[]{:S(2)}, u32[]{:S(2)}) collective-permute-start(f32[32,16,128]{2,1,0:T(8,128)S(1)} %get-tuple-element.80), channel_id=1, source_target_pairs={{0,2},{1,3},{2,0},{3,1},{4,6},{5,7},{6,4},{7,5},{8,10},{9,11},{10,... | collective-permute-start | bytes 786440 | tf_op jit(solution)/shard_map/ppermute | solution.py:1076
  71.0 8.1 %collective-permute-start.9 = (f32[2,256,128]{2,1,0:T(8,128)S(1)}, f32[2,256,128]{2,1,0:T(8,128)S(1)}, u32[]{:S(2)}, u32[]{:S(2)}) collective-permute-start(f32[2,256,128]{2,1,0:T(8,128)S(1)} %get-tuple-element.83), channel_id=1, source_target_pairs={{0,4},{4,0},{8,12},{12,8},{1,5},{5,1},{9,13},{13,9},{2,6},{6,2},{1... | collective-permute-start | bytes 786440 | tf_op jit(solution)/shard_map/ppermute | solution.py:1076
  79.5 6.5 %collective-permute-start.10 = (f32[2,128,128]{2,1,0:T(8,128)S(1)}, f32[2,128,128]{2,1,0:T(8,128)S(1)}, u32[]{:S(2)}, u32[]{:S(2)}) collective-permute-start(f32[2,128,128]{2,1,0:T(8,128)S(1)} %get-tuple-element.86), channel_id=1, source_target_pairs={{0,4},{4,0},{8,12},{12,8},{1,5},{5,1},{9,13},{13,9},{2,6},{6,2},{1... | collective-permute-start | bytes 393224 | tf_op jit(solution)/shard_map/ppermute | solution.py:1076
  80.5 8.1 %collective-permute-start.11 = (f32[256,128]{1,0:T(8,128)S(1)}, f32[256,128]{1,0:T(8,128)S(1)}, u32[]{:S(2)}, u32[]{:S(2)}) collective-permute-start(f32[256,128]{1,0:T(8,128)S(1)} %get-tuple-element.88), channel_id=1, source_target_pairs={{0,8},{4,12},{8,0},{12,4},{1,9},{5,13},{9,1},{13,5},{2,10},{6,14},... | collective-permute-start | bytes 393224 | tf_op jit(solution)/shard_map/ppermute | solution.py:1076
  88.6 5.2 %collective-permute-start.12 = (f32[128,128]{1,0:T(8,128)S(1)}, f32[128,128]{1,0:T(8,128)S(1)}, u32[]{:S(2)}, u32[]{:S(2)}) collective-permute-start(f32[128,128]{1,0:T(8,128)S(1)} %get-tuple-element.90), channel_id=1, source_target_pairs={{0,8},{4,12},{8,0},{12,4},{1,9},{5,13},{9,1},{13,5},{2,10},{6,14},... | collective-permute-start | bytes 196616 | tf_op jit(solution)/shard_map/ppermute | solution.py:1076
  88.8 5.1 %collective-permute-start.13 = (f32[128,128]{1,0:T(8,128)S(1)}, f32[128,128]{1,0:T(8,128)S(1)}, u32[]{:S(2)}, u32[]{:S(2)}) collective-permute-start(f32[128,128]{1,0:T(8,128)S(1)} %get-tuple-element.92), channel_id=1, source_target_pairs={{0,2},{1,3},{2,0},{3,1},{4,6},{5,7},{6,4},{7,5},{8,10},{9,11},{10,... | collective-permute-start | bytes 196616 | tf_op jit(solution)/shard_map/ppermute | solution.py:1076
  94.5 5.0 %collective-permute-start.14 = (f32[64,512]{1,0:T(8,128)S(1)}, f32[64,512]{1,0:T(8,128)S(1)}, u32[]{:S(2)}, u32[]{:S(2)}) collective-permute-start(f32[64,512]{1,0:T(8,128)S(1)} %get-tuple-element.96), channel_id=1, source_target_pairs={{0,16},{16,0},{1,17},{17,1},{2,18},{18,2},{3,19},{19,3},{4,20},{20... | collective-permute-start | bytes 393224 | tf_op jit(solution)/shard_map/ppermute | solution.py:1076

commit v7 on v6

--- a/solution.py
+++ b/solution.py
@@ -138,8 +138,11 @@
             plane_z = near[2, start + k]
             ends = jnp.where(lanes(shape) == 2 * k, plane_z[:, 0:1], ends)
             ends = jnp.where(lanes(shape) == 2 * k + 1, plane_z[:, nz - 1 : nz], ends)
-        message[base : base + ny, :] = ends
-        base += ny
+        ends = jnp.transpose(ends)[0 : 2 * REACH]
+        message[base : base + 2 * REACH, :] = jnp.concatenate(
+            [ends, jnp.zeros((2 * REACH, nz - ny), F32)], axis=1
+        )
+        base += 2 * REACH
         for k in range(REACH):
             message[base + 2 * k : base + 2 * k + 1, :] = near[1, start + k, 0:1, :]
             message[base + 2 * k + 1 : base + 2 * k + 2, :] = near[1, start + k, ny - 1 : ny, :]
@@ -154,6 +157,11 @@
     else:
         fill(0, *upper)
         fill(1, *lower)
+
+
+def column_ends(message, ny, nz):
+    rows = message[pl.ds((REACH + 1 + LAYERS) * ny, 2 * REACH), :]
+    return jnp.transpose(jnp.concatenate([rows, jnp.zeros((nz - 2 * REACH, nz), F32)], axis=0))[0:ny]
 
 
 class Scaled:
@@ -284,10 +292,10 @@
             sign, source = extra
             low = low + sign * velocity[0, source, 0:REACH, :]
             high = high + sign * velocity[0, source, ny - REACH : ny, :]
-        ends = (REACH + 1 + LAYERS) * ny
-        lines = ends + ny + 2 * k_rhs
+        lines = (REACH + 1 + LAYERS) * ny + 2 * REACH + 2 * k_rhs
         ghost = (message[pl.ds(lines, 1), :], message[pl.ds(lines + 1, 1), :])
-        head, tail = message[pl.ds(ends, REACH), :], message[pl.ds(ends + ny - REACH, REACH), :]
+        ends = column_ends(message, ny, nz)
+        head, tail = ends[0:REACH], ends[ny - REACH : ny]
         first = (head[:, 2 * k_rhs : 2 * k_rhs + 1], tail[:, 2 * k_rhs : 2 * k_rhs + 1])
         last = (head[:, 2 * k_rhs + 1 : 2 * k_rhs + 2], tail[:, 2 * k_rhs + 1 : 2 * k_rhs + 2])
         put(up, down, pair, x % 2, (low, high), ghost, rows_inv, first, last, same)
@@ -318,8 +326,12 @@
     edge = (WIDE, nz)
     groups = strip_rhs.shape[0]
 
+    columns = [column_ends(message, ny, nz) for message in (below, above)]
     for k in range(LAYERS):
-        for message, x, layer in ((below, k, k - 1), (above, nx + LAYERS + k, k if k < REACH else -1)):
+        for message, line, x, layer in (
+            (below, columns[0], k, k - 1),
+            (above, columns[1], nx + LAYERS + k, k if k < REACH else -1),
+        ):
             base = (REACH + 1 + k) * ny
             inv_wide[x, mine, :] = message[pl.ds(base, ny), :]
             if layer < 0:
@@ -332,7 +344,6 @@
             if x == nx + LAYERS:
                 part = part + 0.5 * velocity[0, nx - 1]
             rhs_wide[x, mine, :] = part
-            line = message[pl.ds((REACH + 1 + LAYERS) * ny, ny), :]
             ends[x, mine, :] = jnp.where(
                 lanes((ny, nz)) == 0, line[:, 2 * layer : 2 * layer + 1], line[:, 2 * layer + 1 : 2 * layer + 2]
             )
@@ -419,7 +430,7 @@
 
     for k in range(LAYERS):
         for message, x, layer in ((below, k, k - 1), (above, nx + LAYERS + k, k if k < REACH else -1)):
-            lines = (REACH + 1 + LAYERS + 1) * ny + 2 * layer
+            lines = (REACH + 1 + LAYERS) * ny + 2 * REACH + 2 * layer
             if layer < 0:
                 zero = jnp.zeros((1, nz), F32)
                 finish(x, zero, zero)
@@ -430,7 +441,7 @@
         finish(x + LAYERS, velocity[1, x, 0:1, :], velocity[1, x, ny - 1 : ny, :])
         return carry
 
-    lax.fori_loop(1, nx - 1, middle, 0, unroll=10)
+    lax.fori_loop(1, nx - 1, middle, 0, unroll=30)
     for x in (0, nx - 1):
         finish(x + LAYERS, velocity[1, x, 0:1, :], velocity[1, x, ny - 1 : ny, :])
     copies = [
@@ -479,7 +490,7 @@
         down[n] = jnp.where(same, two, one)
         return carry
 
-    lax.fori_loop(0, halves, both, 0, unroll=2)
+    lax.fori_loop(0, halves, both, 0, unroll=3)
 
     def more(n, carry):
         one, two = pack(n + halves)
@@ -487,7 +498,7 @@
         down[n] += pltpu.roll(jnp.where(same, two, one), SPAN // 2, 1)
         return carry
 
-    lax.fori_loop(0, groups - halves, more, 0, unroll=2)
+    lax.fori_loop(0, groups - halves, more, 0, unroll=5)
     for ref, far in ((strip_rhs, strip_rhs_far), (strip_inv, strip_inv_far)):
         copies.append(pltpu.make_async_copy(ref, far, sems.at[len(copies)]))
         copies[-1].start()
@@ -506,7 +517,7 @@
 
 
 class Stencil:
-    def __init__(self, inv, root, ax, ay, az, vs, planes, edges=None, unroll=6):
+    def __init__(self, inv, root, ax, ay, az, vs, planes, edges=None, unroll=10):
         self.inv, self.root, self.ax, self.ay, self.az, self.vs = inv, root, ax, ay, az, vs
         self.planes, self.edges, self.unroll = planes, edges or (lambda ref: None), unroll
         self.count, self.rows, self.nz = inv.shape
@@ -1086,7 +1097,7 @@
     index_x = lax.axis_index("gx").reshape(1)
     index = jnp.stack([jnp.int32(f(axis)) for axis in AXES for f in (lax.axis_index, lax.axis_size)])
 
-    shape = (((REACH + 1 + LAYERS + 1) * ny + 2 * REACH), nz)
+    shape = ((REACH + 1 + LAYERS) * ny + 4 * REACH, nz)
     number = 1 if count_x == 2 else 2
     sent = call(
         pack_x,

time: 101 us -> 99.5 us (0.985)
  Pallas kernels: 41 us -> 39.7 us
    pallas_call x11, Pallas kernels: 40.2 us -> 38.9 us  [call(): pl.pallas_call(body, out_shape=[pltpu.HBM(shape, F32) if n in far_out or...]
where the time goes in v7:
time: 99.5 us; the launch traced here: 99.3 us
  Pallas kernels  39.7 us (40%)
  waiting for transfers between devices  32.8 us (33%)
  starting transfers between devices  24.1 us (24%)
  local copies, waits for them, and re-layouts  1.7 us (2%)
    pallas_call x11, Pallas kernels, call(): pl.pallas_call(body, out_shape=[pltpu.HBM(shape, F32) if n in far_out or...  38.9 us
    ppermute x9, waiting for transfers between devices, swap(): return lax.ppermute(value, axis, [(i, i ^ mask) for i in range(count)])  23.5 us
    ppermute x6, starting transfers between devices, ring(): return (lax.ppermute(one, axis, near), lax.ppermute(two, axis, far))  9.11 us
    ppermute x9, starting transfers between devices, swap(): return lax.ppermute(value, axis, [(i, i ^ mask) for i in range(count)])  9.06 us
    all_to_all x1, waiting for transfers between devices, per_device(): dots = lax.all_to_all(dots, AXES, 0, 0, tiled=True)  8.02 us
    all_to_all x1, starting transfers between devices, per_device(): dots = lax.all_to_all(dots, AXES, 0, 0, tiled=True)  5.94 us
  transfers between devices with their start and end apart: 16, of which 9 were waited for; matrix products, arithmetic and copies ran while one was open for 1% of the time, Pallas kernels for 14%

profile of v7, /device:TPU:0, one launch (start us, length us, event | category | flops | bytes accessed | tf_op | source)
XLA Modules:
  0.0 99.3 jit_solution(14075320444445094900)
XLA Ops:
  0.6 1.6 %shard_map.76.sent = f32[656,128]{1,0:T(8,128)S(1)} custom-call(s32[1]{0:T(128)} %bitcast.index, f32[3,32,64,128]{3,2,1,0:T(8,128)} %refs_9_.1, f32[32,64,128]{2,1,0:T(8,128)} %refs_10_.1), custom_call_target="tpu_custom_call" | custom-call | tf_op jit(solution)/shard_map/pallas_call | solution.py:33
  2.3 3.0 %collective-permute-start = (f32[656,128]{1,0:T(8,128)S(1)}, f32[656,128]{1,0:T(8,128)}, u32[]{:S(2)}, u32[]{:S(2)}) collective-permute-start(f32[656,128]{1,0:T(8,128)S(1)} %shard_map.76.sent), channel_id=1, source_target_pairs={{0,16},{16,0},{1,17},{17,1},{2,18},{18,2},{3,19},{19,3},{4,20},{20... | collective-permute-start | bytes 1007624 | tf_op jit(solution)/shard_map/ppermute | solution.py:1087
  5.4 1.2 %copy-done.1 = f32[32,64,128]{2,1,0:T(8,128)S(1)} copy-done((f32[32,64,128]{2,1,0:T(8,128)S(1)}, f32[32,64,128]{2,1,0:T(8,128)}, u32[]{:S(2)}) %copy-start.1) | copy-done | bytes 1048600
  6.6 2.3 %shard_map.77 = (f32[32,64,128]{2,1,0:T(8,128)S(1)}, f32[17,24,128]{2,1,0:T(8,128)S(1)}, f32[17,24,128]{2,1,0:T(8,128)S(1)}, f32[1,64,128]{2,1,0:T(8,128)S(1)}, f32[1,64,128]{2,1,0:T(8,128)S(1)}) custom-call(s32[6]{0:T(128)S(1)} %stack.34.index, f32[3,32,64,128]{3,2,1,0:T(8,128)S(1)} %copy-done, f32[32,64,128]{2,1,0:T(8,128)S(1)} %copy-done.1, ...), custom_call_target="tpu_custom_call" | custom-call | flops 2621440 | bytes 6291456 | tf_op jit(solution)/shard_map/pallas_call | solution.py:33
  8.9 1.6 %collective-permute-start.1 = (f32[17,24,128]{2,1,0:T(8,128)S(1)}, f32[17,24,128]{2,1,0:T(8,128)S(1)}, u32[]{:S(2)}, u32[]{:S(2)}) collective-permute-start(f32[17,24,128]{2,1,0:T(8,128)S(1)} %get-tuple-element.51), channel_id=1, source_target_pairs={{0,4},{4,0},{8,12},{12,8},{1,5},{5,1},{9,13},{13,9},{2,6},{6,2},{1... | collective-permute-start | bytes 626696 | tf_op jit(solution)/shard_map/ppermute | solution.py:103
  10.5 0.7 collective-permute-start.2
  11.2 4.5 %collective-permute-start.3 = (f32[1,64,128]{2,1,0:T(8,128)S(1)}, f32[1,64,128]{2,1,0:T(8,128)S(1)}, u32[]{:S(2)}, u32[]{:S(2)}) collective-permute-start(f32[1,64,128]{2,1,0:T(8,128)S(1)} %get-tuple-element.53), channel_id=1, source_target_pairs={{0,20},{4,16},{8,28},{12,24},{16,4},{20,0},{24,12},{28,8},{1,21},{... | collective-permute-start | bytes 98312 | tf_op jit(solution)/shard_map/ppermute | solution.py:103
  15.7 0.7 collective-permute-start.4
  16.3 1.2 %collective-permute-done.3.refs_3_ = f32[1,64,128]{2,1,0:T(8,128)S(1)} collective-permute-done((f32[1,64,128]{2,1,0:T(8,128)S(1)}, f32[1,64,128]{2,1,0:T(8,128)S(1)}, u32[]{:S(2)}, u32[]{:S(2)}) %collective-permute-start.3) | collective-permute-done | bytes 32800 | tf_op jit(solution)/shard_map/ppermute | solution.py:103
  17.6 7.4 %shard_map.78 = (f32[42,80,128]{2,1,0:T(8,128)}, f32[42,80,128]{2,1,0:T(8,128)}, f32[6,80,128]{2,1,0:T(8,128)}, f32[6,80,128]{2,1,0:T(8,128)S(1)}, f32[11,80,128]{2,1,0:T(8,128)}, /*index=5*/f32[11,80,128]{2,1,0:T(8,128)}) custom-call(s32[6]{0:T(128)S(1)} %stack.34.index, f32[3,32,64,128]{3,2,1,0:T(8,128)S(1)} %copy-done, f32[32,64,128]{2,1,0:T(8,128)S(1)} %copy-done.2, ...), custom_call_target="tpu_custom_call" | custom-call | tf_op jit(solution)/shard_map/pallas_call | solution.py:33
  25.1 1.6 %collective-permute-start.6 = (f32[6,80,128]{2,1,0:T(8,128)S(1)}, f32[6,80,128]{2,1,0:T(8,128)S(1)}, u32[]{:S(2)}, u32[]{:S(2)}) collective-permute-start(f32[6,80,128]{2,1,0:T(8,128)S(1)} %get-tuple-element.58), channel_id=1, source_target_pairs={{0,3},{1,2},{2,1},{3,0},{4,7},{5,6},{6,5},{7,4},{8,11},{9,10},{10,... | collective-permute-start | bytes 737288 | tf_op jit(solution)/shard_map/ppermute | solution.py:103
  26.7 10.5 %shard_map.79 = (f32[34,80,128]{2,1,0:T(8,128)}, f32[34,80,128]{2,1,0:T(8,128)}, f32[34,80,128]{2,1,0:T(8,128)}, f32[34,80,128]{2,1,0:T(8,128)}, f32[34,80,128]{2,1,0:T(8,128)}, /*index=5*/f32[11,8,128]{2,1,0:T(8,128)S(1)}) custom-call(f32[42,80,128]{2,1,0:T(8,128)} %get-tuple-element.59.rhs_far, f32[42,80,128]{2,1,0:T(8,128)} %get-tuple-element.60.inv_far), custom_call_target="tpu_custom_call" | custom-call | flops 43008000 | bytes 12042240 | tf_op jit(solution)/shard_map/pallas_call | solution.py:33
  37.3 6.1 %shard_map.80 = (f32[11,80,128]{2,1,0:T(8,128)}, f32[11,80,128]{2,1,0:T(8,128)}, f32[11,80,128]{2,1,0:T(8,128)}, f32[11,80,128]{2,1,0:T(8,128)}, f32[32,8,128]{2,1,0:T(8,128)}) custom-call(s32[6]{0:T(128)S(1)} %stack.34.index, f32[11,80,128]{2,1,0:T(8,128)} %get-tuple-element.55.rhs_far, f32[11,80,128]{2,1,0:T(8,128)} %get-tuple-element.56.inv_far, ...), custom_call_target="tpu_custom_call" | custom-call | tf_op jit(solution)/shard_map/pallas_call | solution.py:33
  43.4 5.9 %all-to-all-start = ((f32[32,8,128]{2,1,0:T(8,128)}), f32[32,8,128]{2,1,0:T(8,128)S(1)}, u32[]{:S(2)}, u32[]{:S(2)}) async-start(f32[32,8,128]{2,1,0:T(8,128)} %get-tuple-element.62), calls=%async_computation | async-start | bytes 262144 | tf_op jit(solution)/shard_map/all_to_all | solution.py:1170
  49.4 8.0 %all-to-all-done.dots = f32[32,8,128]{2,1,0:T(8,128)S(1)} async-done(((f32[32,8,128]{2,1,0:T(8,128)}), f32[32,8,128]{2,1,0:T(8,128)S(1)}, u32[]{:S(2)}, u32[]{:S(2)}) %all-to-all-start) | async-done | bytes 131104 | tf_op jit(solution)/shard_map/all_to_all | solution.py:1170
  57.4 8.4 %shard_map.81 = (f32[32,64,128]{2,1,0:T(8,128)}, f32[3,32,64,128]{3,2,1,0:T(8,128)}, f32[64,16,128]{2,1,0:T(8,128)S(1)}, f32[64,16,128]{2,1,0:T(8,128)S(1)}, f32[2,64,16,128]{3,2,1,0:T(8,128)S(1)}) custom-call(f32[32,8,128]{2,1,0:T(8,128)S(1)} %all-to-all-done.dots, bf16[128,256]{1,0:T(8,128)(2,1)S(1)} %maximum_maximum_fusion.columns, ...), custom_call_target="tpu_custom_call" | custom-call | tf_op jit(solution)/shard_map/pallas_call | solution.py:33
  66.6 0.8 shard_map.82
  67.3 1.1 %collective-permute-done.7.came = f32[2,64,16,128]{3,2,1,0:T(8,128)S(1)} collective-permute-done((f32[2,64,16,128]{3,2,1,0:T(8,128)S(1)}, f32[2,64,16,128]{3,2,1,0:T(8,128)S(1)}, u32[]{:S(2)}, u32[]{:S(2)}) %collective-permute-start.7) | collective-permute-done | bytes 1048608 | tf_op jit(solution)/shard_map/ppermute | solution.py:1087
  68.5 0.6 shard_map.83
  69.1 0.6 collective-permute-start.8
  69.7 0.9 collective-permute-start.9
  70.6 7.0 %collective-permute-done.8.p_came = f32[32,16,128]{2,1,0:T(8,128)S(1)} collective-permute-done((f32[32,16,128]{2,1,0:T(8,128)S(1)}, f32[32,16,128]{2,1,0:T(8,128)S(1)}, u32[]{:S(2)}, u32[]{:S(2)}) %collective-permute-start.8) | collective-permute-done | bytes 262176 | tf_op jit(solution)/shard_map/ppermute | solution.py:1087
  78.2 1.0 %collective-permute-start.10 = (f32[2,128,128]{2,1,0:T(8,128)S(1)}, f32[2,128,128]{2,1,0:T(8,128)S(1)}, u32[]{:S(2)}, u32[]{:S(2)}) collective-permute-start(f32[2,128,128]{2,1,0:T(8,128)S(1)} %get-tuple-element.86), channel_id=1, source_target_pairs={{0,4},{4,0},{8,12},{12,8},{1,5},{5,1},{9,13},{13,9},{2,6},{6,2},{1... | collective-permute-start | bytes 393224 | tf_op jit(solution)/shard_map/ppermute | solution.py:1087
  79.2 1.2 %collective-permute-start.11 = (f32[256,128]{1,0:T(8,128)S(1)}, f32[256,128]{1,0:T(8,128)S(1)}, u32[]{:S(2)}, u32[]{:S(2)}) collective-permute-start(f32[256,128]{1,0:T(8,128)S(1)} %get-tuple-element.88), channel_id=1, source_target_pairs={{0,8},{4,12},{8,0},{12,4},{1,9},{5,13},{9,1},{13,5},{2,10},{6,14},... | collective-permute-start | bytes 393224 | tf_op jit(solution)/shard_map/ppermute | solution.py:1087
  80.3 4.3 %collective-permute-done.10.p_came = f32[2,128,128]{2,1,0:T(8,128)S(1)} collective-permute-done((f32[2,128,128]{2,1,0:T(8,128)S(1)}, f32[2,128,128]{2,1,0:T(8,128)S(1)}, u32[]{:S(2)}, u32[]{:S(2)}) %collective-permute-start.10) | collective-permute-done | bytes 131104 | tf_op jit(solution)/shard_map/ppermute | solution.py:1087
  84.7 2.7 %collective-permute-done.11.q_came = f32[256,128]{1,0:T(8,128)S(1)} collective-permute-done((f32[256,128]{1,0:T(8,128)S(1)}, f32[256,128]{1,0:T(8,128)S(1)}, u32[]{:S(2)}, u32[]{:S(2)}) %collective-permute-start.11) | collective-permute-done | bytes 131104 | tf_op jit(solution)/shard_map/ppermute | solution.py:1087
  87.5 1.2 %collective-permute-start.13 = (f32[128,128]{1,0:T(8,128)S(1)}, f32[128,128]{1,0:T(8,128)S(1)}, u32[]{:S(2)}, u32[]{:S(2)}) collective-permute-start(f32[128,128]{1,0:T(8,128)S(1)} %get-tuple-element.92), channel_id=1, source_target_pairs={{0,2},{1,3},{2,0},{3,1},{4,6},{5,7},{6,4},{7,5},{8,10},{9,11},{10,... | collective-permute-start | bytes 196616 | tf_op jit(solution)/shard_map/ppermute | solution.py:1087
  88.7 3.9 %collective-permute-done.12.p_came = f32[128,128]{1,0:T(8,128)S(1)} collective-permute-done((f32[128,128]{1,0:T(8,128)S(1)}, f32[128,128]{1,0:T(8,128)S(1)}, u32[]{:S(2)}, u32[]{:S(2)}) %collective-permute-start.12) | collective-permute-done | bytes 65568 | tf_op jit(solution)/shard_map/ppermute | solution.py:1087
  92.6 0.7 shard_map.86
  93.3 0.7 collective-permute-start.14
  93.9 4.4 %collective-permute-done.14.came = f32[64,512]{1,0:T(8,128)S(1)} collective-permute-done((f32[64,512]{1,0:T(8,128)S(1)}, f32[64,512]{1,0:T(8,128)S(1)}, u32[]{:S(2)}, u32[]{:S(2)}) %collective-permute-start.14) | collective-permute-done | bytes 131104 | tf_op jit(solution)/shard_map/ppermute | solution.py:1087
  98.3 1.0 shard_map.87
  (39 shorter events, 1.6 us)
Async XLA Ops:
  0.6 4.8 %copy-start = (f32[3,32,64,128]{3,2,1,0:T(8,128)S(1)}, f32[3,32,64,128]{3,2,1,0:T(8,128)}, u32[]{:S(2)}) copy-start(f32[3,32,64,128]{3,2,1,0:T(8,128)} %refs_9_.1) | copy-start | bytes 9437188
  2.3 3.1 %copy-start.3 = (f32[656,128]{1,0:T(8,128)}, f32[656,128]{1,0:T(8,128)S(1)}, u32[]{:S(2)}) copy-start(f32[656,128]{1,0:T(8,128)S(1)} %shard_map.76.sent) | copy-start | bytes 1007620
  2.3 15.3 %collective-permute-start = (f32[656,128]{1,0:T(8,128)S(1)}, f32[656,128]{1,0:T(8,128)}, u32[]{:S(2)}, u32[]{:S(2)}) collective-permute-start(f32[656,128]{1,0:T(8,128)S(1)} %shard_map.76.sent), channel_id=1, source_target_pairs={{0,16},{16,0},{1,17},{17,1},{2,18},{18,2},{3,19},{19,3},{4,20},{20... | collective-permute-start | bytes 1007624 | tf_op jit(solution)/shard_map/ppermute | solution.py:1087
  5.4 1.2 %copy-start.1 = (f32[32,64,128]{2,1,0:T(8,128)S(1)}, f32[32,64,128]{2,1,0:T(8,128)}, u32[]{:S(2)}) copy-start(f32[32,64,128]{2,1,0:T(8,128)} %refs_10_.1) | copy-start | bytes 3145732
  6.6 11.0 %copy-start.2 = (f32[32,64,128]{2,1,0:T(8,128)S(1)}, f32[32,64,128]{2,1,0:T(8,128)}, u32[]{:S(2)}) copy-start(f32[32,64,128]{2,1,0:T(8,128)} %refs_10_.1) | copy-start | bytes 3145732
  8.9 8.7 %collective-permute-start.1 = (f32[17,24,128]{2,1,0:T(8,128)S(1)}, f32[17,24,128]{2,1,0:T(8,128)S(1)}, u32[]{:S(2)}, u32[]{:S(2)}) collective-permute-start(f32[17,24,128]{2,1,0:T(8,128)S(1)} %get-tuple-element.51), channel_id=1, source_target_pairs={{0,4},{4,0},{8,12},{12,8},{1,5},{5,1},{9,13},{13,9},{2,6},{6,2},{1... | collective-permute-start | bytes 626696 | tf_op jit(solution)/shard_map/ppermute | solution.py:103
  10.5 7.0 %collective-permute-start.2 = (f32[17,24,128]{2,1,0:T(8,128)S(1)}, f32[17,24,128]{2,1,0:T(8,128)S(1)}, u32[]{:S(2)}, u32[]{:S(2)}) collective-permute-start(f32[17,24,128]{2,1,0:T(8,128)S(1)} %get-tuple-element.52), channel_id=1, source_target_pairs={{4,8},{8,4},{5,9},{9,5},{6,10},{10,6},{7,11},{11,7},{20,24},{24,20... | collective-permute-start | bytes 626696 | tf_op jit(solution)/shard_map/ppermute | solution.py:103
  11.2 6.3 %collective-permute-start.3 = (f32[1,64,128]{2,1,0:T(8,128)S(1)}, f32[1,64,128]{2,1,0:T(8,128)S(1)}, u32[]{:S(2)}, u32[]{:S(2)}) collective-permute-start(f32[1,64,128]{2,1,0:T(8,128)S(1)} %get-tuple-element.53), channel_id=1, source_target_pairs={{0,20},{4,16},{8,28},{12,24},{16,4},{20,0},{24,12},{28,8},{1,21},{... | collective-permute-start | bytes 98312 | tf_op jit(solution)/shard_map/ppermute | solution.py:103
  15.7 1.9 %collective-permute-start.4 = (f32[1,64,128]{2,1,0:T(8,128)S(1)}, f32[1,64,128]{2,1,0:T(8,128)S(1)}, u32[]{:S(2)}, u32[]{:S(2)}) collective-permute-start(f32[1,64,128]{2,1,0:T(8,128)S(1)} %get-tuple-element.54), channel_id=1, source_target_pairs={{4,24},{8,20},{20,8},{24,4},{5,25},{9,21},{21,9},{25,5},{6,26},{10... | collective-permute-start | bytes 98312 | tf_op jit(solution)/shard_map/ppermute | solution.py:103
  17.6 9.2 %copy-start.4 = (f32[128,64]{0,1:T(8,128)S(1)}, f32[128,64]{0,1:T(8,128)}, u32[]{:S(2)}) copy-start(f32[128,64]{0,1:T(8,128)} %param.9) | copy-start | bytes 98308
  25.0 12.3 %collective-permute-start.5 = (f32[6,80,128]{2,1,0:T(8,128)}, f32[6,80,128]{2,1,0:T(8,128)S(1)}, u32[]{:S(2)}, u32[]{:S(2)}) collective-permute-start(f32[6,80,128]{2,1,0:T(8,128)} %get-tuple-element.57), channel_id=1, source_target_pairs={{0,1},{1,0},{2,3},{3,2},{4,5},{5,4},{6,7},{7,6},{8,9},{9,8},{10,11... | collective-permute-start | bytes 737288 | tf_op jit(solution)/shard_map/ppermute | solution.py:103
  25.1 12.2 %collective-permute-start.6 = (f32[6,80,128]{2,1,0:T(8,128)S(1)}, f32[6,80,128]{2,1,0:T(8,128)S(1)}, u32[]{:S(2)}, u32[]{:S(2)}) collective-permute-start(f32[6,80,128]{2,1,0:T(8,128)S(1)} %get-tuple-element.58), channel_id=1, source_target_pairs={{0,3},{1,2},{2,1},{3,0},{4,7},{5,6},{6,5},{7,4},{8,11},{9,10},{10,... | collective-permute-start | bytes 737288 | tf_op jit(solution)/shard_map/ppermute | solution.py:103
  43.4 14.0 %all-to-all-start = ((f32[32,8,128]{2,1,0:T(8,128)}), f32[32,8,128]{2,1,0:T(8,128)S(1)}, u32[]{:S(2)}, u32[]{:S(2)}) async-start(f32[32,8,128]{2,1,0:T(8,128)} %get-tuple-element.62), calls=%async_computation | async-start | bytes 262144 | tf_op jit(solution)/shard_map/all_to_all | solution.py:1170
  57.4 8.7 %copy-start.5 = (f32[64,64]{1,0:T(8,128)S(1)}, f32[64,64]{1,0:T(8,128)}, u32[]{:S(2)}) copy-start(f32[64,64]{1,0:T(8,128)} %param.8) | copy-start | bytes 49156
  57.4 8.9 %copy-start.6 = (f32[32,64]{1,0:T(8,128)S(1)}, f32[32,64]{1,0:T(8,128)}, u32[]{:S(2)}) copy-start(f32[32,64]{1,0:T(8,128)} %param.7) | copy-start | bytes 24580
  65.8 2.7 %collective-permute-start.7 = (f32[2,64,16,128]{3,2,1,0:T(8,128)S(1)}, f32[2,64,16,128]{3,2,1,0:T(8,128)S(1)}, u32[]{:S(2)}, u32[]{:S(2)}) collective-permute-start(f32[2,64,16,128]{3,2,1,0:T(8,128)S(1)} %get-tuple-element.76), channel_id=1, source_target_pairs={{0,1},{1,0},{2,3},{3,2},{4,5},{5,4},{6,7},{7,6},{8,9},{9,8},{10,11... | collective-permute-start | bytes 3145736 | tf_op jit(solution)/shard_map/ppermute | solution.py:1087
  69.1 8.5 %collective-permute-start.8 = (f32[32,16,128]{2,1,0:T(8,128)S(1)}, f32[32,16,128]{2,1,0:T(8,128)S(1)}, u32[]{:S(2)}, u32[]{:S(2)}) collective-permute-start(f32[32,16,128]{2,1,0:T(8,128)S(1)} %get-tuple-element.80), channel_id=1, source_target_pairs={{0,2},{1,3},{2,0},{3,1},{4,6},{5,7},{6,4},{7,5},{8,10},{9,11},{10,... | collective-permute-start | bytes 786440 | tf_op jit(solution)/shard_map/ppermute | solution.py:1087
  69.7 8.1 %collective-permute-start.9 = (f32[2,256,128]{2,1,0:T(8,128)S(1)}, f32[2,256,128]{2,1,0:T(8,128)S(1)}, u32[]{:S(2)}, u32[]{:S(2)}) collective-permute-start(f32[2,256,128]{2,1,0:T(8,128)S(1)} %get-tuple-element.83), channel_id=1, source_target_pairs={{0,4},{4,0},{8,12},{12,8},{1,5},{5,1},{9,13},{13,9},{2,6},{6,2},{1... | collective-permute-start | bytes 786440 | tf_op jit(solution)/shard_map/ppermute | solution.py:1087
  78.2 6.5 %collective-permute-start.10 = (f32[2,128,128]{2,1,0:T(8,128)S(1)}, f32[2,128,128]{2,1,0:T(8,128)S(1)}, u32[]{:S(2)}, u32[]{:S(2)}) collective-permute-start(f32[2,128,128]{2,1,0:T(8,128)S(1)} %get-tuple-element.86), channel_id=1, source_target_pairs={{0,4},{4,0},{8,12},{12,8},{1,5},{5,1},{9,13},{13,9},{2,6},{6,2},{1... | collective-permute-start | bytes 393224 | tf_op jit(solution)/shard_map/ppermute | solution.py:1087
  79.2 8.2 %collective-permute-start.11 = (f32[256,128]{1,0:T(8,128)S(1)}, f32[256,128]{1,0:T(8,128)S(1)}, u32[]{:S(2)}, u32[]{:S(2)}) collective-permute-start(f32[256,128]{1,0:T(8,128)S(1)} %get-tuple-element.88), channel_id=1, source_target_pairs={{0,8},{4,12},{8,0},{12,4},{1,9},{5,13},{9,1},{13,5},{2,10},{6,14},... | collective-permute-start | bytes 393224 | tf_op jit(solution)/shard_map/ppermute | solution.py:1087
  87.4 5.2 %collective-permute-start.12 = (f32[128,128]{1,0:T(8,128)S(1)}, f32[128,128]{1,0:T(8,128)S(1)}, u32[]{:S(2)}, u32[]{:S(2)}) collective-permute-start(f32[128,128]{1,0:T(8,128)S(1)} %get-tuple-element.90), channel_id=1, source_target_pairs={{0,8},{4,12},{8,0},{12,4},{1,9},{5,13},{9,1},{13,5},{2,10},{6,14},... | collective-permute-start | bytes 196616 | tf_op jit(solution)/shard_map/ppermute | solution.py:1087
  87.5 5.1 %collective-permute-start.13 = (f32[128,128]{1,0:T(8,128)S(1)}, f32[128,128]{1,0:T(8,128)S(1)}, u32[]{:S(2)}, u32[]{:S(2)}) collective-permute-start(f32[128,128]{1,0:T(8,128)S(1)} %get-tuple-element.92), channel_id=1, source_target_pairs={{0,2},{1,3},{2,0},{3,1},{4,6},{5,7},{6,4},{7,5},{8,10},{9,11},{10,... | collective-permute-start | bytes 196616 | tf_op jit(solution)/shard_map/ppermute | solution.py:1087
  93.3 5.0 %collective-permute-start.14 = (f32[64,512]{1,0:T(8,128)S(1)}, f32[64,512]{1,0:T(8,128)S(1)}, u32[]{:S(2)}, u32[]{:S(2)}) collective-permute-start(f32[64,512]{1,0:T(8,128)S(1)} %get-tuple-element.96), channel_id=1, source_target_pairs={{0,16},{16,0},{1,17},{17,1},{2,18},{18,2},{3,19},{19,3},{4,20},{20... | collective-permute-start | bytes 393224 | tf_op jit(solution)/shard_map/ppermute | solution.py:1087

commit v8 on v7

--- a/solution.py
+++ b/solution.py
@@ -621,7 +621,7 @@
             return tuple(sums)
 
         zero = jnp.zeros((WIDE, self.nz), F32)
-        return lax.fori_loop(start, stop, measure, (zero,) * (len(PAIRS) + 1), unroll=4)
+        return lax.fori_loop(start, stop, measure, (zero,) * (len(PAIRS) + 1), unroll=11 if self.unroll > 10 else 4)
 
 
 def basis_main(rhs_far, inv_far, *refs):
@@ -713,8 +713,8 @@
         receive(n + halves, pltpu.roll(before[n], half, 1), pltpu.roll(after[n], half, 1))
         return carry
 
-    lax.fori_loop(0, halves, first, 0, unroll=3)
-    lax.fori_loop(0, groups - halves, second, 0, unroll=3)
+    lax.fori_loop(0, halves, first, 0, unroll=6)
+    lax.fori_loop(0, groups - halves, second, 0, unroll=5)
     stencil = Stencil(inv, root, ax, ay, az, vs, lambda k: (1, groups + 1), edges, groups)
     stencil.prepare(rhs)
     copies = []

time: 99.5 us -> 100 us (level)
  no operation moved by 1% of the time
where the time goes in v8:
time: 100 us
  Pallas kernels  40.4 us (40%)
  waiting for transfers between devices  32.8 us (33%)
  starting transfers between devices  24.1 us (24%)
  local copies, waits for them, and re-layouts  1.7 us (2%)
    pallas_call x11, Pallas kernels, call(): pl.pallas_call(body, out_shape=[pltpu.HBM(shape, F32) if n in far_out or...  39.7 us
    ppermute x9, waiting for transfers between devices, swap(): return lax.ppermute(value, axis, [(i, i ^ mask) for i in range(count)])  23.6 us
    ppermute x6, starting transfers between devices, ring(): return (lax.ppermute(one, axis, near), lax.ppermute(two, axis, far))  9.11 us
    ppermute x9, starting transfers between devices, swap(): return lax.ppermute(value, axis, [(i, i ^ mask) for i in range(count)])  9.03 us
    all_to_all x1, waiting for transfers between devices, per_device(): dots = lax.all_to_all(dots, AXES, 0, 0, tiled=True)  8.02 us
    all_to_all x1, starting transfers between devices, per_device(): dots = lax.all_to_all(dots, AXES, 0, 0, tiled=True)  5.94 us
  transfers between devices with their start and end apart: 16, of which 9 were waited for; matrix products, arithmetic and copies ran while one was open for 1% of the time, Pallas kernels for 14%

profile of v8, /device:TPU:0, one launch (start us, length us, event | category | flops | bytes accessed | tf_op | source)
XLA Modules:
  0.0 100.0 jit_solution(8244972452125606767)
XLA Ops:
  0.6 1.6 %shard_map.76.sent = f32[656,128]{1,0:T(8,128)S(1)} custom-call(s32[1]{0:T(128)} %bitcast.index, f32[3,32,64,128]{3,2,1,0:T(8,128)} %refs_9_.1, f32[32,64,128]{2,1,0:T(8,128)} %refs_10_.1), custom_call_target="tpu_custom_call" | custom-call | tf_op jit(solution)/shard_map/pallas_call | solution.py:33
  2.3 3.0 %collective-permute-start = (f32[656,128]{1,0:T(8,128)S(1)}, f32[656,128]{1,0:T(8,128)}, u32[]{:S(2)}, u32[]{:S(2)}) collective-permute-start(f32[656,128]{1,0:T(8,128)S(1)} %shard_map.76.sent), channel_id=1, source_target_pairs={{0,16},{16,0},{1,17},{17,1},{2,18},{18,2},{3,19},{19,3},{4,20},{20... | collective-permute-start | bytes 1007624 | tf_op jit(solution)/shard_map/ppermute | solution.py:1087
  5.4 1.2 %copy-done.1 = f32[32,64,128]{2,1,0:T(8,128)S(1)} copy-done((f32[32,64,128]{2,1,0:T(8,128)S(1)}, f32[32,64,128]{2,1,0:T(8,128)}, u32[]{:S(2)}) %copy-start.1) | copy-done | bytes 1048600
  6.6 2.3 %shard_map.77 = (f32[32,64,128]{2,1,0:T(8,128)S(1)}, f32[17,24,128]{2,1,0:T(8,128)S(1)}, f32[17,24,128]{2,1,0:T(8,128)S(1)}, f32[1,64,128]{2,1,0:T(8,128)S(1)}, f32[1,64,128]{2,1,0:T(8,128)S(1)}) custom-call(s32[6]{0:T(128)S(1)} %stack.34.index, f32[3,32,64,128]{3,2,1,0:T(8,128)S(1)} %copy-done, f32[32,64,128]{2,1,0:T(8,128)S(1)} %copy-done.1, ...), custom_call_target="tpu_custom_call" | custom-call | flops 2621440 | bytes 6291456 | tf_op jit(solution)/shard_map/pallas_call | solution.py:33
  8.9 1.6 %collective-permute-start.1 = (f32[17,24,128]{2,1,0:T(8,128)S(1)}, f32[17,24,128]{2,1,0:T(8,128)S(1)}, u32[]{:S(2)}, u32[]{:S(2)}) collective-permute-start(f32[17,24,128]{2,1,0:T(8,128)S(1)} %get-tuple-element.51), channel_id=1, source_target_pairs={{0,4},{4,0},{8,12},{12,8},{1,5},{5,1},{9,13},{13,9},{2,6},{6,2},{1... | collective-permute-start | bytes 626696 | tf_op jit(solution)/shard_map/ppermute | solution.py:103
  10.5 0.7 collective-permute-start.2
  11.2 4.5 %collective-permute-start.3 = (f32[1,64,128]{2,1,0:T(8,128)S(1)}, f32[1,64,128]{2,1,0:T(8,128)S(1)}, u32[]{:S(2)}, u32[]{:S(2)}) collective-permute-start(f32[1,64,128]{2,1,0:T(8,128)S(1)} %get-tuple-element.53), channel_id=1, source_target_pairs={{0,20},{4,16},{8,28},{12,24},{16,4},{20,0},{24,12},{28,8},{1,21},{... | collective-permute-start | bytes 98312 | tf_op jit(solution)/shard_map/ppermute | solution.py:103
  15.7 0.7 collective-permute-start.4
  16.3 1.2 %collective-permute-done.3.refs_3_ = f32[1,64,128]{2,1,0:T(8,128)S(1)} collective-permute-done((f32[1,64,128]{2,1,0:T(8,128)S(1)}, f32[1,64,128]{2,1,0:T(8,128)S(1)}, u32[]{:S(2)}, u32[]{:S(2)}) %collective-permute-start.3) | collective-permute-done | bytes 32800 | tf_op jit(solution)/shard_map/ppermute | solution.py:103
  17.6 7.4 %shard_map.78 = (f32[42,80,128]{2,1,0:T(8,128)}, f32[42,80,128]{2,1,0:T(8,128)}, f32[6,80,128]{2,1,0:T(8,128)}, f32[6,80,128]{2,1,0:T(8,128)S(1)}, f32[11,80,128]{2,1,0:T(8,128)}, /*index=5*/f32[11,80,128]{2,1,0:T(8,128)}) custom-call(s32[6]{0:T(128)S(1)} %stack.34.index, f32[3,32,64,128]{3,2,1,0:T(8,128)S(1)} %copy-done, f32[32,64,128]{2,1,0:T(8,128)S(1)} %copy-done.2, ...), custom_call_target="tpu_custom_call" | custom-call | tf_op jit(solution)/shard_map/pallas_call | solution.py:33
  25.1 1.6 %collective-permute-start.6 = (f32[6,80,128]{2,1,0:T(8,128)S(1)}, f32[6,80,128]{2,1,0:T(8,128)S(1)}, u32[]{:S(2)}, u32[]{:S(2)}) collective-permute-start(f32[6,80,128]{2,1,0:T(8,128)S(1)} %get-tuple-element.58), channel_id=1, source_target_pairs={{0,3},{1,2},{2,1},{3,0},{4,7},{5,6},{6,5},{7,4},{8,11},{9,10},{10,... | collective-permute-start | bytes 737288 | tf_op jit(solution)/shard_map/ppermute | solution.py:103
  26.7 10.5 %shard_map.79 = (f32[34,80,128]{2,1,0:T(8,128)}, f32[34,80,128]{2,1,0:T(8,128)}, f32[34,80,128]{2,1,0:T(8,128)}, f32[34,80,128]{2,1,0:T(8,128)}, f32[34,80,128]{2,1,0:T(8,128)}, /*index=5*/f32[11,8,128]{2,1,0:T(8,128)S(1)}) custom-call(f32[42,80,128]{2,1,0:T(8,128)} %get-tuple-element.59.rhs_far, f32[42,80,128]{2,1,0:T(8,128)} %get-tuple-element.60.inv_far), custom_call_target="tpu_custom_call" | custom-call | flops 43008000 | bytes 12042240 | tf_op jit(solution)/shard_map/pallas_call | solution.py:33
  37.3 6.8 %shard_map.80 = (f32[11,80,128]{2,1,0:T(8,128)}, f32[11,80,128]{2,1,0:T(8,128)}, f32[11,80,128]{2,1,0:T(8,128)}, f32[11,80,128]{2,1,0:T(8,128)}, f32[32,8,128]{2,1,0:T(8,128)}) custom-call(s32[6]{0:T(128)S(1)} %stack.34.index, f32[11,80,128]{2,1,0:T(8,128)} %get-tuple-element.55.rhs_far, f32[11,80,128]{2,1,0:T(8,128)} %get-tuple-element.56.inv_far, ...), custom_call_target="tpu_custom_call" | custom-call | tf_op jit(solution)/shard_map/pallas_call | solution.py:33
  44.1 5.9 %all-to-all-start = ((f32[32,8,128]{2,1,0:T(8,128)}), f32[32,8,128]{2,1,0:T(8,128)S(1)}, u32[]{:S(2)}, u32[]{:S(2)}) async-start(f32[32,8,128]{2,1,0:T(8,128)} %get-tuple-element.62), calls=%async_computation | async-start | bytes 262144 | tf_op jit(solution)/shard_map/all_to_all | solution.py:1170
  50.1 8.0 %all-to-all-done.dots = f32[32,8,128]{2,1,0:T(8,128)S(1)} async-done(((f32[32,8,128]{2,1,0:T(8,128)}), f32[32,8,128]{2,1,0:T(8,128)S(1)}, u32[]{:S(2)}, u32[]{:S(2)}) %all-to-all-start) | async-done | bytes 131104 | tf_op jit(solution)/shard_map/all_to_all | solution.py:1170
  58.1 8.4 %shard_map.81 = (f32[32,64,128]{2,1,0:T(8,128)}, f32[3,32,64,128]{3,2,1,0:T(8,128)}, f32[64,16,128]{2,1,0:T(8,128)S(1)}, f32[64,16,128]{2,1,0:T(8,128)S(1)}, f32[2,64,16,128]{3,2,1,0:T(8,128)S(1)}) custom-call(f32[32,8,128]{2,1,0:T(8,128)S(1)} %all-to-all-done.dots, bf16[128,256]{1,0:T(8,128)(2,1)S(1)} %maximum_maximum_fusion.columns, ...), custom_call_target="tpu_custom_call" | custom-call | tf_op jit(solution)/shard_map/pallas_call | solution.py:33
  67.3 0.8 shard_map.82
  68.1 1.1 %collective-permute-done.7.came = f32[2,64,16,128]{3,2,1,0:T(8,128)S(1)} collective-permute-done((f32[2,64,16,128]{3,2,1,0:T(8,128)S(1)}, f32[2,64,16,128]{3,2,1,0:T(8,128)S(1)}, u32[]{:S(2)}, u32[]{:S(2)}) %collective-permute-start.7) | collective-permute-done | bytes 1048608 | tf_op jit(solution)/shard_map/ppermute | solution.py:1087
  69.2 0.6 shard_map.83
  69.8 0.6 collective-permute-start.8
  70.4 1.0 collective-permute-start.9
  71.4 7.0 %collective-permute-done.8.p_came = f32[32,16,128]{2,1,0:T(8,128)S(1)} collective-permute-done((f32[32,16,128]{2,1,0:T(8,128)S(1)}, f32[32,16,128]{2,1,0:T(8,128)S(1)}, u32[]{:S(2)}, u32[]{:S(2)}) %collective-permute-start.8) | collective-permute-done | bytes 262176 | tf_op jit(solution)/shard_map/ppermute | solution.py:1087
  78.9 1.0 %collective-permute-start.10 = (f32[2,128,128]{2,1,0:T(8,128)S(1)}, f32[2,128,128]{2,1,0:T(8,128)S(1)}, u32[]{:S(2)}, u32[]{:S(2)}) collective-permute-start(f32[2,128,128]{2,1,0:T(8,128)S(1)} %get-tuple-element.86), channel_id=1, source_target_pairs={{0,4},{4,0},{8,12},{12,8},{1,5},{5,1},{9,13},{13,9},{2,6},{6,2},{1... | collective-permute-start | bytes 393224 | tf_op jit(solution)/shard_map/ppermute | solution.py:1087
  79.9 1.2 %collective-permute-start.11 = (f32[256,128]{1,0:T(8,128)S(1)}, f32[256,128]{1,0:T(8,128)S(1)}, u32[]{:S(2)}, u32[]{:S(2)}) collective-permute-start(f32[256,128]{1,0:T(8,128)S(1)} %get-tuple-element.88), channel_id=1, source_target_pairs={{0,8},{4,12},{8,0},{12,4},{1,9},{5,13},{9,1},{13,5},{2,10},{6,14},... | collective-permute-start | bytes 393224 | tf_op jit(solution)/shard_map/ppermute | solution.py:1087
  81.1 4.3 %collective-permute-done.10.p_came = f32[2,128,128]{2,1,0:T(8,128)S(1)} collective-permute-done((f32[2,128,128]{2,1,0:T(8,128)S(1)}, f32[2,128,128]{2,1,0:T(8,128)S(1)}, u32[]{:S(2)}, u32[]{:S(2)}) %collective-permute-start.10) | collective-permute-done | bytes 131104 | tf_op jit(solution)/shard_map/ppermute | solution.py:1087
  85.4 2.7 %collective-permute-done.11.q_came = f32[256,128]{1,0:T(8,128)S(1)} collective-permute-done((f32[256,128]{1,0:T(8,128)S(1)}, f32[256,128]{1,0:T(8,128)S(1)}, u32[]{:S(2)}, u32[]{:S(2)}) %collective-permute-start.11) | collective-permute-done | bytes 131104 | tf_op jit(solution)/shard_map/ppermute | solution.py:1087
  88.2 1.2 %collective-permute-start.13 = (f32[128,128]{1,0:T(8,128)S(1)}, f32[128,128]{1,0:T(8,128)S(1)}, u32[]{:S(2)}, u32[]{:S(2)}) collective-permute-start(f32[128,128]{1,0:T(8,128)S(1)} %get-tuple-element.92), channel_id=1, source_target_pairs={{0,2},{1,3},{2,0},{3,1},{4,6},{5,7},{6,4},{7,5},{8,10},{9,11},{10,... | collective-permute-start | bytes 196616 | tf_op jit(solution)/shard_map/ppermute | solution.py:1087
  89.4 3.9 %collective-permute-done.12.p_came = f32[128,128]{1,0:T(8,128)S(1)} collective-permute-done((f32[128,128]{1,0:T(8,128)S(1)}, f32[128,128]{1,0:T(8,128)S(1)}, u32[]{:S(2)}, u32[]{:S(2)}) %collective-permute-start.12) | collective-permute-done | bytes 65568 | tf_op jit(solution)/shard_map/ppermute | solution.py:1087
  93.4 0.7 shard_map.86
  94.0 0.7 collective-permute-start.14
  94.7 4.4 %collective-permute-done.14.came = f32[64,512]{1,0:T(8,128)S(1)} collective-permute-done((f32[64,512]{1,0:T(8,128)S(1)}, f32[64,512]{1,0:T(8,128)S(1)}, u32[]{:S(2)}, u32[]{:S(2)}) %collective-permute-start.14) | collective-permute-done | bytes 131104 | tf_op jit(solution)/shard_map/ppermute | solution.py:1087
  99.1 1.0 shard_map.87
  (39 shorter events, 1.6 us)
Async XLA Ops:
  0.6 4.8 %copy-start = (f32[3,32,64,128]{3,2,1,0:T(8,128)S(1)}, f32[3,32,64,128]{3,2,1,0:T(8,128)}, u32[]{:S(2)}) copy-start(f32[3,32,64,128]{3,2,1,0:T(8,128)} %refs_9_.1) | copy-start | bytes 9437188
  2.3 3.1 %copy-start.3 = (f32[656,128]{1,0:T(8,128)}, f32[656,128]{1,0:T(8,128)S(1)}, u32[]{:S(2)}) copy-start(f32[656,128]{1,0:T(8,128)S(1)} %shard_map.76.sent) | copy-start | bytes 1007620
  2.3 15.3 %collective-permute-start = (f32[656,128]{1,0:T(8,128)S(1)}, f32[656,128]{1,0:T(8,128)}, u32[]{:S(2)}, u32[]{:S(2)}) collective-permute-start(f32[656,128]{1,0:T(8,128)S(1)} %shard_map.76.sent), channel_id=1, source_target_pairs={{0,16},{16,0},{1,17},{17,1},{2,18},{18,2},{3,19},{19,3},{4,20},{20... | collective-permute-start | bytes 1007624 | tf_op jit(solution)/shard_map/ppermute | solution.py:1087
  5.4 1.2 %copy-start.1 = (f32[32,64,128]{2,1,0:T(8,128)S(1)}, f32[32,64,128]{2,1,0:T(8,128)}, u32[]{:S(2)}) copy-start(f32[32,64,128]{2,1,0:T(8,128)} %refs_10_.1) | copy-start | bytes 3145732
  6.6 11.0 %copy-start.2 = (f32[32,64,128]{2,1,0:T(8,128)S(1)}, f32[32,64,128]{2,1,0:T(8,128)}, u32[]{:S(2)}) copy-start(f32[32,64,128]{2,1,0:T(8,128)} %refs_10_.1) | copy-start | bytes 3145732
  8.9 8.7 %collective-permute-start.1 = (f32[17,24,128]{2,1,0:T(8,128)S(1)}, f32[17,24,128]{2,1,0:T(8,128)S(1)}, u32[]{:S(2)}, u32[]{:S(2)}) collective-permute-start(f32[17,24,128]{2,1,0:T(8,128)S(1)} %get-tuple-element.51), channel_id=1, source_target_pairs={{0,4},{4,0},{8,12},{12,8},{1,5},{5,1},{9,13},{13,9},{2,6},{6,2},{1... | collective-permute-start | bytes 626696 | tf_op jit(solution)/shard_map/ppermute | solution.py:103
  10.5 7.0 %collective-permute-start.2 = (f32[17,24,128]{2,1,0:T(8,128)S(1)}, f32[17,24,128]{2,1,0:T(8,128)S(1)}, u32[]{:S(2)}, u32[]{:S(2)}) collective-permute-start(f32[17,24,128]{2,1,0:T(8,128)S(1)} %get-tuple-element.52), channel_id=1, source_target_pairs={{4,8},{8,4},{5,9},{9,5},{6,10},{10,6},{7,11},{11,7},{20,24},{24,20... | collective-permute-start | bytes 626696 | tf_op jit(solution)/shard_map/ppermute | solution.py:103
  11.2 6.3 %collective-permute-start.3 = (f32[1,64,128]{2,1,0:T(8,128)S(1)}, f32[1,64,128]{2,1,0:T(8,128)S(1)}, u32[]{:S(2)}, u32[]{:S(2)}) collective-permute-start(f32[1,64,128]{2,1,0:T(8,128)S(1)} %get-tuple-element.53), channel_id=1, source_target_pairs={{0,20},{4,16},{8,28},{12,24},{16,4},{20,0},{24,12},{28,8},{1,21},{... | collective-permute-start | bytes 98312 | tf_op jit(solution)/shard_map/ppermute | solution.py:103
  15.7 1.9 %collective-permute-start.4 = (f32[1,64,128]{2,1,0:T(8,128)S(1)}, f32[1,64,128]{2,1,0:T(8,128)S(1)}, u32[]{:S(2)}, u32[]{:S(2)}) collective-permute-start(f32[1,64,128]{2,1,0:T(8,128)S(1)} %get-tuple-element.54), channel_id=1, source_target_pairs={{4,24},{8,20},{20,8},{24,4},{5,25},{9,21},{21,9},{25,5},{6,26},{10... | collective-permute-start | bytes 98312 | tf_op jit(solution)/shard_map/ppermute | solution.py:103
  17.6 9.2 %copy-start.4 = (f32[128,64]{0,1:T(8,128)S(1)}, f32[128,64]{0,1:T(8,128)}, u32[]{:S(2)}) copy-start(f32[128,64]{0,1:T(8,128)} %param.9) | copy-start | bytes 98308
  25.0 12.3 %collective-permute-start.5 = (f32[6,80,128]{2,1,0:T(8,128)}, f32[6,80,128]{2,1,0:T(8,128)S(1)}, u32[]{:S(2)}, u32[]{:S(2)}) collective-permute-start(f32[6,80,128]{2,1,0:T(8,128)} %get-tuple-element.57), channel_id=1, source_target_pairs={{0,1},{1,0},{2,3},{3,2},{4,5},{5,4},{6,7},{7,6},{8,9},{9,8},{10,11... | collective-permute-start | bytes 737288 | tf_op jit(solution)/shard_map/ppermute | solution.py:103
  25.1 12.2 %collective-permute-start.6 = (f32[6,80,128]{2,1,0:T(8,128)S(1)}, f32[6,80,128]{2,1,0:T(8,128)S(1)}, u32[]{:S(2)}, u32[]{:S(2)}) collective-permute-start(f32[6,80,128]{2,1,0:T(8,128)S(1)} %get-tuple-element.58), channel_id=1, source_target_pairs={{0,3},{1,2},{2,1},{3,0},{4,7},{5,6},{6,5},{7,4},{8,11},{9,10},{10,... | collective-permute-start | bytes 737288 | tf_op jit(solution)/shard_map/ppermute | solution.py:103
  44.1 14.0 %all-to-all-start = ((f32[32,8,128]{2,1,0:T(8,128)}), f32[32,8,128]{2,1,0:T(8,128)S(1)}, u32[]{:S(2)}, u32[]{:S(2)}) async-start(f32[32,8,128]{2,1,0:T(8,128)} %get-tuple-element.62), calls=%async_computation | async-start | bytes 262144 | tf_op jit(solution)/shard_map/all_to_all | solution.py:1170
  58.1 8.7 %copy-start.5 = (f32[64,64]{1,0:T(8,128)S(1)}, f32[64,64]{1,0:T(8,128)}, u32[]{:S(2)}) copy-start(f32[64,64]{1,0:T(8,128)} %param.8) | copy-start | bytes 49156
  58.1 8.9 %copy-start.6 = (f32[32,64]{1,0:T(8,128)S(1)}, f32[32,64]{1,0:T(8,128)}, u32[]{:S(2)}) copy-start(f32[32,64]{1,0:T(8,128)} %param.7) | copy-start | bytes 24580
  66.5 2.7 %collective-permute-start.7 = (f32[2,64,16,128]{3,2,1,0:T(8,128)S(1)}, f32[2,64,16,128]{3,2,1,0:T(8,128)S(1)}, u32[]{:S(2)}, u32[]{:S(2)}) collective-permute-start(f32[2,64,16,128]{3,2,1,0:T(8,128)S(1)} %get-tuple-element.76), channel_id=1, source_target_pairs={{0,1},{1,0},{2,3},{3,2},{4,5},{5,4},{6,7},{7,6},{8,9},{9,8},{10,11... | collective-permute-start | bytes 3145736 | tf_op jit(solution)/shard_map/ppermute | solution.py:1087
  69.8 8.5 %collective-permute-start.8 = (f32[32,16,128]{2,1,0:T(8,128)S(1)}, f32[32,16,128]{2,1,0:T(8,128)S(1)}, u32[]{:S(2)}, u32[]{:S(2)}) collective-permute-start(f32[32,16,128]{2,1,0:T(8,128)S(1)} %get-tuple-element.80), channel_id=1, source_target_pairs={{0,2},{1,3},{2,0},{3,1},{4,6},{5,7},{6,4},{7,5},{8,10},{9,11},{10,... | collective-permute-start | bytes 786440 | tf_op jit(solution)/shard_map/ppermute | solution.py:1087
  70.4 8.1 %collective-permute-start.9 = (f32[2,256,128]{2,1,0:T(8,128)S(1)}, f32[2,256,128]{2,1,0:T(8,128)S(1)}, u32[]{:S(2)}, u32[]{:S(2)}) collective-permute-start(f32[2,256,128]{2,1,0:T(8,128)S(1)} %get-tuple-element.83), channel_id=1, source_target_pairs={{0,4},{4,0},{8,12},{12,8},{1,5},{5,1},{9,13},{13,9},{2,6},{6,2},{1... | collective-permute-start | bytes 786440 | tf_op jit(solution)/shard_map/ppermute | solution.py:1087
  78.9 6.5 %collective-permute-start.10 = (f32[2,128,128]{2,1,0:T(8,128)S(1)}, f32[2,128,128]{2,1,0:T(8,128)S(1)}, u32[]{:S(2)}, u32[]{:S(2)}) collective-permute-start(f32[2,128,128]{2,1,0:T(8,128)S(1)} %get-tuple-element.86), channel_id=1, source_target_pairs={{0,4},{4,0},{8,12},{12,8},{1,5},{5,1},{9,13},{13,9},{2,6},{6,2},{1... | collective-permute-start | bytes 393224 | tf_op jit(solution)/shard_map/ppermute | solution.py:1087
  79.9 8.2 %collective-permute-start.11 = (f32[256,128]{1,0:T(8,128)S(1)}, f32[256,128]{1,0:T(8,128)S(1)}, u32[]{:S(2)}, u32[]{:S(2)}) collective-permute-start(f32[256,128]{1,0:T(8,128)S(1)} %get-tuple-element.88), channel_id=1, source_target_pairs={{0,8},{4,12},{8,0},{12,4},{1,9},{5,13},{9,1},{13,5},{2,10},{6,14},... | collective-permute-start | bytes 393224 | tf_op jit(solution)/shard_map/ppermute | solution.py:1087
  88.1 5.2 %collective-permute-start.12 = (f32[128,128]{1,0:T(8,128)S(1)}, f32[128,128]{1,0:T(8,128)S(1)}, u32[]{:S(2)}, u32[]{:S(2)}) collective-permute-start(f32[128,128]{1,0:T(8,128)S(1)} %get-tuple-element.90), channel_id=1, source_target_pairs={{0,8},{4,12},{8,0},{12,4},{1,9},{5,13},{9,1},{13,5},{2,10},{6,14},... | collective-permute-start | bytes 196616 | tf_op jit(solution)/shard_map/ppermute | solution.py:1087
  88.2 5.2 %collective-permute-start.13 = (f32[128,128]{1,0:T(8,128)S(1)}, f32[128,128]{1,0:T(8,128)S(1)}, u32[]{:S(2)}, u32[]{:S(2)}) collective-permute-start(f32[128,128]{1,0:T(8,128)S(1)} %get-tuple-element.92), channel_id=1, source_target_pairs={{0,2},{1,3},{2,0},{3,1},{4,6},{5,7},{6,4},{7,5},{8,10},{9,11},{10,... | collective-permute-start | bytes 196616 | tf_op jit(solution)/shard_map/ppermute | solution.py:1087
  94.0 5.0 %collective-permute-start.14 = (f32[64,512]{1,0:T(8,128)S(1)}, f32[64,512]{1,0:T(8,128)S(1)}, u32[]{:S(2)}, u32[]{:S(2)}) collective-permute-start(f32[64,512]{1,0:T(8,128)S(1)} %get-tuple-element.96), channel_id=1, source_target_pairs={{0,16},{16,0},{1,17},{17,1},{2,18},{18,2},{3,19},{19,3},{4,20},{20... | collective-permute-start | bytes 393224 | tf_op jit(solution)/shard_map/ppermute | solution.py:1087
